TPU v7x, 128 devices: a whole 4x4x4 slice. The times are simulated.
128 devices in a mesh: fsdp: 32 (over x, y, z_hi), tp: 4 (over z_lo, core).
Axes of the slice: x: 4, y: 4, z: 4 (z_hi: 2, z_lo: 2; z = z_hi * 2 + z_lo), core: 2. Of those that a mesh axis runs over, the one named last changes fastest.
Arguments:
- tokens: bfloat16 [32, 1024, 1024], P('fsdp', 'tp'), may hold values from -6 to 6
- attention_gain: bfloat16 [1024], P('fsdp'), may hold values from 0.25 to 1.75
- query_weight: bfloat16 [1024, 2048], P('fsdp', 'tp'), may hold values from -0.1875 to 0.1875
- key_weight: bfloat16 [1024, 1024], P('fsdp', 'tp'), may hold values from -0.1875 to 0.1875
- value_weight: bfloat16 [1024, 1024], P('fsdp', 'tp'), may hold values from -0.1875 to 0.1875
- query_gain: bfloat16 [128], P('fsdp'), may hold values from 0.25 to 1.75
- key_gain: bfloat16 [128], P('fsdp'), may hold values from 0.25 to 1.75
- output_weight: bfloat16 [1024, 2048], P('fsdp', 'tp'), may hold values from -0.375 to 0.375
- feed_gain: bfloat16 [1024], P('fsdp'), may hold values from 0.25 to 1.75
- gate_weight: bfloat16 [1024, 3072], P('fsdp', 'tp'), may hold values from -0.1875 to 0.1875
- up_weight: bfloat16 [1024, 3072], P('fsdp', 'tp'), may hold values from -0.1875 to 0.1875
- down_weight: bfloat16 [1024, 3072], P('fsdp', 'tp'), may hold values from -0.109375 to 0.109375
- cotangent: bfloat16 [32, 1024, 1024], P('fsdp', 'tp'), may hold values from -6 to 6
Outputs:
- layer_output: bfloat16 [32, 1024, 1024], P('fsdp', 'tp')
- tokens_grad: float32 [32, 1024, 1024], P('fsdp', 'tp')
- attention_gain_grad: float32 [1024], P('fsdp')
- query_weight_grad: float32 [1024, 2048], P('fsdp', 'tp')
- key_weight_grad: float32 [1024, 1024], P('fsdp', 'tp')
- value_weight_grad: float32 [1024, 1024], P('fsdp', 'tp')
- query_gain_grad: float32 [128], P('fsdp')
- key_gain_grad: float32 [128], P('fsdp')
- output_weight_grad: float32 [1024, 2048], P('fsdp', 'tp')
- feed_gain_grad: float32 [1024], P('fsdp')
- gate_weight_grad: float32 [1024, 3072], P('fsdp', 'tp')
- up_weight_grad: float32 [1024, 3072], P('fsdp', 'tp')
- down_weight_grad: float32 [1024, 3072], P('fsdp', 'tp')
All inputs are finite; a program needn't handle non-finite values.
Results may differ from a plain program's by a relative error of at most 0.017.
Values may be sent and summed in bfloat16 or wider, within the bound.
No kernel may reach another device: no remote copies, remote signals or barrier semaphores. Data moves between devices by JAX's collectives and lax.ppermute only.
A program may use at most 192 MiB of HBM per device.

v0:
```python
import functools
import math

import jax
import jax.numpy as jnp
import numpy as np
from jax import lax
from jax.experimental import pallas as pl
from jax.experimental.pallas import tpu as pltpu
from jax.sharding import Mesh, PartitionSpec as P

HD = 128
ROWS = 256
WIDTH = 1024
GROUP = 2
CHUNK = 256
BLOCK_ORDER = (0, 2, 1, 3)
epsilon = 1e-06
rope_base = 1000000.0
score_scale = 1.0 / math.sqrt(HD)
log2_scale = score_scale / math.log(2.0)
FSDP = ("x", "y", "zh")
PLANE = ("x", "y")
EVERY = ("x", "y", "zh", "zl", "core")
f32 = jnp.float32
bf16 = jnp.bfloat16


def matmul(a, b):
    return lax.dot_general(a, b, (((1,), (0,)), ((), ())), preferred_element_type=f32)


def matmul_t(a, b):
    return lax.dot_general(a, b, (((1,), (1,)), ((), ())), preferred_element_type=f32)


def t_matmul(a, b):
    return lax.dot_general(a, b, (((0,), (0,)), ((), ())), preferred_element_type=f32)


def inverse_rms(values):
    return lax.rsqrt(jnp.mean(values * values, axis=-1, keepdims=True) + epsilon)


def norm_back(values, gain, upstream):
    inverse = inverse_rms(values)
    scaled = gain * upstream
    moment = jnp.mean(scaled * values, axis=-1, keepdims=True)
    grad = inverse * scaled - values * (inverse * inverse * inverse) * moment
    return grad, jnp.sum(upstream * values * inverse, axis=0, keepdims=True)


def far(value):
    return pltpu.with_memory_space_constraint(value, pltpu.HBM)


def params(mib):
    return pltpu.CompilerParams(vmem_limit_bytes=mib * 1024 * 1024)


def cost(flops, nbytes, trans=0):
    return pl.CostEstimate(flops=int(flops / 8), bytes_accessed=int(nbytes / 8), transcendentals=int(trans / 8))


def whole(shape, index=None):
    index = index or (0,) * len(shape)
    return pl.BlockSpec(shape, lambda i, *_: index, pipeline_mode=pl.Buffered(1))


def halves(width):
    return [
        pl.BlockSpec((1, ROWS, width), lambda i: (jnp.minimum(i, 1), 0, 0)),
        pl.BlockSpec((1, ROWS, width), lambda i: (jnp.maximum(i - 2, 0), 0, 0)),
    ]


def whole_out(shape):
    return pl.BlockSpec(shape, lambda i, *_: (0,) * len(shape))


def pick(which, pieces, target):
    for k, piece in enumerate(pieces):

        @pl.when(which == k)
        def _(piece=piece):
            target[...] = piece[...]


def equal_iota(rows, cols, make):
    r = lax.broadcasted_iota(jnp.int32, (rows, cols), 0)
    c = lax.broadcasted_iota(jnp.int32, (rows, cols), 1)
    return make(r, c)


def row_of(columns, k):
    same = equal_iota(128, 128, lambda r, c: r == c)
    parts = []
    for m in range(columns.shape[0] // 128):
        col = columns[m * 128 : (m + 1) * 128, k : k + 1].astype(f32)
        parts.append(jnp.sum(jnp.where(same, col, 0.0), axis=0, keepdims=True))
    return jnp.concatenate(parts, axis=1)


def of_head(rows, per_device, first_row=0):
    held = HD * per_device // WIDTH
    return equal_iota(
        rows, HD, lambda r, c: ((r + first_row) // per_device * held + (r + first_row) % per_device == c)
        & ((r + first_row) % per_device < held)
    )


def heads_of(columns, k, per_device):
    col = columns[:, k : k + 1].astype(f32)
    return jnp.sum(jnp.where(of_head(columns.shape[0], per_device), col, 0.0), axis=0, keepdims=True)


def put_pair(which, value, mine, other):
    top, bottom = value[:ROWS], value[ROWS:]

    @pl.when(which < 2)
    def _():
        mine[0] = top
        other[0] = bottom

    @pl.when(which >= 2)
    def _():
        mine[0] = bottom
        other[0] = top


def put(which, value, mine, other):
    @pl.when(which < 2)
    def _():
        mine[0] = value

    @pl.when(which >= 2)
    def _():
        other[0] = value


def forward_attention_kernel(per_device, n_pieces, place, order, *refs):
    tokens = refs[:4]
    pieces, refs = refs[4 : 4 + n_pieces], refs[4 + n_pieces :]
    cos, sin = refs[:2]
    first, qraw, kraw, low, att, totals, mine, other, gains, head_gains, ordered = refs[2:13]
    rows, keys, values, weights, piece_sems, ordered_sem = refs[13:]
    i = pl.program_id(0)
    nq, nqkv = qraw.shape[1], low.shape[1]
    wqkv = weights.at[:, :nqkv]
    wo = weights.at[:, nqkv : nqkv + nq]
    columns = weights.at[:, nqkv + nq :]
    keep = pltpu.make_async_copy(weights, ordered, ordered_sem)

    @pl.when(i == 0)
    def _():
        for copy in load_pieces(order, pieces, weights, piece_sems):
            copy.wait()
        keep.start()
        gains[:2, :] = jnp.concatenate([row_of(columns, 0), row_of(columns, 1)], axis=0)
        gains[2:, :] = jnp.zeros_like(gains[2:, :])
        head_gains[:2, :] = jnp.concatenate([heads_of(columns, k, per_device) for k in (2, 3)], axis=0)
        head_gains[2:, :] = jnp.zeros_like(head_gains[2:, :])

    gain, qgain, kgain = gains[:1, :], head_gains[:1, :], head_gains[1:2, :]
    for a in range(2):
        pick(place[2 * i + a], tokens, rows.at[a * ROWS : (a + 1) * ROWS, :])
    x = rows[...].astype(f32)
    normed = (x * inverse_rms(x) * gain).astype(bf16)
    first[...] = normed
    qkv = matmul(normed, wqkv[...])
    nq, nk = qraw.shape[1], kraw.shape[1]
    qraw[...] = qkv[:, :nq]
    kraw[...] = qkv[:, nq : nq + nk]
    here = pl.ds(pl.multiple_of(i * 2 * ROWS, 2 * ROWS), 2 * ROWS)
    c, s = cos[...], sin[...]

    def turned(v, g):
        n = v * inverse_rms(v) * g
        return (n * c + pltpu.roll(n, HD // 2, 1) * s).astype(bf16)

    for h in range(nk // HD):
        k_low = turned(qkv[:, nq + h * HD : nq + (h + 1) * HD], kgain)
        v_low = qkv[:, nq + nk + h * HD : nq + nk + (h + 1) * HD].astype(bf16)
        low[:, nq + h * HD : nq + (h + 1) * HD] = k_low
        low[:, nq + nk + h * HD : nq + nk + (h + 1) * HD] = v_low
        keys[h, here, :] = k_low
        values[h, here, :HD] = v_low
        values[h, here, HD:] = jnp.ones((2 * ROWS, HD), bf16)
    for h in range(nq // HD):
        low[:, h * HD : (h + 1) * HD] = turned(qkv[:, h * HD : (h + 1) * HD], qgain)
    mask_q = lax.broadcasted_iota(jnp.int32, (GROUP * ROWS, ROWS), 0) % ROWS
    mask_k = lax.broadcasted_iota(jnp.int32, (GROUP * ROWS, ROWS), 1)

    def attend(block):
        half = block % 2 * ROWS
        n = block * ROWS
        sums = []
        for h in range(nk // HD):
            cols = [(h * GROUP + a) * HD for a in range(GROUP)]
            q2 = jnp.concatenate([low[half : half + ROWS, col : col + HD] for col in cols], axis=0)
            scores = matmul_t(q2, keys[h, : n + ROWS, :]) * log2_scale
            weights = jnp.exp2(scores[:, n:])
            weights = jnp.where(mask_k <= mask_q, weights, 0.0).astype(bf16)
            if n:
                weights = jnp.concatenate([jnp.exp2(scores[:, :n]).astype(bf16), weights], axis=1)
            acc = matmul(weights, values[h, : n + ROWS, :])
            total = acc[:, HD:]
            o = (acc[:, :HD] / total).astype(bf16)
            for a, col in enumerate(cols):
                att[half : half + ROWS, col : col + HD] = o[a * ROWS : (a + 1) * ROWS]
            sums.append(jnp.log2(total).T[:1, :])
        sums = jnp.concatenate(sums + [jnp.zeros((8 - len(sums), GROUP * ROWS), f32)], axis=0)
        totals[block % 2] = sums

    for k in range(2):

        @pl.when(i == k)
        def _(k=k):
            attend(2 * k)
            attend(2 * k + 1)

    put_pair(place[2 * i], matmul_t(att[...], wo[...]).astype(bf16), mine, other)

    @pl.when(i == pl.num_programs(0) - 1)
    def _():
        keep.wait()


def forward_attention(place, order, tokens, pieces, nq, nk, cos, sin):
    n, width = 4, tokens[0].shape[1]
    length = n * ROWS
    nqkv = nq + 2 * nk
    row = lambda cols: pl.BlockSpec((2 * ROWS, cols), lambda i, p, o: (i, 0))
    out = [
        ((length, width), bf16, row(width)),
        ((length, nq), f32, row(nq)),
        ((length, nk), f32, row(nk)),
        ((length, nqkv), bf16, row(nqkv)),
        ((length, nq), bf16, row(nq)),
        ((n, 8, GROUP * ROWS), f32, pl.BlockSpec((2, 8, GROUP * ROWS), lambda i, p, o: (i, 0, 0))),
        *[((2, ROWS, width), bf16, pl.BlockSpec((1, ROWS, width), lambda i, p, o: (p[2 * i] % 2, 0, 0)))] * 2,
        ((8, width), f32, whole_out((8, width))),
        ((8, HD), f32, whole_out((8, HD))),
        ((width, nqkv + nq + HD), bf16, pl.BlockSpec(memory_space=pltpu.HBM)),
    ]
    return pl.pallas_call(
        functools.partial(forward_attention_kernel, width // lax.axis_size(FSDP), len(pieces)),
        grid_spec=pltpu.PrefetchScalarGridSpec(
            num_scalar_prefetch=2,
            grid=(n // 2,),
            in_specs=[
                *[whole((ROWS, width))] * 4,
                *[pl.BlockSpec(memory_space=pl.ANY)] * len(pieces),
                row(HD),
                row(HD),
            ],
            out_specs=[o[2] for o in out],
            scratch_shapes=[
                pltpu.VMEM((2 * ROWS, width), bf16),
                pltpu.VMEM((nk // HD, length, HD), bf16),
                pltpu.VMEM((nk // HD, length, 2 * HD), bf16),
                pltpu.VMEM((width, nqkv + nq + HD), bf16),
                pltpu.SemaphoreType.DMA(order.shape),
                pltpu.SemaphoreType.DMA,
            ],
        ),
        out_shape=[(pltpu.HBM if k < 6 or k == 10 else jax.ShapeDtypeStruct)(o[0], o[1]) for k, o in enumerate(out)],
        compiler_params=params(40),
        cost_estimate=cost(7e9, 16e6, 3e6),
        name="forward_attention",
    )(place, order, far(tokens[0]), *tokens[1:], *pieces, far(cos), far(sin))


def middle_kernel(tokens, mine, from_core, from_z, gain, middle, second):
    total = mine[...].astype(f32) + from_core[...].astype(f32) + from_z[...].astype(f32)
    v = tokens[...].astype(f32) + total
    middle[...] = v
    second[...] = (v * inverse_rms(v) * gain[1:2, :]).astype(bf16)


def middle_step(tokens, part, from_core, from_z, gain):
    width = tokens.shape[1]
    half = ROWS // 2
    row = pl.BlockSpec((half, width), lambda i: (i, 0))
    first = pl.BlockSpec((None, half, width), lambda i: (0, i, 0))
    return pl.pallas_call(
        middle_kernel,
        grid=(2,),
        in_specs=[row, first, first, row, whole((8, width))],
        out_specs=[row, row],
        out_shape=[pltpu.HBM((ROWS, width), f32), jax.ShapeDtypeStruct((ROWS, width), bf16)],
        compiler_params=params(12),
        cost_estimate=cost(2e6, 4e6),
        name="middle_step",
    )(far(tokens), part, from_core, from_z, gain)


def feed_kernel(*refs):
    second, grads, weights = refs[:2], refs[2:4], refs[4]
    hidden, grad_units, mine, other = refs[5:9]
    rows_s, rows_g, matrices, row_sems, matrix_sems = refs[9:]
    units = hidden.shape[1]
    loads = []
    for k in range(2):
        at = slice(k * ROWS, (k + 1) * ROWS)
        loads.append(pltpu.make_async_copy(second[k], rows_s.at[at, :], row_sems.at[0, k]))
        loads.append(pltpu.make_async_copy(grads[k], rows_g.at[at, :], row_sems.at[1, k]))
    chunks = []
    for c in range(units // CHUNK):
        for m in range(3):
            some = slice(m * units + c * CHUNK, m * units + (c + 1) * CHUNK)
            chunks.append(
                pltpu.make_async_copy(weights.at[:, some], matrices.at[:, some], matrix_sems.at[m, c])
            )
    for copy in loads + chunks:
        copy.start()
    for copy in loads:
        copy.wait()
    s, g = rows_s[...], rows_g[...]
    for c, at in enumerate(range(0, units, CHUNK)):
        for copy in chunks[3 * c : 3 * c + 3]:
            copy.wait()
        gate = matmul(s, matrices[:, at : at + CHUNK])
        up = matmul(s, matrices[:, units + at : units + at + CHUNK])
        gh = matmul(g, matrices[:, 2 * units + at : 2 * units + at + CHUNK])
        sig = 0.5 * jnp.tanh(0.5 * gate) + 0.5
        swish = gate * sig
        hidden[:, at : at + CHUNK] = (swish * up).astype(bf16)
        grad_units[:, at : at + CHUNK] = (gh * up * (sig + swish * (1.0 - sig))).astype(bf16)
        grad_units[:, units + at : units + at + CHUNK] = (gh * swish).astype(bf16)
    part = matmul_t(grad_units[...], matrices[:, : 2 * units]).astype(bf16)
    mine[...] = part[:ROWS]
    other[...] = part[ROWS:]


def feed_step(second, grads, weights, units):
    width = second[0].shape[1]
    return pl.pallas_call(
        feed_kernel,
        in_specs=[pl.BlockSpec(memory_space=pl.ANY)] * 5,
        out_shape=[
            pltpu.HBM((2 * ROWS, units), bf16),
            pltpu.HBM((2 * ROWS, 2 * units), bf16),
            *[jax.ShapeDtypeStruct((ROWS, width), bf16)] * 2,
        ],
        scratch_shapes=[
            *[pltpu.VMEM((2 * ROWS, width), bf16)] * 2,
            pltpu.VMEM((width, 3 * units), bf16),
            pltpu.SemaphoreType.DMA((2, 2)),
            pltpu.SemaphoreType.DMA((3, units // CHUNK)),
        ],
        compiler_params=params(32),
        cost_estimate=cost(4e9, 8e6, 1e6),
        name="feed_step",
    )(*second, *map(far, grads), far(weights))


def feed_out_kernel(first, then, wd, mine, other):
    for k, hidden in enumerate((first, then)):

        @pl.when(pl.program_id(0) == k)
        def _(hidden=hidden):
            part = matmul_t(hidden[...], wd[...]).astype(bf16)
            mine[0] = part[:ROWS]
            other[0] = part[ROWS:]


def feed_out(hidden, weights):
    pair, units = hidden[0].shape
    width = weights.shape[0]
    block = pl.BlockSpec((1, ROWS, width), lambda i: (i, 0, 0))
    return pl.pallas_call(
        feed_out_kernel,
        grid=(2,),
        in_specs=[whole((pair, units)), whole((pair, units)), whole((width, units), (0, 2))],
        out_specs=[block, block],
        out_shape=[jax.ShapeDtypeStruct((2, ROWS, width), bf16)] * 2,
        compiler_params=params(20),
        cost_estimate=cost(1.6e9, 5e6),
        name="feed_out",
    )(*map(far, hidden), far(weights))


def feed_weights_kernel(*refs):
    second, grads, grad_units, hidden = refs[:4], refs[4:8], refs[8:10], refs[10:12]
    out, rows_s, rows_g = refs[12:]
    wide = grad_units[0].shape[1]
    pair = 2 * ROWS
    for k, block in enumerate(BLOCK_ORDER):
        rows_s[k * ROWS : (k + 1) * ROWS, :] = second[block][...]
        rows_g[k * ROWS : (k + 1) * ROWS, :] = grads[block][...]
    both = lambda rows, others: sum(
        t_matmul(rows[k * pair : (k + 1) * pair, :], other[...]) for k, other in enumerate(others)
    )
    out[:, :wide] = both(rows_s, grad_units).astype(bf16)
    out[:, wide:] = both(rows_g, hidden).astype(bf16)


def feed_weights(second, grads, grad_units, hidden):
    width = second[0].shape[1]
    pair, wide = grad_units[0].shape
    units = hidden[0].shape[1]
    return pl.pallas_call(
        feed_weights_kernel,
        grid=(width // 512,),
        in_specs=[
            *[pl.BlockSpec((ROWS, 512), lambda i: (0, i))] * 8,
            *[whole((pair, wide))] * 2,
            *[whole((pair, units))] * 2,
        ],
        out_specs=pl.BlockSpec((512, wide + units), lambda i: (i, 0)),
        out_shape=pltpu.HBM((width, wide + units), bf16),
        scratch_shapes=[pltpu.VMEM((2 * pair, 512), bf16)] * 2,
        compiler_params=params(36),
        cost_estimate=cost(4.8e9, 14e6),
        name="feed_weights",
    )(*map(far, second), *map(far, grads), *map(far, grad_units), *map(far, hidden))


def middle_back_kernel(middle, mine, from_core, from_z, cotangent, gain, grad_middle, branch, gain_part):
    u = mine[...].astype(f32) + from_core[...].astype(f32) + from_z[...].astype(f32)
    grad, part = norm_back(middle[...], gain[1:2, :], u)
    grad = cotangent[...].astype(f32) + grad
    grad_middle[...] = grad
    branch[...] = grad.astype(bf16)

    @pl.when(pl.program_id(0) == 0)
    def _():
        gain_part[...] = jnp.zeros_like(gain_part)

    gain_part[:1, :] += part


def middle_back(middle, part, from_core, from_z, cotangent, gain):
    width = middle.shape[1]
    half = ROWS // 2
    row = pl.BlockSpec((half, width), lambda i: (i, 0))
    return pl.pallas_call(
        middle_back_kernel,
        grid=(2,),
        in_specs=[row, row, row, row, row, whole((8, width))],
        out_specs=[row, row, whole_out((8, width))],
        out_shape=[
            pltpu.HBM((ROWS, width), f32),
            jax.ShapeDtypeStruct((ROWS, width), bf16),
            pltpu.HBM((8, width), f32),
        ],
        compiler_params=params(14),
        cost_estimate=cost(4e6, 5e6),
        name="middle_back",
    )(far(middle), part, from_core, from_z, far(cotangent), gain)


def backward_attention_kernel(place, *refs):
    branch = refs[:4]
    tokens = refs[4:8]
    weights, low, att, totals, qraw, kraw, cos, sin, head_gains = refs[8:17]
    grads, mine, other, branch_out, gain_part, head_part = refs[17:23]
    matrices, rows_all, xs_all, grad_att, dk, dv, dq, row_sems, matrix_sems = refs[23:]
    qgain, kgain = head_gains[:1, :], head_gains[1:2, :]
    step_id = pl.program_id(0)
    i = pl.num_programs(0) - 1 - step_id
    nq, nk = qraw.shape[1], kraw.shape[1]

    @pl.when(step_id == 0)
    def _():
        gain_part[...] = jnp.zeros_like(gain_part)
        head_part[...] = jnp.zeros_like(head_part)

    nqkv = nq + 2 * nk
    wqkv = matrices.at[:, :nqkv]
    wo = matrices.at[:, nqkv:]
    load_o = pltpu.make_async_copy(weights.at[:, nqkv : nqkv + nq], wo, matrix_sems.at[0])
    load_qkv = pltpu.make_async_copy(weights.at[:, :nqkv], wqkv, matrix_sems.at[1])
    loads = []
    for pieces, target, sem in ((branch, rows_all, row_sems.at[0]), (tokens, xs_all, row_sems.at[1])):
        for k, piece in enumerate(pieces):
            at = pl.ds(pl.multiple_of(place[4 + k] * ROWS, ROWS), ROWS)
            loads.append(pltpu.make_async_copy(piece, target.at[at, :], sem.at[k]))

    @pl.when(step_id == 0)
    def _():
        for copy in [load_o, *loads[:4], load_qkv, *loads[4:]]:
            copy.start()
        for copy in [load_o, *loads[:4]]:
            copy.wait()

    here = pl.ds(pl.multiple_of(i * 2 * ROWS, 2 * ROWS), 2 * ROWS)
    branch_out[...] = rows_all[here, :]
    grad_att[...] = matmul(rows_all[here, :], wo[...]).astype(bf16)
    mask_k = lax.broadcasted_iota(jnp.int32, (ROWS, GROUP * ROWS), 0)
    mask_q = lax.broadcasted_iota(jnp.int32, (ROWS, GROUP * ROWS), 1) % ROWS

    def attend_back(block):
        half = block % 2 * ROWS
        n = block * ROWS
        end = n + ROWS
        for h in range(nk // HD):
            cols = [(h * GROUP + a) * HD for a in range(GROUP)]
            q2 = jnp.concatenate([low[n:end, col : col + HD] for col in cols], axis=0)
            g2 = jnp.concatenate([grad_att[half : half + ROWS, col : col + HD] for col in cols], axis=0)
            o2 = jnp.concatenate([att[half : half + ROWS, col : col + HD] for col in cols], axis=0)
            total = totals[block % 2, h : h + 1, :]
            dot = jnp.sum((g2.astype(f32) * o2.astype(f32)).T, axis=0, keepdims=True)
            k = low[:end, nq + h * HD : nq + (h + 1) * HD]
            v = low[:end, nq + nk + h * HD : nq + nk + (h + 1) * HD]
            probs = jnp.exp2(matmul_t(k, q2) * log2_scale - total)
            last = jnp.where(mask_k <= mask_q, probs[n:], 0.0)
            probs = jnp.concatenate([probs[:n], last], axis=0) if n else last
            grad_scores = (probs * (matmul_t(v, g2) - dot)).astype(bf16)
            dv_part = matmul(probs.astype(bf16), g2)
            dk_part = matmul(grad_scores, q2)
            if end == keys:
                dv[h] = dv_part
                dk[h] = dk_part
            else:
                dv[h, :end, :] += dv_part
                dk[h, :end, :] += dk_part
            d = t_matmul(grad_scores, k) * score_scale
            for a, col in enumerate(cols):
                dq[half : half + ROWS, col : col + HD] = d[a * ROWS : (a + 1) * ROWS]

    keys = low.shape[0]
    for k in range(keys // (2 * ROWS)):

        @pl.when(i == k)
        def _(k=k):
            attend_back(2 * k + 1)
            attend_back(2 * k)

    c, s = cos[...], sin[...]

    def unturned(w):
        return w * c - pltpu.roll(w, HD // 2, 1) * s

    for h in range(nq // HD):
        col = slice(h * HD, (h + 1) * HD)
        grad, gp = norm_back(qraw[:, col], qgain, unturned(dq[:, col]))
        grads[:, col] = grad.astype(bf16)
        head_part[:1, :] += gp
    for h in range(nk // HD):
        col = slice(h * HD, (h + 1) * HD)
        grad, gp = norm_back(kraw[:, col], kgain, unturned(dk[h, here, :] * score_scale))
        grads[:, nq + h * HD : nq + (h + 1) * HD] = grad.astype(bf16)
        head_part[1:2, :] += gp
        grads[:, nq + nk + h * HD : nq + nk + (h + 1) * HD] = dv[h, here, :].astype(bf16)
    @pl.when(step_id == 0)
    def _():
        for copy in [load_qkv, *loads[4:]]:
            copy.wait()

    upstream = matmul_t(grads[...], wqkv[...])
    put_pair(place[2 * i], upstream.astype(bf16), mine, other)
    x = xs_all[here, :].astype(f32)
    gain_part[:1, :] += jnp.sum(upstream * x * inverse_rms(x), axis=0, keepdims=True)


def backward_attention(place, branch, tokens, weights, low, att, totals, qraw, kraw, cos, sin, head_gains):
    n, width = 4, branch[0].shape[1]
    length, nqkv = low.shape
    nq, nk = qraw.shape[1], kraw.shape[1]
    row = lambda cols: pl.BlockSpec((2 * ROWS, cols), lambda i, p: (n // 2 - 1 - i, 0))
    out = [
        ((length, nqkv), bf16, row(nqkv)),
        *[((2, ROWS, width), bf16, pl.BlockSpec((1, ROWS, width), lambda i, p: (p[n - 2 - 2 * i] % 2, 0, 0)))] * 2,
        ((length, width), bf16, row(width)),
        ((8, width), f32, whole_out((8, width))),
        ((8, HD), f32, whole_out((8, HD))),
    ]
    return pl.pallas_call(
        backward_attention_kernel,
        grid_spec=pltpu.PrefetchScalarGridSpec(
            num_scalar_prefetch=1,
            grid=(n // 2,),
            in_specs=[
                *[pl.BlockSpec(memory_space=pl.ANY)] * 9,
                whole((length, nqkv)),
                row(nq),
                pl.BlockSpec((2, 8, GROUP * ROWS), lambda i, p: (n // 2 - 1 - i, 0, 0)),
                row(nq),
                row(nk),
                row(HD),
                row(HD),
                whole((8, HD)),
            ],
            out_specs=[o[2] for o in out],
            scratch_shapes=[
                pltpu.VMEM((width, nqkv + nq), bf16),
                pltpu.VMEM((length, width), bf16),
                pltpu.VMEM((length, width), bf16),
                pltpu.VMEM((2 * ROWS, nq), bf16),
                pltpu.VMEM((nk // HD, length, HD), f32),
                pltpu.VMEM((nk // HD, length, HD), f32),
                pltpu.VMEM((2 * ROWS, nq), f32),
                pltpu.SemaphoreType.DMA((2, 4)),
                pltpu.SemaphoreType.DMA((2,)),
            ],
        ),
        out_shape=[(pltpu.HBM if k in (0, 1, 3) else jax.ShapeDtypeStruct)(o[0], o[1]) for k, o in enumerate(out)],
        compiler_params=params(48),
        cost_estimate=cost(9e9, 18e6, 3e6),
        name="backward_attention",
    )(
        place, *branch, *map(far, tokens), far(weights), far(low), far(att), far(totals),
        far(qraw), far(kraw), far(cos), far(sin), far(head_gains),
    )


def projection_weights_kernel(per_device, first, branch, grads, att, gain, second_gain, heads, out):
    wide = grads.shape[1]
    more = wide + att.shape[1]
    out[:, :wide] = t_matmul(first[...], grads[...]).astype(bf16)
    out[:, wide:more] = t_matmul(branch[...], att[...]).astype(bf16)
    rows = out.shape[0]
    same = equal_iota(rows, rows, lambda r, c: r == c)
    stands = of_head(rows, per_device, pl.program_id(0) * rows)
    lane = lax.broadcasted_iota(jnp.int32, (rows, HD), 1)
    columns = jnp.zeros((rows, HD), f32)
    for k, (mask, values) in enumerate(
        [(same, gain[:1, :]), (same, second_gain[:1, :]), (stands, heads[:1, :]), (stands, heads[1:2, :])]
    ):
        column = jnp.sum(jnp.where(mask, values, 0.0), axis=1, keepdims=True)
        columns = jnp.where(lane == k, column, columns)
    out[:, more:] = columns.astype(bf16)


def projection_weights(first, branch, grads, att, gain, second_gain, heads):
    length, width = first.shape
    wide, nq = grads.shape[1], att.shape[1]
    return pl.pallas_call(
        functools.partial(projection_weights_kernel, width // lax.axis_size(FSDP)),
        grid=(width // 512,),
        in_specs=[
            pl.BlockSpec((length, 512), lambda i: (0, i)),
            pl.BlockSpec((length, 512), lambda i: (0, i)),
            whole((length, wide)),
            whole((length, nq)),
            pl.BlockSpec((8, 512), lambda i: (0, i)),
            pl.BlockSpec((8, 512), lambda i: (0, i)),
            whole((8, HD)),
        ],
        out_specs=pl.BlockSpec((512, wide + nq + HD), lambda i: (i, 0)),
        out_shape=pltpu.HBM((width, wide + nq + HD), bf16),
        compiler_params=params(30),
        cost_estimate=cost(3.2e9, 10e6),
        name="projection_weights",
    )(far(first), far(branch), far(grads), far(att), gain, far(second_gain), heads)


def tokens_back_kernel(tokens, mine, from_core, from_z, grad_middle, gain, grad_tokens):
    u = mine[...].astype(f32) + from_core[...].astype(f32) + from_z[...].astype(f32)
    grad, _ = norm_back(tokens[...].astype(f32), gain[:1, :], u)
    grad_tokens[...] = grad_middle[...] + grad


def tokens_back(tokens, mine, from_core, from_z, grad_middle, gain):
    width = tokens.shape[1]
    half = ROWS // 2
    row = pl.BlockSpec((half, width), lambda i: (i, 0))
    first = pl.BlockSpec((None, half, width), lambda i: (0, i, 0))
    return pl.pallas_call(
        tokens_back_kernel,
        grid=(2,),
        in_specs=[row, first, first, row, row, whole((8, width))],
        out_specs=row,
        out_shape=pltpu.HBM((ROWS, width), f32),
        compiler_params=params(14),
        cost_estimate=cost(4e6, 4e6),
        name="tokens_back",
    )(far(tokens), mine, from_core, from_z, far(grad_middle), far(gain))


def close(zh, parts, summed):
    planes, both, wide = parts.shape
    rows = both // 2
    total = wide + summed.shape[1]

    def kernel(zh, parts, summed, keep, give):
        for which, out in ((zh[0], keep), (1 - zh[0], give)):
            at = pl.ds(pl.multiple_of(which * rows, rows), rows)
            added = parts[0, at, :].astype(f32)
            for k in range(1, planes):
                added = added + parts[k, at, :].astype(f32)
            out[:, :wide] = added.astype(out.dtype)
            out[:, wide:] = summed[at, :].astype(out.dtype)

    return pl.pallas_call(
        kernel,
        grid_spec=pltpu.PrefetchScalarGridSpec(
            num_scalar_prefetch=1,
            grid=(1,),
            in_specs=[whole(parts.shape), whole(summed.shape)],
            out_specs=[whole_out((rows, total))] * 2,
        ),
        out_shape=[
            jax.ShapeDtypeStruct((rows, total), f32),
            jax.ShapeDtypeStruct((rows, total), bf16),
        ],
        compiler_params=params(14),
        cost_estimate=cost(2e6, 4e6),
        name="close",
    )(zh, parts, summed)


def finish(keep, arrived, widths):
    rows = keep.shape[0]

    def kernel(keep, arrived, *outs):
        at = 0
        for out in outs:
            some = slice(at, at + out.shape[1])
            out[...] = keep[:, some] + arrived[:, some].astype(f32)
            at += out.shape[1]

    return pl.pallas_call(
        kernel,
        out_shape=[jax.ShapeDtypeStruct((rows, w), f32) for w in widths],
        compiler_params=params(8),
        cost_estimate=cost(1e5, 1e6),
        name="finish",
    )(keep, arrived)


def finish_gains(parts, rows, heads):
    def kernel(*refs):
        total = refs[0][...] + refs[1][...] + refs[2][...] + refs[3][...]
        same = equal_iota(rows, rows, lambda r, c: r == c)
        for k, out in enumerate(refs[4:]):
            line = jnp.sum(jnp.where(same, total[:, k : k + 1], 0.0), axis=0, keepdims=True)
            out[...] = line[:, : out.shape[1]]

    widths = (rows, rows, heads, heads)
    outs = pl.pallas_call(
        kernel,
        out_shape=[jax.ShapeDtypeStruct((1, w), f32) for w in widths],
        compiler_params=params(4),
        cost_estimate=cost(1e4, 1e5),
        name="finish_gains",
    )(*parts)
    return [out.reshape(-1) for out in outs]


def pack(first, second, gains, rows, heads):
    widths = [a.shape[1] for a in first], [a.shape[1] for a in second]
    split = sum(widths[0])

    def kernel(gains, *refs):
        out = refs[-1]
        at = 0
        for k, ref in enumerate(refs[:-1]):
            at += HD * (k == len(first))
            out[:, at : at + ref.shape[1]] = ref[...]
            at += ref.shape[1]
        g = gains[...].astype(f32)
        lane = lax.broadcasted_iota(jnp.int32, (rows, HD), 1)
        line = lax.broadcasted_iota(jnp.int32, (rows, HD), 0)
        columns = jnp.zeros((rows, HD), f32)
        places = [(0, rows), (rows, rows), (2 * rows, heads), (2 * rows + heads, heads)]
        for k, (start, count) in enumerate(places):
            mask = (lane == line + start) & (line < count)
            column = jnp.sum(jnp.where(mask, g, 0.0), axis=1, keepdims=True)
            columns = jnp.where(lane == k, column, columns)
        out[:, split : split + HD] = columns.astype(bf16)

    return pl.pallas_call(
        kernel,
        out_shape=jax.ShapeDtypeStruct((rows, split + HD + sum(widths[1])), bf16),
        compiler_params=params(8),
        cost_estimate=cost(1e3, 5e5),
        name="pack",
    )(gains, *map(far, first), *map(far, second))


def pair(zh, shard, other, cut, split):
    rows, wide = shard.shape

    def kernel(zh, shard, other, left, right, rest):
        for k, ref in enumerate((shard, other)):
            left[k] = ref[:, :cut]
            right[k] = ref[:, cut:split]
            rest[pl.ds(pl.multiple_of((zh[0] ^ k) * rows, rows), rows), :] = ref[:, split:]

    shapes = [(2, rows, cut), (2, rows, split - cut), (2 * rows, wide - split)]
    return pl.pallas_call(
        kernel,
        grid_spec=pltpu.PrefetchScalarGridSpec(
            num_scalar_prefetch=1,
            grid=(1,),
            in_specs=[whole((rows, wide))] * 2,
            out_specs=[whole_out(s) for s in shapes],
        ),
        out_shape=[
            *[jax.ShapeDtypeStruct(s, bf16) for s in shapes[:2]],
            pltpu.HBM(shapes[2], bf16),
        ],
        compiler_params=params(8),
        cost_estimate=cost(1e3, 1e6),
        name="pair",
    )(zh, shard, other)


def load_pieces(order, pieces, target, semaphores):
    copies = []
    half = len(pieces) // 2
    cut = pieces[0].shape[3]
    for side in range(2):
        n = 0
        for piece in pieces[side * half : (side + 1) * half]:
            rows, wide = piece.shape[2:]
            for j in range(piece.shape[0]):
                for k in range(2):
                    place = pl.multiple_of(order[side, n] * rows, rows)
                    copy = pltpu.make_async_copy(
                        piece.at[j, k],
                        target.at[pl.ds(place, rows), side * cut : side * cut + wide],
                        semaphores.at[side, n],
                    )
                    copy.start()
                    copies.append(copy)
                    n += 1
    return copies


def swapped(value, axis):
    return lax.ppermute(value, axis, [(0, 1), (1, 0)])


def tp_gather(own, over_z=None):
    over_z = swapped(own, "zl") if over_z is None else over_z
    return [own, over_z, swapped(own, "core"), swapped(over_z, "core")]


def tp_scatter(mine, other):
    from_core = swapped(other, "core")
    passed = (mine[1].astype(f32) + from_core[1].astype(f32)).astype(bf16)
    return mine, from_core, swapped(passed, "zl"), passed


def after(value, *others):
    return lax.optimization_barrier((value, *others))[0]


def sent_rows(part):
    planes = lax.axis_size(PLANE)
    blocks = part.reshape(planes, part.shape[0] // planes, part.shape[1])
    return lax.all_to_all(blocks, PLANE, 0, 0, tiled=True)


def by_distance(sides):
    done = [{0: own} for own, _ in sides]
    before = []
    for near in (True, False):
        arrived = []
        for kept, (own, axis) in zip(done, sides):
            n = lax.axis_size(axis)
            for j in range(1, n):
                if (j in (1, n - 1)) == near:
                    perm = [(s, (s - j) % n) for s in range(n)]
                    kept[j] = lax.ppermute(after(own, *before) if before else own, axis, perm)
                    arrived.append(kept[j])
        before = arrived
    return [[kept[j] for j in sorted(kept)] for kept in done]


def gathered_order():
    nx, ny = lax.axis_size("x"), lax.axis_size("y")
    x, y = (lax.axis_index("x") + jnp.arange(nx)) % nx, (lax.axis_index("y") + jnp.arange(ny)) % ny
    z = lax.axis_index("zh") ^ jnp.arange(2)
    block = lambda x, y: ((x * ny + y) * 2 + z).reshape(-1)
    left = block(x[None, :, None], y[:, None, None])
    right = block(x[:, None, None], y[None, :, None])
    return jnp.stack([left, right]).astype(jnp.int32)


def rotary_tables(length):
    midway = HD // 2
    frequency = 1.0 / rope_base ** (np.arange(midway) * 2.0 / HD)
    angles = np.arange(length)[:, None] * frequency[None, :]
    cos, sin = np.cos(angles), np.sin(angles)
    tables = np.concatenate([cos, cos], axis=1), np.concatenate([-sin, sin], axis=1)
    return [jnp.asarray(t.astype(np.float32)) for t in tables]


def local(
    tokens,
    attention_gain,
    query_weight,
    key_weight,
    value_weight,
    query_gain,
    key_gain,
    output_weight,
    feed_gain,
    gate_weight,
    up_weight,
    down_weight,
    cotangent,
):
    width = tokens.shape[2]
    nq, nk = query_weight.shape[1], key_weight.shape[1]
    units = gate_weight.shape[1]
    rows = query_weight.shape[0]
    x = tokens[0]
    dy = cotangent[0]
    zl, core = lax.axis_index("zl"), lax.axis_index("core")
    block = jnp.arange(4, dtype=jnp.int32)
    place = ((block % 2) ^ core) * 2 + ((block // 2) ^ zl)
    block_of = ((block // 2) ^ core) + ((block % 2) ^ zl) * 2
    place = jnp.concatenate([place, block_of]).astype(jnp.int32)
    cos, sin = rotary_tables(4 * ROWS)

    heads = query_gain.shape[0]
    gains = jnp.concatenate([attention_gain, feed_gain, query_gain, key_gain])
    gains = jnp.pad(gains, (0, HD - gains.shape[0]))[None]
    shard = pack(
        [query_weight, key_weight, value_weight, output_weight],
        [gate_weight, up_weight, down_weight],
        gains,
        rows,
        heads,
    )
    over_zh = swapped(shard, "zh")
    split = nq + 2 * nk + nq + HD
    left, right, feed = pair(lax.axis_index("zh").reshape(1), shard, over_zh, nq + nk, split)
    order = gathered_order()
    left, right = by_distance([(left, "x"), (right, "y")])
    token_blocks = tp_gather(after(x, over_zh))
    left, right = by_distance([(jnp.stack(left), "y"), (jnp.stack(right), "x")])
    feed = lax.all_gather(after(feed, left[1], left[-1], right[1], right[-1]), PLANE, axis=0, tiled=True)
    grads_over_z = swapped(after(dy, *left, *right), "zl")

    first, qraw, kraw, low, att, totals, mine, other, gains, head_gains, weights = forward_attention(
        place, order, token_blocks, left + right, nq, nk, cos, sin
    )
    grad_blocks = tp_gather(dy, after(grads_over_z, other))
    other = after(other, grads_over_z)
    mine, from_core, from_z, _ = tp_scatter(mine, other)
    middle, second = middle_step(x, mine, from_core, from_z, gains)
    over_z = swapped(second, "zl")
    near = feed_step([second, swapped(second, "core")], grad_blocks[::2], feed, units)
    second_blocks = tp_gather(second, after(over_z, near[1]))
    far_ones = feed_step(second_blocks[1::2], grad_blocks[1::2], feed, units)
    hidden, grad_units = [near[0], far_ones[0]], [near[1], far_ones[1]]
    from_core = swapped(near[3], "core")
    passed = (after(far_ones[2], from_core).astype(f32) + swapped(far_ones[3], "core").astype(f32)).astype(bf16)
    from_z = swapped(passed, "zl")
    grad_units[0] = after(grad_units[0], passed)
    feed_grads = feed_weights(second_blocks, grad_blocks, grad_units, hidden)
    from_z, feed_grads = lax.optimization_barrier((from_z, feed_grads))
    grad_middle, branch, feed_gain_part = middle_back(middle, near[2], from_core, from_z, dy, gains)
    feed_sums = lax.psum_scatter(feed_grads, "x", scatter_dimension=0, tiled=True)
    feed_sums = lax.psum_scatter(feed_sums, "y", scatter_dimension=0, tiled=True)
    over_z = swapped(branch, "zl")
    mine, other = feed_out([after(hidden[0], branch), hidden[1]], feed)
    branch_blocks = tp_gather(branch, after(over_z, other))
    mine, from_core, from_z, _ = tp_scatter(mine, other)
    output = middle + mine[0].astype(f32) + from_core[0].astype(f32) + from_z.astype(f32)
    output = output.astype(bf16)

    grads, mine, other, branch_rows, gain_part, head_part = backward_attention(
        place, branch_blocks, token_blocks, weights, low, att, totals, qraw, kraw, cos, sin, head_gains
    )
    projection_grads = projection_weights(
        first, branch_rows, grads, att, gain_part, feed_gain_part, head_part
    )
    mine, from_core, from_z, _ = tp_scatter(mine, other)
    tokens_grad = tokens_back(
        x, mine, from_core, after(from_z, projection_grads), grad_middle, gains
    )
    parts = after(sent_rows(projection_grads), tokens_grad, output)
    keep, give = close(lax.axis_index("zh").reshape(1), parts, after(feed_sums, tokens_grad, output))
    widths = (nq, nk, nk, nq, HD, units, units, units)
    query, key, value, out, columns, gate, up, down = finish(keep, swapped(give, "zh"), widths)
    both = ("zl", "core")
    across = lax.ppermute(columns, both, [(s, 3 - s) for s in range(4)])
    parts = (columns, swapped(columns, "zl"), swapped(columns, "core"), across)
    first_sum, second_sum, query_sum, key_sum = finish_gains(parts, rows, heads)

    return (
        output[None],
        tokens_grad[None],
        first_sum,
        query,
        key,
        value,
        query_sum,
        key_sum,
        out,
        second_sum,
        gate,
        up,
        down,
    )


def solution(mesh):
    fsdp, tp = mesh.devices.shape
    cut = {32: (4, 4, 2), 2: (1, 1, 2), 1: (1, 1, 1)}[fsdp]
    fine = Mesh(mesh.devices.reshape(*cut, 2, tp // 2), EVERY)
    split = ("zl", "core")
    data = P(FSDP, split, None)
    matrix = P(FSDP, split)
    vector = P(FSDP)
    return jax.shard_map(
        local,
        mesh=fine,
        in_specs=(
            data, vector, matrix, matrix, matrix, vector, vector,
            matrix, vector, matrix, matrix, matrix, data,
        ),
        out_specs=(
            data, data, vector, matrix, matrix, matrix, vector, vector,
            matrix, vector, matrix, matrix, matrix,
        ),
        check_vma=False,
    )
```

profile of v0, /device:TPU:28, one launch (start us, length us, event | category | flops | bytes accessed | tf_op | source)
XLA Modules:
  0.0 284.3 jit_solution(10430868106176528385)
XLA Ops:
  9.0 4.0 %collective-permute-start = (bf16[32,3968]{1,0:T(8,128)(2,1)S(1)}, bf16[32,3968]{1,0:T(8,128)(2,1)S(1)}, u32[]{:S(2)}, u32[]{:S(2)}) collective-permute-start(bf16[32,3968]{1,0:T(8,128)(2,1)S(1)} %pack.1.shard), channel_id=1, source_target_pairs={{0,4},{4,0},{1,5},{5,1},{2,6},{6,2},{3,7},{7,3},{8,12},{12,8},{9,1... | collective-permute-start | bytes 761864 | tf_op jit(solution)/shard_map/ppermute | solution.py:825
  13.0 6.1 %collective-permute-done.other = bf16[32,3968]{1,0:T(8,128)(2,1)S(1)} collective-permute-done((bf16[32,3968]{1,0:T(8,128)(2,1)S(1)}, bf16[32,3968]{1,0:T(8,128)(2,1)S(1)}, u32[]{:S(2)}, u32[]{:S(2)}) %collective-permute-start) | collective-permute-done | bytes 253984 | tf_op jit(solution)/shard_map/ppermute | solution.py:825
  23.9 2.6 collective-permute-done.5
  29.8 4.3 %collective-permute-done.11 = bf16[2,32,896]{2,1,0:T(8,128)(2,1)S(1)} collective-permute-done((bf16[2,32,896]{2,1,0:T(8,128)(2,1)S(1)}, bf16[2,32,896]{2,1,0:T(8,128)(2,1)S(1)}, u32[]{:S(2)}, u32[]{:S(2)}) %collective-permute-start.11) | collective-permute-done | bytes 114720 | tf_op jit(solution)/shard_map/ppermute | solution.py:859
  36.3 2.2 collective-permute-start.10
  38.5 5.6 %collective-permute-done.10.refs_7_ = bf16[4,2,32,768]{3,2,1,0:T(8,128)(2,1)S(1)} collective-permute-done((bf16[4,2,32,768]{3,2,1,0:T(8,128)(2,1)S(1)}, bf16[4,2,32,768]{3,2,1,0:T(8,128)(2,1)S(1)}, u32[]{:S(2)}, u32[]{:S(2)}) %collective-permute-start.10) | collective-permute-done | bytes 393248 | tf_op jit(solution)/shard_map/ppermute | solution.py:859
  44.9 2.6 collective-permute-done.9.refs_5_
  51.2 6.5 %collective-permute-done.1.refs_1_.refs_5_ = bf16[256,1024]{1,0:T(8,128)(2,1)S(1)} collective-permute-done((bf16[256,1024]{1,0:T(8,128)(2,1)}, bf16[256,1024]{1,0:T(8,128)(2,1)S(1)}, u32[]{:S(2)}, u32[]{:S(2)}) %collective-permute-start.1) | collective-permute-done | bytes 524320 | tf_op jit(solution)/shard_map/ppermute | solution.py:825
  57.8 2.5 collective-permute-done.14.refs_6_
  65.6 18.5 %forward_attention.1 = (bf16[1024,1024]{1,0:T(8,128)(2,1)}, f32[1024,512]{1,0:T(8,128)}, f32[1024,256]{1,0:T(8,128)}, bf16[1024,1024]{1,0:T(8,128)(2,1)}, bf16[1...) custom-call(s32[8]{0:T(128)S(1)} %pad_add_fusion.1.place, ...), custom_call_target="tpu_custom_call" | custom-call | flops 875000000 | bytes 2000000 | tf_op jit(solution)/shard_map/forward_attention/pallas_call | solution.py:246
  84.2 2.6 collective-permute-done.17.from_core
  88.4 12.7 %collective-permute-done.18.from_z = bf16[256,1024]{1,0:T(8,128)(2,1)S(1)} collective-permute-done((bf16[256,1024]{1,0:T(8,128)(2,1)S(1)}, bf16[256,1024]{1,0:T(8,128)(2,1)S(1)}, u32[]{:S(2)}, u32[]{:S(2)}) %collective-permute-start.18) | collective-permute-done | bytes 524320 | tf_op jit(solution)/shard_map/ppermute | solution.py:825
  106.4 9.1 %feed_step.2 = (bf16[512,768]{1,0:T(8,128)(2,1)}, bf16[512,1536]{1,0:T(8,128)(2,1)}, bf16[256,1024]{1,0:T(8,128)(2,1)S(1)}, bf16[256,1024]{1,0:T(8,128)(2,1)S(1)}) custom-call(bf16[256,1024]{1,0:T(8,128)(2,1)S(1)} %get-tuple-element.94.refs_0_, bf16[256,1024]{1,0:T(8,128)(2,1)S(1)} %collective-permute-done.19.refs_1_.refs_2_, bf16[256,1024]{1,0:T(8,128)(2,1)} %bitcast.38, ...), custom_call_target="tpu_custom_call" | custom-call | flops 500000000 | bytes 1000000 | tf_op jit(solution)/shard_map/feed_step/pallas_call | solution.py:338
  115.5 2.2 collective-permute-done.22.refs_0_.refs_1_
  119.6 9.2 %feed_step.3 = (bf16[512,768]{1,0:T(8,128)(2,1)}, bf16[512,1536]{1,0:T(8,128)(2,1)}, bf16[256,1024]{1,0:T(8,128)(2,1)S(1)}, bf16[256,1024]{1,0:T(8,128)(2,1)S(1)}) custom-call(bf16[256,1024]{1,0:T(8,128)(2,1)S(1)} %collective-permute-done.22.refs_0_.refs_1_, bf16[256,1024]{1,0:T(8,128)(2,1)S(1)} %collective-permute-done.23.refs_1_.refs_3_, ...), custom_call_target="tpu_custom_call" | custom-call | flops 500000000 | bytes 1000000 | tf_op jit(solution)/shard_map/feed_step/pallas_call | solution.py:338
  132.4 10.0 %feed_weights.1 = bf16[1024,2304]{1,0:T(8,128)(2,1)} custom-call(bf16[256,1024]{1,0:T(8,128)(2,1)} %copy-done.4, bf16[256,1024]{1,0:T(8,128)(2,1)} %copy-done.6, bf16[256,1024]{1,0:T(8,128)(2,1)} %copy-done.5, bf16[256,1024]{1,0:T(8,128)(2,1)} %copy-done.7, bf16[256,1024]{1,0:T(8,128)(2,1)} %bitcast.39, ...), custom_call_target="tpu_custom_call" | custom-call | flops 600000000 | bytes 1750000 | tf_op jit(solution)/shard_map/feed_weights/pallas_call | solution.py:403
  142.4 2.7 collective-permute-done.26.from_z
  145.1 2.7 middle_back.1
  149.3 4.0 %feed_out.1 = (bf16[2,256,1024]{2,1,0:T(8,128)(2,1)S(1)}, bf16[2,256,1024]{2,1,0:T(8,128)(2,1)S(1)}) custom-call(bf16[512,768]{1,0:T(8,128)(2,1)} %get-tuple-element.111.refs_10_.first, bf16[512,768]{1,0:T(8,128)(2,1)} %get-tuple-element.108.refs_11_.then, bf16[1024,2304]{1,0:T(8,128)(2,1)} %all-gather.2.cloned.1.call-done.refs_4_.wd), custom_call_target="tpu_custom_call" | custom-call | flops 200000000 | bytes 625000 | tf_op jit(solution)/shard_map/feed_out/pallas_call | solution.py:372
  155.2 5.8 %collective-permute-done.29.refs_1_ = bf16[256,1024]{1,0:T(8,128)(2,1)S(1)} collective-permute-done((bf16[256,1024]{1,0:T(8,128)(2,1)S(1)}, bf16[256,1024]{1,0:T(8,128)(2,1)S(1)}, u32[]{:S(2)}, u32[]{:S(2)}) %collective-permute-start.29) | collective-permute-done | bytes 524320 | tf_op jit(solution)/shard_map/ppermute | solution.py:825
  162.9 21.7 %backward_attention.1 = (bf16[1024,1024]{1,0:T(8,128)(2,1)}, bf16[2,256,1024]{2,1,0:T(8,128)(2,1)}, bf16[2,256,1024]{2,1,0:T(8,128)(2,1)S(1)}, bf16[1024,1024]{1...) custom-call(s32[8]{0:T(128)S(1)} %pad_add_fusion.1.place, ...), custom_call_target="tpu_custom_call" | custom-call | flops 1124999936 | bytes 2250000 | tf_op jit(solution)/shard_map/backward_attention/pallas_call | solution.py:570
  184.7 8.3 %projection_weights.1 = bf16[1024,1664]{1,0:T(8,128)(2,1)} custom-call(bf16[1024,1024]{1,0:T(8,128)(2,1)} %get-tuple-element.124.first, bf16[1024,1024]{1,0:T(8,128)(2,1)} %get-tuple-element.125.branch, bf16[1024,1024]{1,0:T(8,128)(2,1)} %get-tuple-element.126.grads, bf16[1024,512]{1,0:T(8,128)(2,1)} %get-tuple-element.117.refs_10_.att, ...), custom_call_target="tpu_custom_call" | custom-call | flops 400000000 | bytes 1250000 | tf_op jit(solution)/shard_map/projection_weights/pallas_call | solution.py:630
  193.0 6.9 %all-to-all-start = ((bf16[16,64,1664]{2,1,0:T(8,128)(2,1)}), bf16[16,64,1664]{2,1,0:T(8,128)(2,1)S(1)}, u32[]{:S(2)}, u32[]{:S(2)}) async-start(bf16[16,64,1664]{2,1,0:T(8,128)(2,1)} %bitcast.36), calls=%async_computation | async-start | bytes 6815744 | tf_op jit(solution)/shard_map/all_to_all | solution.py:846
  201.3 2.4 collective-permute-done.27
  208.4 11.3 %collective-permute-done.28 = bf16[256,1024]{1,0:T(8,128)(2,1)S(1)} collective-permute-done((bf16[256,1024]{1,0:T(8,128)(2,1)S(1)}, bf16[256,1024]{1,0:T(8,128)(2,1)S(1)}, u32[]{:S(2)}, u32[]{:S(2)}) %collective-permute-start.28) | collective-permute-done | bytes 524320 | tf_op jit(solution)/shard_map/ppermute | solution.py:825
  220.9 9.3 %collective-permute-done.33.from_z = bf16[256,1024]{1,0:T(8,128)(2,1)S(1)} collective-permute-done((bf16[256,1024]{1,0:T(8,128)(2,1)S(1)}, bf16[256,1024]{1,0:T(8,128)(2,1)S(1)}, u32[]{:S(2)}, u32[]{:S(2)}) %collective-permute-start.33) | collective-permute-done | bytes 524320 | tf_op jit(solution)/shard_map/ppermute | solution.py:825
  230.2 2.6 tokens_back.1
  232.8 19.1 %all-to-all-done.parts = bf16[16,64,1664]{2,1,0:T(8,128)(2,1)S(1)} async-done(((bf16[16,64,1664]{2,1,0:T(8,128)(2,1)}), bf16[16,64,1664]{2,1,0:T(8,128)(2,1)S(1)}, u32[]{:S(2)}, u32[]{:S(2)}) %all-to-all-start) | async-done | bytes 3407904 | tf_op jit(solution)/shard_map/all_to_all | solution.py:846
  251.8 4.0 %reduce-scatter.5.cloned.1.call-done.summed = bf16[64,2304]{1,0:T(8,128)(2,1)} async-done(((bf16[256,2304]{1,0:T(8,128)(2,1)}), bf16[64,2304]{1,0:T(8,128)(2,1)}) %reduce-scatter.5.cloned.1.call-update) | async-done | bytes 294928 | tf_op jit(solution)/shard_map/reduce_scatter | solution.py:952
  257.3 6.3 %collective-permute-start.34 = (bf16[32,3968]{1,0:T(8,128)(2,1)S(1)}, bf16[32,3968]{1,0:T(8,128)(2,1)S(1)}, u32[]{:S(2)}, u32[]{:S(2)}) collective-permute-start(bf16[32,3968]{1,0:T(8,128)(2,1)S(1)} %get-tuple-element.136), channel_id=1, source_target_pairs={{0,4},{4,0},{1,5},{5,1},{2,6},{6,2},{3,7},{7,3},{8,12},{12,8},{9,1... | collective-permute-start | bytes 761864 | tf_op jit(solution)/shard_map/ppermute | solution.py:825
  263.6 6.4 %collective-permute-done.34.arrived = bf16[32,3968]{1,0:T(8,128)(2,1)S(1)} collective-permute-done((bf16[32,3968]{1,0:T(8,128)(2,1)S(1)}, bf16[32,3968]{1,0:T(8,128)(2,1)S(1)}, u32[]{:S(2)}, u32[]{:S(2)}) %collective-permute-start.34) | collective-permute-done | bytes 253984 | tf_op jit(solution)/shard_map/ppermute | solution.py:825
  274.0 2.9 %collective-permute-done.35.refs_1_ = f32[32,128]{1,0:T(8,128)S(1)} collective-permute-done((f32[32,128]{1,0:T(8,128)S(1)}, f32[32,128]{1,0:T(8,128)S(1)}, u32[]{:S(2)}, u32[]{:S(2)}) %collective-permute-start.35) | collective-permute-done | bytes 16416 | tf_op jit(solution)/shard_map/ppermute | solution.py:825
  (137 shorter events, 52.7 us)
Async XLA Ops:
  7.2 99.2 %all-gather.2.cloned.1.call-start = ((), (), s32[]{:S(2)}) async-start(), calls=%async_computation.3 | async-start | bytes 5013504 | tf_op jit(solution)/shard_map/all_gather | solution.py:929
  9.0 10.1 %collective-permute-start = (bf16[32,3968]{1,0:T(8,128)(2,1)S(1)}, bf16[32,3968]{1,0:T(8,128)(2,1)S(1)}, u32[]{:S(2)}, u32[]{:S(2)}) collective-permute-start(bf16[32,3968]{1,0:T(8,128)(2,1)S(1)} %pack.1.shard), channel_id=1, source_target_pairs={{0,4},{4,0},{1,5},{5,1},{2,6},{6,2},{3,7},{7,3},{8,12},{12,8},{9,1... | collective-permute-start | bytes 761864 | tf_op jit(solution)/shard_map/ppermute | solution.py:825
  19.9 7.8 %collective-permute-start.7 = (bf16[2,32,896]{2,1,0:T(8,128)(2,1)S(1)}, bf16[2,32,896]{2,1,0:T(8,128)(2,1)S(1)}, u32[]{:S(2)}, u32[]{:S(2)}) collective-permute-start(bf16[2,32,896]{2,1,0:T(8,128)(2,1)S(1)} %get-tuple-element.85), channel_id=1, source_target_pairs={{0,8},{8,16},{16,24},{24,0},{1,9},{9,17},{17,25},{25,1},{2,10},{10... | collective-permute-start | bytes 344072 | tf_op jit(solution)/shard_map/ppermute | solution.py:859
  20.1 7.6 %collective-permute-start.6 = (bf16[2,32,896]{2,1,0:T(8,128)(2,1)S(1)}, bf16[2,32,896]{2,1,0:T(8,128)(2,1)S(1)}, u32[]{:S(2)}, u32[]{:S(2)}) collective-permute-start(bf16[2,32,896]{2,1,0:T(8,128)(2,1)S(1)} %get-tuple-element.85), channel_id=1, source_target_pairs={{0,24},{8,0},{16,8},{24,16},{1,25},{9,1},{17,9},{25,17},{2,26},{10... | collective-permute-start | bytes 344072 | tf_op jit(solution)/shard_map/ppermute | solution.py:859
  21.9 4.6 %collective-permute-start.5 = (bf16[2,32,768]{2,1,0:T(8,128)(2,1)S(1)}, bf16[2,32,768]{2,1,0:T(8,128)(2,1)S(1)}, u32[]{:S(2)}, u32[]{:S(2)}) collective-permute-start(bf16[2,32,768]{2,1,0:T(8,128)(2,1)S(1)} %get-tuple-element.84), channel_id=1, source_target_pairs={{0,32},{32,64},{64,96},{96,0},{1,33},{33,65},{65,97},{97,1},{2,34}... | collective-permute-start | bytes 294920 | tf_op jit(solution)/shard_map/ppermute | solution.py:859
  23.1 4.6 %collective-permute-start.4 = (bf16[2,32,768]{2,1,0:T(8,128)(2,1)S(1)}, bf16[2,32,768]{2,1,0:T(8,128)(2,1)S(1)}, u32[]{:S(2)}, u32[]{:S(2)}) collective-permute-start(bf16[2,32,768]{2,1,0:T(8,128)(2,1)S(1)} %get-tuple-element.84), channel_id=1, source_target_pairs={{0,96},{32,0},{64,32},{96,64},{1,97},{33,1},{65,33},{97,65},{2,98}... | collective-permute-start | bytes 294920 | tf_op jit(solution)/shard_map/ppermute | solution.py:859
  27.7 6.3 %collective-permute-start.11 = (bf16[2,32,896]{2,1,0:T(8,128)(2,1)S(1)}, bf16[2,32,896]{2,1,0:T(8,128)(2,1)S(1)}, u32[]{:S(2)}, u32[]{:S(2)}) collective-permute-start(bf16[2,32,896]{2,1,0:T(8,128)(2,1)S(1)} %get-tuple-element.85), channel_id=1, source_target_pairs={{0,16},{8,24},{16,0},{24,8},{1,17},{9,25},{17,1},{25,9},{2,18},{10... | collective-permute-start | bytes 344072 | tf_op jit(solution)/shard_map/ppermute | solution.py:859
  29.0 7.2 %collective-permute-start.8 = (bf16[2,32,768]{2,1,0:T(8,128)(2,1)S(1)}, bf16[2,32,768]{2,1,0:T(8,128)(2,1)S(1)}, u32[]{:S(2)}, u32[]{:S(2)}) collective-permute-start(bf16[2,32,768]{2,1,0:T(8,128)(2,1)S(1)} %get-tuple-element.84), channel_id=1, source_target_pairs={{0,64},{32,96},{64,0},{96,32},{1,65},{33,97},{65,1},{97,33},{2,66}... | collective-permute-start | bytes 294920 | tf_op jit(solution)/shard_map/ppermute | solution.py:859
  34.1 14.1 %collective-permute-start.13 = (bf16[4,2,32,896]{3,2,1,0:T(8,128)(2,1)S(1)}, bf16[4,2,32,896]{3,2,1,0:T(8,128)(2,1)S(1)}, u32[]{:S(2)}, u32[]{:S(2)}) collective-permute-start(bf16[4,2,32,896]{3,2,1,0:T(8,128)(2,1)S(1)} %pad_maximum_fusion.refs_8_), channel_id=1, source_target_pairs={{0,32},{32,64},{64,96},{96,0},{1,33},{33,65},{65,97},{97,1},{2,34}... | collective-permute-start | bytes 1376264 | tf_op jit(solution)/shard_map/ppermute | solution.py:859
  35.9 12.4 %collective-permute-start.12 = (bf16[4,2,32,896]{3,2,1,0:T(8,128)(2,1)S(1)}, bf16[4,2,32,896]{3,2,1,0:T(8,128)(2,1)S(1)}, u32[]{:S(2)}, u32[]{:S(2)}) collective-permute-start(bf16[4,2,32,896]{3,2,1,0:T(8,128)(2,1)S(1)} %pad_maximum_fusion.refs_8_), channel_id=1, source_target_pairs={{0,96},{32,0},{64,32},{96,64},{1,97},{33,1},{65,33},{97,65},{2,98}... | collective-permute-start | bytes 1376264 | tf_op jit(solution)/shard_map/ppermute | solution.py:859
  36.3 7.8 %collective-permute-start.10 = (bf16[4,2,32,768]{3,2,1,0:T(8,128)(2,1)S(1)}, bf16[4,2,32,768]{3,2,1,0:T(8,128)(2,1)S(1)}, u32[]{:S(2)}, u32[]{:S(2)}) collective-permute-start(bf16[4,2,32,768]{3,2,1,0:T(8,128)(2,1)S(1)} %pad_maximum_fusion.1.refs_4_), channel_id=1, source_target_pairs={{0,8},{8,16},{16,24},{24,0},{1,9},{9,17},{17,25},{25,1},{2,10},{10... | collective-permute-start | bytes 1179656 | tf_op jit(solution)/shard_map/ppermute | solution.py:859
  38.5 9.0 %collective-permute-start.9 = (bf16[4,2,32,768]{3,2,1,0:T(8,128)(2,1)S(1)}, bf16[4,2,32,768]{3,2,1,0:T(8,128)(2,1)S(1)}, u32[]{:S(2)}, u32[]{:S(2)}) collective-permute-start(bf16[4,2,32,768]{3,2,1,0:T(8,128)(2,1)S(1)} %pad_maximum_fusion.1.refs_4_), channel_id=1, source_target_pairs={{0,24},{8,0},{16,8},{24,16},{1,25},{9,1},{17,9},{25,17},{2,26},{10... | collective-permute-start | bytes 1179656 | tf_op jit(solution)/shard_map/ppermute | solution.py:859
  48.3 151.8 %reduce-scatter.3.cloned.1.call-start = ((), (), s32[]{:S(2)}) async-start(), calls=%async_computation.4 | async-start | bytes 5898240 | tf_op jit(solution)/shard_map/reduce_scatter | solution.py:951
  48.3 9.5 %collective-permute-start.1 = (bf16[256,1024]{1,0:T(8,128)(2,1)}, bf16[256,1024]{1,0:T(8,128)(2,1)S(1)}, u32[]{:S(2)}, u32[]{:S(2)}) collective-permute-start(bf16[256,1024]{1,0:T(8,128)(2,1)} %bitcast.refs_0_.tokens.refs_4_), channel_id=1, source_target_pairs={{0,2},{2,0},{1,3},{3,1},{4,6},{6,4},{5,7},{7,5},{8,10},{10,8},{9,1... | collective-permute-start | bytes 1572872 | tf_op jit(solution)/shard_map/ppermute | solution.py:825
  49.7 11.3 %collective-permute-start.15 = (bf16[4,2,32,896]{3,2,1,0:T(8,128)(2,1)S(1)}, bf16[4,2,32,896]{3,2,1,0:T(8,128)(2,1)}, u32[]{:S(2)}, u32[]{:S(2)}) collective-permute-start(bf16[4,2,32,896]{3,2,1,0:T(8,128)(2,1)S(1)} %pad_maximum_fusion.refs_8_), channel_id=1, source_target_pairs={{0,64},{32,96},{64,0},{96,32},{1,65},{33,97},{65,1},{97,33},{2,66}... | collective-permute-start | bytes 1376264 | tf_op jit(solution)/shard_map/ppermute | solution.py:859
  51.0 9.3 %collective-permute-start.14 = (bf16[4,2,32,768]{3,2,1,0:T(8,128)(2,1)S(1)}, bf16[4,2,32,768]{3,2,1,0:T(8,128)(2,1)S(1)}, u32[]{:S(2)}, u32[]{:S(2)}) collective-permute-start(bf16[4,2,32,768]{3,2,1,0:T(8,128)(2,1)S(1)} %pad_maximum_fusion.1.refs_4_), channel_id=1, source_target_pairs={{0,16},{8,24},{16,0},{24,8},{1,17},{9,25},{17,1},{25,9},{2,18},{10... | collective-permute-start | bytes 1179656 | tf_op jit(solution)/shard_map/ppermute | solution.py:859
  51.2 11.1 %collective-permute-start.2 = (bf16[256,1024]{1,0:T(8,128)(2,1)}, bf16[256,1024]{1,0:T(8,128)(2,1)S(1)}, u32[]{:S(2)}, u32[]{:S(2)}) collective-permute-start(bf16[256,1024]{1,0:T(8,128)(2,1)} %bitcast.refs_0_.tokens.refs_4_), channel_id=1, source_target_pairs={{0,1},{1,0},{2,3},{3,2},{4,5},{5,4},{6,7},{7,6},{8,9},{9,8},{10,11... | collective-permute-start | bytes 1572872 | tf_op jit(solution)/shard_map/ppermute | solution.py:825
  61.0 23.1 %collective-permute-start.16 = (bf16[256,1024]{1,0:T(8,128)(2,1)}, bf16[256,1024]{1,0:T(8,128)(2,1)}, u32[]{:S(2)}, u32[]{:S(2)}) collective-permute-start(bf16[256,1024]{1,0:T(8,128)(2,1)} %bitcast.37), channel_id=1, source_target_pairs={{0,2},{2,0},{1,3},{3,1},{4,6},{6,4},{5,7},{7,5},{8,10},{10,8},{9,1... | collective-permute-start | bytes 1572872 | tf_op jit(solution)/shard_map/ppermute | solution.py:825
  87.1 14.0 %collective-permute-start.18 = (bf16[256,1024]{1,0:T(8,128)(2,1)S(1)}, bf16[256,1024]{1,0:T(8,128)(2,1)S(1)}, u32[]{:S(2)}, u32[]{:S(2)}) collective-permute-start(bf16[256,1024]{1,0:T(8,128)(2,1)S(1)} %fusion.2), channel_id=1, source_target_pairs={{0,2},{2,0},{1,3},{3,1},{4,6},{6,4},{5,7},{7,5},{8,10},{10,8},{9,1... | collective-permute-start | bytes 1572872 | tf_op jit(solution)/shard_map/ppermute | solution.py:825
  88.4 16.8 %collective-permute-start.20 = (bf16[256,1024]{1,0:T(8,128)(2,1)S(1)}, bf16[256,1024]{1,0:T(8,128)(2,1)S(1)}, u32[]{:S(2)}, u32[]{:S(2)}) collective-permute-start(bf16[256,1024]{1,0:T(8,128)(2,1)S(1)} %bitcast.41), channel_id=1, source_target_pairs={{0,1},{1,0},{2,3},{3,2},{4,5},{5,4},{6,7},{7,6},{8,9},{9,8},{10,11... | collective-permute-start | bytes 1572872 | tf_op jit(solution)/shard_map/ppermute | solution.py:825
  103.3 14.3 %collective-permute-start.22 = (bf16[256,1024]{1,0:T(8,128)(2,1)S(1)}, bf16[256,1024]{1,0:T(8,128)(2,1)S(1)}, u32[]{:S(2)}, u32[]{:S(2)}) collective-permute-start(bf16[256,1024]{1,0:T(8,128)(2,1)S(1)} %get-tuple-element.94.refs_0_), channel_id=1, source_target_pairs={{0,2},{2,0},{1,3},{3,1},{4,6},{6,4},{5,7},{7,5},{8,10},{10,8},{9,1... | collective-permute-start | bytes 1572872 | tf_op jit(solution)/shard_map/ppermute | solution.py:825
  104.6 13.6 %collective-permute-start.24 = (bf16[256,1024]{1,0:T(8,128)(2,1)}, bf16[256,1024]{1,0:T(8,128)(2,1)S(1)}, u32[]{:S(2)}, u32[]{:S(2)}) collective-permute-start(bf16[256,1024]{1,0:T(8,128)(2,1)} %collective-permute-done.16.refs_2_.refs_5_), channel_id=1, source_target_pairs={{0,1},{1,0},{2,3},{3,2},{4,5},{5,4},{6,7},{7,6},{8,9},{9,8},{10,11... | collective-permute-start | bytes 1572872 | tf_op jit(solution)/shard_map/ppermute | solution.py:825
  117.7 11.4 %collective-permute-start.21 = (bf16[256,1024]{1,0:T(8,128)(2,1)S(1)}, bf16[256,1024]{1,0:T(8,128)(2,1)S(1)}, u32[]{:S(2)}, u32[]{:S(2)}) collective-permute-start(bf16[256,1024]{1,0:T(8,128)(2,1)S(1)} %get-tuple-element.99), channel_id=1, source_target_pairs={{0,1},{1,0},{2,3},{3,2},{4,5},{5,4},{6,7},{7,6},{8,9},{9,8},{10,11... | collective-permute-start | bytes 1572872 | tf_op jit(solution)/shard_map/ppermute | solution.py:825
  131.0 14.1 %collective-permute-start.26 = (bf16[256,1024]{1,0:T(8,128)(2,1)S(1)}, bf16[256,1024]{1,0:T(8,128)(2,1)S(1)}, u32[]{:S(2)}, u32[]{:S(2)}) collective-permute-start(bf16[256,1024]{1,0:T(8,128)(2,1)S(1)} %add_convert_fusion.2), channel_id=1, source_target_pairs={{0,2},{2,0},{1,3},{3,1},{4,6},{6,4},{5,7},{7,5},{8,10},{10,8},{9,1... | collective-permute-start | bytes 1572872 | tf_op jit(solution)/shard_map/ppermute | solution.py:825
  147.9 13.1 %collective-permute-start.29 = (bf16[256,1024]{1,0:T(8,128)(2,1)S(1)}, bf16[256,1024]{1,0:T(8,128)(2,1)S(1)}, u32[]{:S(2)}, u32[]{:S(2)}) collective-permute-start(bf16[256,1024]{1,0:T(8,128)(2,1)S(1)} %get-tuple-element.110.refs_0_), channel_id=1, source_target_pairs={{0,2},{2,0},{1,3},{3,1},{4,6},{6,4},{5,7},{7,5},{8,10},{10,8},{9,1... | collective-permute-start | bytes 1572872 | tf_op jit(solution)/shard_map/ppermute | solution.py:825
  149.1 11.9 %collective-permute-start.30 = (bf16[256,1024]{1,0:T(8,128)(2,1)S(1)}, bf16[256,1024]{1,0:T(8,128)(2,1)S(1)}, u32[]{:S(2)}, u32[]{:S(2)}) collective-permute-start(bf16[256,1024]{1,0:T(8,128)(2,1)S(1)} %get-tuple-element.110.refs_0_), channel_id=1, source_target_pairs={{0,1},{1,0},{2,3},{3,2},{4,5},{5,4},{6,7},{7,6},{8,9},{9,8},{10,11... | collective-permute-start | bytes 1572872 | tf_op jit(solution)/shard_map/ppermute | solution.py:825
  193.0 58.8 %all-to-all-start = ((bf16[16,64,1664]{2,1,0:T(8,128)(2,1)}), bf16[16,64,1664]{2,1,0:T(8,128)(2,1)S(1)}, u32[]{:S(2)}, u32[]{:S(2)}) async-start(bf16[16,64,1664]{2,1,0:T(8,128)(2,1)} %bitcast.36), calls=%async_computation | async-start | bytes 6815744 | tf_op jit(solution)/shard_map/all_to_all | solution.py:846
  200.0 55.9 %reduce-scatter.5.cloned.1.call-start = ((), (), s32[]{:S(2)}) async-start(), calls=%async_computation.5 | async-start | bytes 1474560 | tf_op jit(solution)/shard_map/reduce_scatter | solution.py:952
  200.8 5.6 %collective-permute-start.32 = (bf16[2,256,1024]{2,1,0:T(8,128)(2,1)}, bf16[2,256,1024]{2,1,0:T(8,128)(2,1)S(1)}, u32[]{:S(2)}, u32[]{:S(2)}) collective-permute-start(bf16[2,256,1024]{2,1,0:T(8,128)(2,1)} %copy-done.20), channel_id=1, source_target_pairs={{0,1},{1,0},{2,3},{3,2},{4,5},{5,4},{6,7},{7,6},{8,9},{9,8},{10,11... | collective-permute-start | bytes 3145736 | tf_op jit(solution)/shard_map/ppermute | solution.py:825
  204.9 14.8 %collective-permute-start.28 = (bf16[256,1024]{1,0:T(8,128)(2,1)S(1)}, bf16[256,1024]{1,0:T(8,128)(2,1)S(1)}, u32[]{:S(2)}, u32[]{:S(2)}) collective-permute-start(bf16[256,1024]{1,0:T(8,128)(2,1)S(1)} %fusion.3), channel_id=1, source_target_pairs={{0,2},{2,0},{1,3},{3,1},{4,6},{6,4},{5,7},{7,5},{8,10},{10,8},{9,1... | collective-permute-start | bytes 1572872 | tf_op jit(solution)/shard_map/ppermute | solution.py:825
  207.7 22.5 %collective-permute-start.33 = (bf16[256,1024]{1,0:T(8,128)(2,1)S(1)}, bf16[256,1024]{1,0:T(8,128)(2,1)S(1)}, u32[]{:S(2)}, u32[]{:S(2)}) collective-permute-start(bf16[256,1024]{1,0:T(8,128)(2,1)S(1)} %fusion.4), channel_id=1, source_target_pairs={{0,2},{2,0},{1,3},{3,1},{4,6},{6,4},{5,7},{7,5},{8,10},{10,8},{9,1... | collective-permute-start | bytes 1572872 | tf_op jit(solution)/shard_map/ppermute | solution.py:825
  257.3 12.7 %collective-permute-start.34 = (bf16[32,3968]{1,0:T(8,128)(2,1)S(1)}, bf16[32,3968]{1,0:T(8,128)(2,1)S(1)}, u32[]{:S(2)}, u32[]{:S(2)}) collective-permute-start(bf16[32,3968]{1,0:T(8,128)(2,1)S(1)} %get-tuple-element.136), channel_id=1, source_target_pairs={{0,4},{4,0},{1,5},{5,1},{2,6},{6,2},{3,7},{7,3},{8,12},{12,8},{9,1... | collective-permute-start | bytes 761864 | tf_op jit(solution)/shard_map/ppermute | solution.py:825
  (35 other events, 320.3 us)
Sparse Core Ops, SparseCore 0:
  48.4 57.9 all-gather.1
  145.2 54.7 reduce-scatter.2
  203.2 52.6 reduce-scatter.4
where the time goes:
time: 290 us; the launch traced here: 284 us
  waiting for transfers between devices  121 us (42%)
  Pallas kernels  92 us (32%)
  starting transfers between devices  43.3 us (15%)
  between operations  14.3 us (5%)
  local copies, waits for them, and re-layouts  8.67 us (3%)
  other arithmetic  5.23 us (2%)
    ppermute x25, waiting for transfers between devices, swapped(): return lax.ppermute(value, axis, [(0, 1), (1, 0)])  76.2 us
    ppermute x25, starting transfers between devices, swapped(): return lax.ppermute(value, axis, [(0, 1), (1, 0)])  23 us
    pallas_call x1, Pallas kernels, backward_attention(): pl.pallas_call(backward_attention_kernel, grid_spec=pltpu.PrefetchScalarG...  21.7 us
    all_to_all x1, waiting for transfers between devices, sent_rows(): return lax.all_to_all(blocks, PLANE, 0, 0, tiled=True)  19.1 us
    ppermute x12, waiting for transfers between devices, by_distance(): kept[j] = lax.ppermute(after(own, *before) if before else own, axis, perm)  18.8 us
    pallas_call x1, Pallas kernels, forward_attention(): pl.pallas_call(functools.partial(forward_attention_kernel, width // lax.a...  18.5 us
    pallas_call x2, Pallas kernels, feed_step(): pl.pallas_call(feed_kernel, in_specs=[pl.BlockSpec(memory_space=pl.ANY)]...  18.3 us
    ppermute x12, starting transfers between devices, by_distance(): kept[j] = lax.ppermute(after(own, *before) if before else own, axis, perm)  11.8 us
  transfers between devices with their start and end apart: 42, of which 25 were waited for; matrix products, arithmetic and copies ran while one was open for 2% of the time, Pallas kernels for 31%

commit v1 on v0

--- a/solution.py
+++ b/solution.py
@@ -265,10 +265,10 @@
             ],
         ),
         out_shape=[(pltpu.HBM if k < 6 or k == 10 else jax.ShapeDtypeStruct)(o[0], o[1]) for k, o in enumerate(out)],
-        compiler_params=params(40),
+        compiler_params=params(24),
         cost_estimate=cost(7e9, 16e6, 3e6),
         name="forward_attention",
-    )(place, order, far(tokens[0]), *tokens[1:], *pieces, far(cos), far(sin))
+    )(place, order, far(tokens[0]), *tokens[1:], *map(far, pieces), far(cos), far(sin))
 
 
 def middle_kernel(tokens, mine, from_core, from_z, gain, middle, second):
@@ -349,7 +349,7 @@
             pltpu.SemaphoreType.DMA((2, 2)),
             pltpu.SemaphoreType.DMA((3, units // CHUNK)),
         ],
-        compiler_params=params(32),
+        compiler_params=params(20),
         cost_estimate=cost(4e9, 8e6, 1e6),
         name="feed_step",
     )(*second, *map(far, grads), far(weights))
@@ -374,7 +374,7 @@
         grid=(2,),
         in_specs=[whole((pair, units)), whole((pair, units)), whole((width, units), (0, 2))],
         out_specs=[block, block],
-        out_shape=[jax.ShapeDtypeStruct((2, ROWS, width), bf16)] * 2,
+        out_shape=[pltpu.HBM((2, ROWS, width), bf16)] * 2,
         compiler_params=params(20),
         cost_estimate=cost(1.6e9, 5e6),
         name="feed_out",
@@ -411,7 +411,7 @@
         out_specs=pl.BlockSpec((512, wide + units), lambda i: (i, 0)),
         out_shape=pltpu.HBM((width, wide + units), bf16),
         scratch_shapes=[pltpu.VMEM((2 * pair, 512), bf16)] * 2,
-        compiler_params=params(36),
+        compiler_params=params(24),
         cost_estimate=cost(4.8e9, 14e6),
         name="feed_weights",
     )(*map(far, second), *map(far, grads), *map(far, grad_units), *map(far, hidden))
@@ -451,12 +451,13 @@
     )(far(middle), part, from_core, from_z, far(cotangent), gain)
 
 
-def backward_attention_kernel(place, *refs):
+def backward_attention_kernel(per_device, place, *refs):
     branch = refs[:4]
     tokens = refs[4:8]
-    weights, low, att, totals, qraw, kraw, cos, sin, head_gains = refs[8:17]
-    grads, mine, other, branch_out, gain_part, head_part = refs[17:23]
-    matrices, rows_all, xs_all, grad_att, dk, dv, dq, row_sems, matrix_sems = refs[23:]
+    weights, first, att_out, low, totals, qraw, kraw, cos, sin, head_gains, second_gain = refs[8:19]
+    mine, other, out = refs[19:22]
+    matrices, rows_all, xs_all, first_all, att, grads_all, block = refs[22:29]
+    grad_att, dk, dv, dq, gain_part, head_part, row_sems, matrix_sems, out_sems = refs[29:]
     qgain, kgain = head_gains[:1, :], head_gains[1:2, :]
     step_id = pl.program_id(0)
     i = pl.num_programs(0) - 1 - step_id
@@ -472,6 +473,8 @@
     wo = matrices.at[:, nqkv:]
     load_o = pltpu.make_async_copy(weights.at[:, nqkv : nqkv + nq], wo, matrix_sems.at[0])
     load_qkv = pltpu.make_async_copy(weights.at[:, :nqkv], wqkv, matrix_sems.at[1])
+    load_att = pltpu.make_async_copy(att_out, att, matrix_sems.at[2])
+    load_first = pltpu.make_async_copy(first, first_all, matrix_sems.at[3])
     loads = []
     for pieces, target, sem in ((branch, rows_all, row_sems.at[0]), (tokens, xs_all, row_sems.at[1])):
         for k, piece in enumerate(pieces):
@@ -480,13 +483,12 @@
 
     @pl.when(step_id == 0)
     def _():
-        for copy in [load_o, *loads[:4], load_qkv, *loads[4:]]:
+        for copy in [load_o, *loads[:4], load_att, load_qkv, *loads[4:], load_first]:
             copy.start()
-        for copy in [load_o, *loads[:4]]:
+        for copy in [load_o, *loads[:4], load_att]:
             copy.wait()
 
     here = pl.ds(pl.multiple_of(i * 2 * ROWS, 2 * ROWS), 2 * ROWS)
-    branch_out[...] = rows_all[here, :]
     grad_att[...] = matmul(rows_all[here, :], wo[...]).astype(bf16)
     mask_k = lax.broadcasted_iota(jnp.int32, (ROWS, GROUP * ROWS), 0)
     mask_q = lax.broadcasted_iota(jnp.int32, (ROWS, GROUP * ROWS), 1) % ROWS
@@ -499,7 +501,7 @@
             cols = [(h * GROUP + a) * HD for a in range(GROUP)]
             q2 = jnp.concatenate([low[n:end, col : col + HD] for col in cols], axis=0)
             g2 = jnp.concatenate([grad_att[half : half + ROWS, col : col + HD] for col in cols], axis=0)
-            o2 = jnp.concatenate([att[half : half + ROWS, col : col + HD] for col in cols], axis=0)
+            o2 = jnp.concatenate([att[n:end, col : col + HD] for col in cols], axis=0)
             total = totals[block % 2, h : h + 1, :]
             dot = jnp.sum((g2.astype(f32) * o2.astype(f32)).T, axis=0, keepdims=True)
             k = low[:end, nq + h * HD : nq + (h + 1) * HD]
@@ -516,7 +518,7 @@
             else:
                 dv[h, :end, :] += dv_part
                 dk[h, :end, :] += dk_part
-            d = t_matmul(grad_scores, k) * score_scale
+            d = t_matmul(k, grad_scores).T * score_scale
             for a, col in enumerate(cols):
                 dq[half : half + ROWS, col : col + HD] = d[a * ROWS : (a + 1) * ROWS]
 
@@ -536,115 +538,111 @@
     for h in range(nq // HD):
         col = slice(h * HD, (h + 1) * HD)
         grad, gp = norm_back(qraw[:, col], qgain, unturned(dq[:, col]))
-        grads[:, col] = grad.astype(bf16)
+        grads_all[here, col] = grad.astype(bf16)
         head_part[:1, :] += gp
     for h in range(nk // HD):
         col = slice(h * HD, (h + 1) * HD)
         grad, gp = norm_back(kraw[:, col], kgain, unturned(dk[h, here, :] * score_scale))
-        grads[:, nq + h * HD : nq + (h + 1) * HD] = grad.astype(bf16)
+        grads_all[here, nq + h * HD : nq + (h + 1) * HD] = grad.astype(bf16)
         head_part[1:2, :] += gp
-        grads[:, nq + nk + h * HD : nq + nk + (h + 1) * HD] = dv[h, here, :].astype(bf16)
+        grads_all[here, nq + nk + h * HD : nq + nk + (h + 1) * HD] = dv[h, here, :].astype(bf16)
     @pl.when(step_id == 0)
     def _():
         for copy in [load_qkv, *loads[4:]]:
             copy.wait()
 
-    upstream = matmul_t(grads[...], wqkv[...])
+    upstream = matmul_t(grads_all[here, :], wqkv[...])
     put_pair(place[2 * i], upstream.astype(bf16), mine, other)
     x = xs_all[here, :].astype(f32)
     gain_part[:1, :] += jnp.sum(upstream * x * inverse_rms(x), axis=0, keepdims=True)
 
-
-def backward_attention(place, branch, tokens, weights, low, att, totals, qraw, kraw, cos, sin, head_gains):
+    @pl.when(step_id == pl.num_programs(0) - 1)
+    def _():
+        load_first.wait()
+        more = nqkv + nq
+        rows = 2 * ROWS
+        stored = []
+        for k in range(first_all.shape[1] // rows):
+            at = slice(k * rows, (k + 1) * rows)
+            block[at, :nqkv] = t_matmul(first_all[:, at], grads_all[...]).astype(bf16)
+            block[at, nqkv:more] = t_matmul(rows_all[:, at], att[...]).astype(bf16)
+            same = equal_iota(rows, rows, lambda r, c: r == c)
+            stands = of_head(rows, per_device, k * rows)
+            lane = lax.broadcasted_iota(jnp.int32, (rows, HD), 1)
+            columns = jnp.zeros((rows, HD), f32)
+            values = [
+                (same, gain_part[:1, at]),
+                (same, second_gain[:1, at]),
+                (stands, head_part[:1, :]),
+                (stands, head_part[1:2, :]),
+            ]
+            for m, (mask, line) in enumerate(values):
+                column = jnp.sum(jnp.where(mask, line, 0.0), axis=1, keepdims=True)
+                columns = jnp.where(lane == m, column, columns)
+            block[at, more:] = columns.astype(bf16)
+            stored.append(pltpu.make_async_copy(block.at[at, :], out.at[at, :], out_sems.at[k]))
+            stored[-1].start()
+        for copy in stored:
+            copy.wait()
+
+
+def backward_attention(
+    place, branch, tokens, weights, first, low, att, totals, qraw, kraw, cos, sin, head_gains, second_gain
+):
     n, width = 4, branch[0].shape[1]
     length, nqkv = low.shape
     nq, nk = qraw.shape[1], kraw.shape[1]
+    total = nqkv + nq + HD
     row = lambda cols: pl.BlockSpec((2 * ROWS, cols), lambda i, p: (n // 2 - 1 - i, 0))
-    out = [
-        ((length, nqkv), bf16, row(nqkv)),
-        *[((2, ROWS, width), bf16, pl.BlockSpec((1, ROWS, width), lambda i, p: (p[n - 2 - 2 * i] % 2, 0, 0)))] * 2,
-        ((length, width), bf16, row(width)),
-        ((8, width), f32, whole_out((8, width))),
-        ((8, HD), f32, whole_out((8, HD))),
-    ]
-    return pl.pallas_call(
-        backward_attention_kernel,
+    half = pl.BlockSpec((1, ROWS, width), lambda i, p: (p[n - 2 - 2 * i] % 2, 0, 0))
+    return pl.pallas_call(
+        functools.partial(backward_attention_kernel, width // lax.axis_size(FSDP)),
         grid_spec=pltpu.PrefetchScalarGridSpec(
             num_scalar_prefetch=1,
             grid=(n // 2,),
             in_specs=[
-                *[pl.BlockSpec(memory_space=pl.ANY)] * 9,
+                *[pl.BlockSpec(memory_space=pl.ANY)] * 11,
                 whole((length, nqkv)),
-                row(nq),
                 pl.BlockSpec((2, 8, GROUP * ROWS), lambda i, p: (n // 2 - 1 - i, 0, 0)),
                 row(nq),
                 row(nk),
                 row(HD),
                 row(HD),
                 whole((8, HD)),
+                whole((8, width)),
             ],
-            out_specs=[o[2] for o in out],
+            out_specs=[half, half, pl.BlockSpec(memory_space=pltpu.HBM)],
             scratch_shapes=[
                 pltpu.VMEM((width, nqkv + nq), bf16),
                 pltpu.VMEM((length, width), bf16),
                 pltpu.VMEM((length, width), bf16),
+                pltpu.VMEM((length, width), bf16),
+                pltpu.VMEM((length, nq), bf16),
+                pltpu.VMEM((length, nqkv), bf16),
+                pltpu.VMEM((width, total), bf16),
                 pltpu.VMEM((2 * ROWS, nq), bf16),
                 pltpu.VMEM((nk // HD, length, HD), f32),
                 pltpu.VMEM((nk // HD, length, HD), f32),
                 pltpu.VMEM((2 * ROWS, nq), f32),
+                pltpu.VMEM((8, width), f32),
+                pltpu.VMEM((8, HD), f32),
                 pltpu.SemaphoreType.DMA((2, 4)),
-                pltpu.SemaphoreType.DMA((2,)),
+                pltpu.SemaphoreType.DMA((4,)),
+                pltpu.SemaphoreType.DMA((width // (2 * ROWS),)),
             ],
         ),
-        out_shape=[(pltpu.HBM if k in (0, 1, 3) else jax.ShapeDtypeStruct)(o[0], o[1]) for k, o in enumerate(out)],
-        compiler_params=params(48),
-        cost_estimate=cost(9e9, 18e6, 3e6),
+        out_shape=[
+            pltpu.HBM((2, ROWS, width), bf16),
+            pltpu.HBM((2, ROWS, width), bf16),
+            pltpu.HBM((width, total), bf16),
+        ],
+        compiler_params=params(46),
+        cost_estimate=cost(6e11, 18e6, 3e6),
         name="backward_attention",
     )(
-        place, *branch, *map(far, tokens), far(weights), far(low), far(att), far(totals),
-        far(qraw), far(kraw), far(cos), far(sin), far(head_gains),
+        place, *branch, *map(far, tokens), far(weights), far(first), far(att), far(low), far(totals),
+        far(qraw), far(kraw), far(cos), far(sin), far(head_gains), far(second_gain),
     )
-
-
-def projection_weights_kernel(per_device, first, branch, grads, att, gain, second_gain, heads, out):
-    wide = grads.shape[1]
-    more = wide + att.shape[1]
-    out[:, :wide] = t_matmul(first[...], grads[...]).astype(bf16)
-    out[:, wide:more] = t_matmul(branch[...], att[...]).astype(bf16)
-    rows = out.shape[0]
-    same = equal_iota(rows, rows, lambda r, c: r == c)
-    stands = of_head(rows, per_device, pl.program_id(0) * rows)
-    lane = lax.broadcasted_iota(jnp.int32, (rows, HD), 1)
-    columns = jnp.zeros((rows, HD), f32)
-    for k, (mask, values) in enumerate(
-        [(same, gain[:1, :]), (same, second_gain[:1, :]), (stands, heads[:1, :]), (stands, heads[1:2, :])]
-    ):
-        column = jnp.sum(jnp.where(mask, values, 0.0), axis=1, keepdims=True)
-        columns = jnp.where(lane == k, column, columns)
-    out[:, more:] = columns.astype(bf16)
-
-
-def projection_weights(first, branch, grads, att, gain, second_gain, heads):
-    length, width = first.shape
-    wide, nq = grads.shape[1], att.shape[1]
-    return pl.pallas_call(
-        functools.partial(projection_weights_kernel, width // lax.axis_size(FSDP)),
-        grid=(width // 512,),
-        in_specs=[
-            pl.BlockSpec((length, 512), lambda i: (0, i)),
-            pl.BlockSpec((length, 512), lambda i: (0, i)),
-            whole((length, wide)),
-            whole((length, nq)),
-            pl.BlockSpec((8, 512), lambda i: (0, i)),
-            pl.BlockSpec((8, 512), lambda i: (0, i)),
-            whole((8, HD)),
-        ],
-        out_specs=pl.BlockSpec((512, wide + nq + HD), lambda i: (i, 0)),
-        out_shape=pltpu.HBM((width, wide + nq + HD), bf16),
-        compiler_params=params(30),
-        cost_estimate=cost(3.2e9, 10e6),
-        name="projection_weights",
-    )(far(first), far(branch), far(grads), far(att), gain, far(second_gain), heads)
 
 
 def tokens_back_kernel(tokens, mine, from_core, from_z, grad_middle, gain, grad_tokens):
@@ -670,36 +668,34 @@
     )(far(tokens), mine, from_core, from_z, far(grad_middle), far(gain))
 
 
-def close(zh, parts, summed):
-    planes, both, wide = parts.shape
+def close(zh, parts):
+    senders, both, wide = parts.shape
     rows = both // 2
-    total = wide + summed.shape[1]
-
-    def kernel(zh, parts, summed, keep, give):
+
+    def kernel(zh, parts, keep, give):
         for which, out in ((zh[0], keep), (1 - zh[0], give)):
             at = pl.ds(pl.multiple_of(which * rows, rows), rows)
             added = parts[0, at, :].astype(f32)
-            for k in range(1, planes):
+            for k in range(1, senders):
                 added = added + parts[k, at, :].astype(f32)
-            out[:, :wide] = added.astype(out.dtype)
-            out[:, wide:] = summed[at, :].astype(out.dtype)
+            out[...] = added.astype(out.dtype)
 
     return pl.pallas_call(
         kernel,
         grid_spec=pltpu.PrefetchScalarGridSpec(
             num_scalar_prefetch=1,
             grid=(1,),
-            in_specs=[whole(parts.shape), whole(summed.shape)],
-            out_specs=[whole_out((rows, total))] * 2,
+            in_specs=[whole(parts.shape)],
+            out_specs=[whole_out((rows, wide))] * 2,
         ),
         out_shape=[
-            jax.ShapeDtypeStruct((rows, total), f32),
-            jax.ShapeDtypeStruct((rows, total), bf16),
+            jax.ShapeDtypeStruct((rows, wide), f32),
+            jax.ShapeDtypeStruct((rows, wide), bf16),
         ],
         compiler_params=params(14),
         cost_estimate=cost(2e6, 4e6),
         name="close",
-    )(zh, parts, summed)
+    )(zh, far(parts) if senders == 1 else parts)
 
 
 def finish(keep, arrived, widths):
@@ -946,7 +942,7 @@
     from_z = swapped(passed, "zl")
     grad_units[0] = after(grad_units[0], passed)
     feed_grads = feed_weights(second_blocks, grad_blocks, grad_units, hidden)
-    from_z, feed_grads = lax.optimization_barrier((from_z, feed_grads))
+    from_z = after(from_z, feed_grads)
     grad_middle, branch, feed_gain_part = middle_back(middle, near[2], from_core, from_z, dy, gains)
     feed_sums = lax.psum_scatter(feed_grads, "x", scatter_dimension=0, tiled=True)
     feed_sums = lax.psum_scatter(feed_sums, "y", scatter_dimension=0, tiled=True)
@@ -957,20 +953,21 @@
     output = middle + mine[0].astype(f32) + from_core[0].astype(f32) + from_z.astype(f32)
     output = output.astype(bf16)
 
-    grads, mine, other, branch_rows, gain_part, head_part = backward_attention(
-        place, branch_blocks, token_blocks, weights, low, att, totals, qraw, kraw, cos, sin, head_gains
-    )
-    projection_grads = projection_weights(
-        first, branch_rows, grads, att, gain_part, feed_gain_part, head_part
+    mine, other, projection_grads = backward_attention(
+        place, branch_blocks, token_blocks, weights, first, low, att, totals, qraw, kraw, cos, sin,
+        head_gains, feed_gain_part,
     )
     mine, from_core, from_z, _ = tp_scatter(mine, other)
     tokens_grad = tokens_back(
         x, mine, from_core, after(from_z, projection_grads), grad_middle, gains
     )
     parts = after(sent_rows(projection_grads), tokens_grad, output)
-    keep, give = close(lax.axis_index("zh").reshape(1), parts, after(feed_sums, tokens_grad, output))
-    widths = (nq, nk, nk, nq, HD, units, units, units)
-    query, key, value, out, columns, gate, up, down = finish(keep, swapped(give, "zh"), widths)
+    zh = lax.axis_index("zh").reshape(1)
+    keep, give = close(zh, parts)
+    arrived = swapped(give, "zh")
+    query, key, value, out, columns = finish(keep, arrived, (nq, nk, nk, nq, HD))
+    feed_keep, feed_give = close(zh, after(feed_sums, arrived)[None])
+    gate, up, down = finish(feed_keep, swapped(feed_give, "zh"), (units, units, units))
     both = ("zl", "core")
     across = lax.ppermute(columns, both, [(s, 3 - s) for s in range(4)])
     parts = (columns, swapped(columns, "zl"), swapped(columns, "core"), across)

time: 290 us -> 277 us (0.955)
  waiting for transfers between devices: 121 us -> 114 us
  local copies, waits for them, and re-layouts: 8.67 us -> 4.46 us
    unnamed x50 -> x48, local copies, waits for them, and re-layouts: 8.48 us -> 4.27 us
    reduce_scatter x1, waiting for transfers between devices: 4.03 us -> 0.01 us  [local(): lax.psum_scatter(feed_sums, 'y', scatter_dimension=0, tiled=True)]
    pallas_call x2 -> x1, Pallas kernels: 30.1 us -> 26.5 us  [backward_attention(): pl.pallas_call(functools.partial(backward_attention_kernel, width // lax....]
    ppermute x25 -> x26, waiting for transfers between devices: 76.2 us -> 73 us  [swapped(): return lax.ppermute(value, axis, [(0, 1), (1, 0)])]
    ppermute x25 -> x26, starting transfers between devices: 23 us -> 24.5 us  [swapped(): return lax.ppermute(value, axis, [(0, 1), (1, 0)])]
  transfers between devices with their start and end apart: 42 -> 43, of which waited for: 25 -> 24; matrix products, arithmetic and copies ran while one was open for 2% -> 2% of each run, Pallas kernels for 31% -> 32%
where the time goes in v1:
time: 277 us; the launch traced here: 272 us
  waiting for transfers between devices  114 us (41%)
  Pallas kernels  90.7 us (33%)
  starting transfers between devices  43.4 us (16%)
  between operations  14.4 us (5%)
  other arithmetic  5.27 us (2%)
  local copies, waits for them, and re-layouts  4.46 us (2%)
    ppermute x26, waiting for transfers between devices, swapped(): return lax.ppermute(value, axis, [(0, 1), (1, 0)])  73 us
    pallas_call x1, Pallas kernels, backward_attention(): pl.pallas_call(functools.partial(backward_attention_kernel, width // lax....  26.5 us
    ppermute x26, starting transfers between devices, swapped(): return lax.ppermute(value, axis, [(0, 1), (1, 0)])  24.5 us
    ppermute x12, waiting for transfers between devices, by_distance(): kept[j] = lax.ppermute(after(own, *before) if before else own, axis, perm)  19.7 us
    all_to_all x1, waiting for transfers between devices, sent_rows(): return lax.all_to_all(blocks, PLANE, 0, 0, tiled=True)  19 us
    pallas_call x2, Pallas kernels, feed_step(): pl.pallas_call(feed_kernel, in_specs=[pl.BlockSpec(memory_space=pl.ANY)]...  18.4 us
    pallas_call x1, Pallas kernels, forward_attention(): pl.pallas_call(functools.partial(forward_attention_kernel, width // lax.a...  18.1 us
    ppermute x12, starting transfers between devices, by_distance(): kept[j] = lax.ppermute(after(own, *before) if before else own, axis, perm)  11.8 us
  transfers between devices with their start and end apart: 43, of which 24 were waited for; matrix products, arithmetic and copies ran while one was open for 2% of the time, Pallas kernels for 32%

profile of v1, /device:TPU:28, one launch (start us, length us, event | category | flops | bytes accessed | tf_op | source)
XLA Modules:
  0.0 271.9 jit_solution(14510210859759132614)
XLA Ops:
  9.1 4.0 %collective-permute-start = (bf16[32,3968]{1,0:T(8,128)(2,1)S(1)}, bf16[32,3968]{1,0:T(8,128)(2,1)S(1)}, u32[]{:S(2)}, u32[]{:S(2)}) collective-permute-start(bf16[32,3968]{1,0:T(8,128)(2,1)S(1)} %pack.1.shard), channel_id=1, source_target_pairs={{0,4},{4,0},{1,5},{5,1},{2,6},{6,2},{3,7},{7,3},{8,12},{12,8},{9,1... | collective-permute-start | bytes 761864 | tf_op jit(solution)/shard_map/ppermute | solution.py:821
  13.0 6.1 %collective-permute-done.other = bf16[32,3968]{1,0:T(8,128)(2,1)S(1)} collective-permute-done((bf16[32,3968]{1,0:T(8,128)(2,1)S(1)}, bf16[32,3968]{1,0:T(8,128)(2,1)S(1)}, u32[]{:S(2)}, u32[]{:S(2)}) %collective-permute-start) | collective-permute-done | bytes 253984 | tf_op jit(solution)/shard_map/ppermute | solution.py:821
  24.0 2.6 collective-permute-done.5
  29.8 4.3 %collective-permute-done.11 = bf16[2,32,896]{2,1,0:T(8,128)(2,1)S(1)} collective-permute-done((bf16[2,32,896]{2,1,0:T(8,128)(2,1)S(1)}, bf16[2,32,896]{2,1,0:T(8,128)(2,1)S(1)}, u32[]{:S(2)}, u32[]{:S(2)}) %collective-permute-start.11) | collective-permute-done | bytes 114720 | tf_op jit(solution)/shard_map/ppermute | solution.py:855
  36.3 2.2 collective-permute-start.10
  38.5 5.6 %collective-permute-done.10.refs_7_ = bf16[4,2,32,768]{3,2,1,0:T(8,128)(2,1)S(1)} collective-permute-done((bf16[4,2,32,768]{3,2,1,0:T(8,128)(2,1)S(1)}, bf16[4,2,32,768]{3,2,1,0:T(8,128)(2,1)S(1)}, u32[]{:S(2)}, u32[]{:S(2)}) %collective-permute-start.10) | collective-permute-done | bytes 393248 | tf_op jit(solution)/shard_map/ppermute | solution.py:855
  44.2 3.3 %collective-permute-done.9.refs_5_ = bf16[4,2,32,768]{3,2,1,0:T(8,128)(2,1)S(1)} collective-permute-done((bf16[4,2,32,768]{3,2,1,0:T(8,128)(2,1)S(1)}, bf16[4,2,32,768]{3,2,1,0:T(8,128)(2,1)S(1)}, u32[]{:S(2)}, u32[]{:S(2)}) %collective-permute-start.9) | collective-permute-done | bytes 393248 | tf_op jit(solution)/shard_map/ppermute | solution.py:855
  52.2 6.3 %collective-permute-done.1.refs_1_.refs_5_ = bf16[256,1024]{1,0:T(8,128)(2,1)S(1)} collective-permute-done((bf16[256,1024]{1,0:T(8,128)(2,1)S(1)}, bf16[256,1024]{1,0:T(8,128)(2,1)S(1)}, u32[]{:S(2)}, u32[]{:S(2)}) %collective-permute-start.1) | collective-permute-done | bytes 524320 | tf_op jit(solution)/shard_map/ppermute | solution.py:821
  58.6 2.7 collective-permute-done.14.refs_6_
  63.5 18.1 %forward_attention.1 = (bf16[1024,1024]{1,0:T(8,128)(2,1)}, f32[1024,512]{1,0:T(8,128)}, f32[1024,256]{1,0:T(8,128)}, bf16[1024,1024]{1,0:T(8,128)(2,1)}, bf16[1...) custom-call(s32[8]{0:T(128)S(1)} %pad_add_fusion.1.place, ...), custom_call_target="tpu_custom_call" | custom-call | flops 875000000 | bytes 2000000 | tf_op jit(solution)/shard_map/forward_attention/pallas_call | solution.py:246
  81.8 2.6 collective-permute-done.17.from_core
  86.1 12.7 %collective-permute-done.18.from_z = bf16[256,1024]{1,0:T(8,128)(2,1)S(1)} collective-permute-done((bf16[256,1024]{1,0:T(8,128)(2,1)S(1)}, bf16[256,1024]{1,0:T(8,128)(2,1)S(1)}, u32[]{:S(2)}, u32[]{:S(2)}) %collective-permute-start.18) | collective-permute-done | bytes 524320 | tf_op jit(solution)/shard_map/ppermute | solution.py:821
  98.7 2.2 middle_step.1
  103.2 9.1 %feed_step.2 = (bf16[512,768]{1,0:T(8,128)(2,1)}, bf16[512,1536]{1,0:T(8,128)(2,1)}, bf16[256,1024]{1,0:T(8,128)(2,1)S(1)}, bf16[256,1024]{1,0:T(8,128)(2,1)S(1)}) custom-call(bf16[256,1024]{1,0:T(8,128)(2,1)S(1)} %get-tuple-element.92.refs_0_, bf16[256,1024]{1,0:T(8,128)(2,1)S(1)} %collective-permute-done.19.refs_1_.refs_2_, ...), custom_call_target="tpu_custom_call" | custom-call | flops 500000000 | bytes 1000000 | tf_op jit(solution)/shard_map/feed_step/pallas_call | solution.py:338
  112.3 3.0 %collective-permute-done.22.refs_0_.refs_1_ = bf16[256,1024]{1,0:T(8,128)(2,1)S(1)} collective-permute-done((bf16[256,1024]{1,0:T(8,128)(2,1)S(1)}, bf16[256,1024]{1,0:T(8,128)(2,1)S(1)}, u32[]{:S(2)}, u32[]{:S(2)}) %collective-permute-start.22) | collective-permute-done | bytes 524320 | tf_op jit(solution)/shard_map/ppermute | solution.py:821
  117.2 9.3 %feed_step.3 = (bf16[512,768]{1,0:T(8,128)(2,1)}, bf16[512,1536]{1,0:T(8,128)(2,1)}, bf16[256,1024]{1,0:T(8,128)(2,1)S(1)}, bf16[256,1024]{1,0:T(8,128)(2,1)S(1)}) custom-call(bf16[256,1024]{1,0:T(8,128)(2,1)S(1)} %collective-permute-done.22.refs_0_.refs_1_, bf16[256,1024]{1,0:T(8,128)(2,1)S(1)} %collective-permute-done.23.refs_1_.refs_3_, ...), custom_call_target="tpu_custom_call" | custom-call | flops 500000000 | bytes 1000000 | tf_op jit(solution)/shard_map/feed_step/pallas_call | solution.py:338
  130.1 10.0 %feed_weights.1 = bf16[1024,2304]{1,0:T(8,128)(2,1)} custom-call(bf16[256,1024]{1,0:T(8,128)(2,1)} %copy-done.1, bf16[256,1024]{1,0:T(8,128)(2,1)} %copy-done.3, bf16[256,1024]{1,0:T(8,128)(2,1)} %copy-done.2, bf16[256,1024]{1,0:T(8,128)(2,1)} %copy-done.4, bf16[256,1024]{1,0:T(8,128)(2,1)} %bitcast.11.refs_2_.refs_4_.cotangent, ...), custom_call_target="tpu_custom_call" | custom-call | flops 600000000 | bytes 1750000 | tf_op jit(solution)/shard_map/feed_weights/pallas_call | solution.py:403
  140.1 2.6 collective-permute-done.26.from_z
  142.8 2.7 %middle_back.1 = (f32[256,1024]{1,0:T(8,128)}, bf16[256,1024]{1,0:T(8,128)(2,1)S(1)}, f32[8,1024]{1,0:T(8,128)}) custom-call(f32[256,1024]{1,0:T(8,128)} %get-tuple-element.91.middle, bf16[256,1024]{1,0:T(8,128)(2,1)S(1)} %get-tuple-element.96.mine, bf16[256,1024]{1,0:T(8,128)(2,1)S(1)} %collective-permute-done.21.from_core, ...), custom_call_target="tpu_custom_call" | custom-call | flops 500000 | bytes 625000 | tf_op jit(solution)/shard_map/middle_back/pallas_call | solution.py:438
  146.8 4.9 %feed_out.1 = (bf16[2,256,1024]{2,1,0:T(8,128)(2,1)}, bf16[2,256,1024]{2,1,0:T(8,128)(2,1)}) custom-call(bf16[512,768]{1,0:T(8,128)(2,1)} %get-tuple-element.109.refs_10_.first, bf16[512,768]{1,0:T(8,128)(2,1)} %get-tuple-element.106.refs_11_.then, bf16[1024,2304]{1,0:T(8,128)(2,1)} %all-gather.2.cloned.1.call-done.refs_4_.wd), custom_call_target="tpu_custom_call" | custom-call | flops 200000000 | bytes 625000 | tf_op jit(solution)/shard_map/feed_out/pallas_call | solution.py:372
  151.7 6.9 %collective-permute-done.29.refs_1_ = bf16[256,1024]{1,0:T(8,128)(2,1)S(1)} collective-permute-done((bf16[256,1024]{1,0:T(8,128)(2,1)S(1)}, bf16[256,1024]{1,0:T(8,128)(2,1)S(1)}, u32[]{:S(2)}, u32[]{:S(2)}) %collective-permute-start.29) | collective-permute-done | bytes 524320 | tf_op jit(solution)/shard_map/ppermute | solution.py:821
  158.6 1.9 collective-permute-done.31.refs_3_
  160.5 26.5 %backward_attention.1 = (bf16[2,256,1024]{2,1,0:T(8,128)(2,1)}, bf16[2,256,1024]{2,1,0:T(8,128)(2,1)}, bf16[1024,1664]{1,0:T(8,128)(2,1)}) custom-call(s32[8]{0:T(128)S(1)} %pad_add_fusion.1.place, bf16[256,1024]{1,0:T(8,128)(2,1)S(1)} %get-tuple-element.108.refs_0_, bf16[256,1024]{1,0:T(8,128)(2,1)S(1)} %collective-permute-done.29.refs_1_, ...), custom_call_target="tpu_custom_call" | custom-call | flops 74999996416 | bytes 2250000 | tf_op jit(solution)/shard_map/backward_attention/pallas_call | solution.py:598
  187.0 6.9 %all-to-all-start = ((bf16[16,64,1664]{2,1,0:T(8,128)(2,1)}), bf16[16,64,1664]{2,1,0:T(8,128)(2,1)S(1)}, u32[]{:S(2)}, u32[]{:S(2)}) async-start(bf16[16,64,1664]{2,1,0:T(8,128)(2,1)} %bitcast.43), calls=%async_computation | async-start | bytes 6815744 | tf_op jit(solution)/shard_map/all_to_all | solution.py:842
  195.3 2.4 collective-permute-done.27
  202.4 11.3 %collective-permute-done.28 = bf16[256,1024]{1,0:T(8,128)(2,1)S(1)} collective-permute-done((bf16[256,1024]{1,0:T(8,128)(2,1)S(1)}, bf16[256,1024]{1,0:T(8,128)(2,1)S(1)}, u32[]{:S(2)}, u32[]{:S(2)}) %collective-permute-start.28) | collective-permute-done | bytes 524320 | tf_op jit(solution)/shard_map/ppermute | solution.py:821
  214.9 9.3 %collective-permute-done.33.from_z = bf16[256,1024]{1,0:T(8,128)(2,1)S(1)} collective-permute-done((bf16[256,1024]{1,0:T(8,128)(2,1)S(1)}, bf16[256,1024]{1,0:T(8,128)(2,1)S(1)}, u32[]{:S(2)}, u32[]{:S(2)}) %collective-permute-start.33) | collective-permute-done | bytes 524320 | tf_op jit(solution)/shard_map/ppermute | solution.py:821
  224.2 2.6 tokens_back.1
  226.8 19.0 %all-to-all-done.parts = bf16[16,64,1664]{2,1,0:T(8,128)(2,1)S(1)} async-done(((bf16[16,64,1664]{2,1,0:T(8,128)(2,1)}), bf16[16,64,1664]{2,1,0:T(8,128)(2,1)S(1)}, u32[]{:S(2)}, u32[]{:S(2)}) %all-to-all-start) | async-done | bytes 3407904 | tf_op jit(solution)/shard_map/all_to_all | solution.py:842
  246.9 3.2 %collective-permute-start.34 = (bf16[32,1664]{1,0:T(8,128)(2,1)S(1)}, bf16[32,1664]{1,0:T(8,128)(2,1)S(1)}, u32[]{:S(2)}, u32[]{:S(2)}) collective-permute-start(bf16[32,1664]{1,0:T(8,128)(2,1)S(1)} %get-tuple-element.129), channel_id=1, source_target_pairs={{0,4},{4,0},{1,5},{5,1},{2,6},{6,2},{3,7},{7,3},{8,12},{12,8},{9,1... | collective-permute-start | bytes 319496 | tf_op jit(solution)/shard_map/ppermute | solution.py:821
  250.1 3.0 %collective-permute-done.34.arrived = bf16[32,1664]{1,0:T(8,128)(2,1)S(1)} collective-permute-done((bf16[32,1664]{1,0:T(8,128)(2,1)S(1)}, bf16[32,1664]{1,0:T(8,128)(2,1)S(1)}, u32[]{:S(2)}, u32[]{:S(2)}) %collective-permute-start.34) | collective-permute-done | bytes 106528 | tf_op jit(solution)/shard_map/ppermute | solution.py:821
  254.1 3.3 %collective-permute-start.38 = (bf16[32,2304]{1,0:T(8,128)(2,1)S(1)}, bf16[32,2304]{1,0:T(8,128)(2,1)S(1)}, u32[]{:S(2)}, u32[]{:S(2)}) collective-permute-start(bf16[32,2304]{1,0:T(8,128)(2,1)S(1)} %get-tuple-element.141), channel_id=1, source_target_pairs={{0,4},{4,0},{1,5},{5,1},{2,6},{6,2},{3,7},{7,3},{8,12},{12,8},{9,1... | collective-permute-start | bytes 442376 | tf_op jit(solution)/shard_map/ppermute | solution.py:821
  (138 shorter events, 46.8 us)
Async XLA Ops:
  7.2 96.0 %all-gather.2.cloned.1.call-start = ((), (), s32[]{:S(2)}) async-start(), calls=%async_computation.3 | async-start | bytes 5013504 | tf_op jit(solution)/shard_map/all_gather | solution.py:925
  9.1 10.1 %collective-permute-start = (bf16[32,3968]{1,0:T(8,128)(2,1)S(1)}, bf16[32,3968]{1,0:T(8,128)(2,1)S(1)}, u32[]{:S(2)}, u32[]{:S(2)}) collective-permute-start(bf16[32,3968]{1,0:T(8,128)(2,1)S(1)} %pack.1.shard), channel_id=1, source_target_pairs={{0,4},{4,0},{1,5},{5,1},{2,6},{6,2},{3,7},{7,3},{8,12},{12,8},{9,1... | collective-permute-start | bytes 761864 | tf_op jit(solution)/shard_map/ppermute | solution.py:821
  19.9 7.8 %collective-permute-start.7 = (bf16[2,32,896]{2,1,0:T(8,128)(2,1)S(1)}, bf16[2,32,896]{2,1,0:T(8,128)(2,1)S(1)}, u32[]{:S(2)}, u32[]{:S(2)}) collective-permute-start(bf16[2,32,896]{2,1,0:T(8,128)(2,1)S(1)} %get-tuple-element.83), channel_id=1, source_target_pairs={{0,8},{8,16},{16,24},{24,0},{1,9},{9,17},{17,25},{25,1},{2,10},{10... | collective-permute-start | bytes 344072 | tf_op jit(solution)/shard_map/ppermute | solution.py:855
  20.2 7.6 %collective-permute-start.6 = (bf16[2,32,896]{2,1,0:T(8,128)(2,1)S(1)}, bf16[2,32,896]{2,1,0:T(8,128)(2,1)S(1)}, u32[]{:S(2)}, u32[]{:S(2)}) collective-permute-start(bf16[2,32,896]{2,1,0:T(8,128)(2,1)S(1)} %get-tuple-element.83), channel_id=1, source_target_pairs={{0,24},{8,0},{16,8},{24,16},{1,25},{9,1},{17,9},{25,17},{2,26},{10... | collective-permute-start | bytes 344072 | tf_op jit(solution)/shard_map/ppermute | solution.py:855
  27.8 6.3 %collective-permute-start.11 = (bf16[2,32,896]{2,1,0:T(8,128)(2,1)S(1)}, bf16[2,32,896]{2,1,0:T(8,128)(2,1)S(1)}, u32[]{:S(2)}, u32[]{:S(2)}) collective-permute-start(bf16[2,32,896]{2,1,0:T(8,128)(2,1)S(1)} %get-tuple-element.83), channel_id=1, source_target_pairs={{0,16},{8,24},{16,0},{24,8},{1,17},{9,25},{17,1},{25,9},{2,18},{10... | collective-permute-start | bytes 344072 | tf_op jit(solution)/shard_map/ppermute | solution.py:855
  29.0 7.2 %collective-permute-start.8 = (bf16[2,32,768]{2,1,0:T(8,128)(2,1)S(1)}, bf16[2,32,768]{2,1,0:T(8,128)(2,1)S(1)}, u32[]{:S(2)}, u32[]{:S(2)}) collective-permute-start(bf16[2,32,768]{2,1,0:T(8,128)(2,1)S(1)} %get-tuple-element.82), channel_id=1, source_target_pairs={{0,64},{32,96},{64,0},{96,32},{1,65},{33,97},{65,1},{97,33},{2,66}... | collective-permute-start | bytes 294920 | tf_op jit(solution)/shard_map/ppermute | solution.py:855
  34.2 13.4 %collective-permute-start.13 = (bf16[4,2,32,896]{3,2,1,0:T(8,128)(2,1)S(1)}, bf16[4,2,32,896]{3,2,1,0:T(8,128)(2,1)S(1)}, u32[]{:S(2)}, u32[]{:S(2)}) collective-permute-start(bf16[4,2,32,896]{3,2,1,0:T(8,128)(2,1)S(1)} %pad_maximum_fusion.refs_8_), channel_id=1, source_target_pairs={{0,32},{32,64},{64,96},{96,0},{1,33},{33,65},{65,97},{97,1},{2,34}... | collective-permute-start | bytes 1376264 | tf_op jit(solution)/shard_map/ppermute | solution.py:855
  35.9 11.6 %collective-permute-start.12 = (bf16[4,2,32,896]{3,2,1,0:T(8,128)(2,1)S(1)}, bf16[4,2,32,896]{3,2,1,0:T(8,128)(2,1)S(1)}, u32[]{:S(2)}, u32[]{:S(2)}) collective-permute-start(bf16[4,2,32,896]{3,2,1,0:T(8,128)(2,1)S(1)} %pad_maximum_fusion.refs_8_), channel_id=1, source_target_pairs={{0,96},{32,0},{64,32},{96,64},{1,97},{33,1},{65,33},{97,65},{2,98}... | collective-permute-start | bytes 1376264 | tf_op jit(solution)/shard_map/ppermute | solution.py:855
  36.3 7.8 %collective-permute-start.10 = (bf16[4,2,32,768]{3,2,1,0:T(8,128)(2,1)S(1)}, bf16[4,2,32,768]{3,2,1,0:T(8,128)(2,1)S(1)}, u32[]{:S(2)}, u32[]{:S(2)}) collective-permute-start(bf16[4,2,32,768]{3,2,1,0:T(8,128)(2,1)S(1)} %pad_maximum_fusion.1.refs_4_), channel_id=1, source_target_pairs={{0,8},{8,16},{16,24},{24,0},{1,9},{9,17},{17,25},{25,1},{2,10},{10... | collective-permute-start | bytes 1179656 | tf_op jit(solution)/shard_map/ppermute | solution.py:855
  38.5 9.0 %collective-permute-start.9 = (bf16[4,2,32,768]{3,2,1,0:T(8,128)(2,1)S(1)}, bf16[4,2,32,768]{3,2,1,0:T(8,128)(2,1)S(1)}, u32[]{:S(2)}, u32[]{:S(2)}) collective-permute-start(bf16[4,2,32,768]{3,2,1,0:T(8,128)(2,1)S(1)} %pad_maximum_fusion.1.refs_4_), channel_id=1, source_target_pairs={{0,24},{8,0},{16,8},{24,16},{1,25},{9,1},{17,9},{25,17},{2,26},{10... | collective-permute-start | bytes 1179656 | tf_op jit(solution)/shard_map/ppermute | solution.py:855
  49.2 144.8 %reduce-scatter.3.cloned.1.call-start = ((), (), s32[]{:S(2)}) async-start(), calls=%async_computation.4 | async-start | bytes 5898240 | tf_op jit(solution)/shard_map/reduce_scatter | solution.py:947
  49.3 9.3 %collective-permute-start.1 = (bf16[256,1024]{1,0:T(8,128)(2,1)S(1)}, bf16[256,1024]{1,0:T(8,128)(2,1)S(1)}, u32[]{:S(2)}, u32[]{:S(2)}) collective-permute-start(bf16[256,1024]{1,0:T(8,128)(2,1)S(1)} %bitcast.41), channel_id=1, source_target_pairs={{0,2},{2,0},{1,3},{3,1},{4,6},{6,4},{5,7},{7,5},{8,10},{10,8},{9,1... | collective-permute-start | bytes 1572872 | tf_op jit(solution)/shard_map/ppermute | solution.py:821
  50.7 10.6 %collective-permute-start.15 = (bf16[4,2,32,896]{3,2,1,0:T(8,128)(2,1)S(1)}, bf16[4,2,32,896]{3,2,1,0:T(8,128)(2,1)S(1)}, u32[]{:S(2)}, u32[]{:S(2)}) collective-permute-start(bf16[4,2,32,896]{3,2,1,0:T(8,128)(2,1)S(1)} %pad_maximum_fusion.refs_8_), channel_id=1, source_target_pairs={{0,64},{32,96},{64,0},{96,32},{1,65},{33,97},{65,1},{97,33},{2,66}... | collective-permute-start | bytes 1376264 | tf_op jit(solution)/shard_map/ppermute | solution.py:855
  52.0 9.3 %collective-permute-start.14 = (bf16[4,2,32,768]{3,2,1,0:T(8,128)(2,1)S(1)}, bf16[4,2,32,768]{3,2,1,0:T(8,128)(2,1)S(1)}, u32[]{:S(2)}, u32[]{:S(2)}) collective-permute-start(bf16[4,2,32,768]{3,2,1,0:T(8,128)(2,1)S(1)} %pad_maximum_fusion.1.refs_4_), channel_id=1, source_target_pairs={{0,16},{8,24},{16,0},{24,8},{1,17},{9,25},{17,1},{25,9},{2,18},{10... | collective-permute-start | bytes 1179656 | tf_op jit(solution)/shard_map/ppermute | solution.py:855
  52.2 11.2 %collective-permute-start.2 = (bf16[256,1024]{1,0:T(8,128)(2,1)S(1)}, bf16[256,1024]{1,0:T(8,128)(2,1)S(1)}, u32[]{:S(2)}, u32[]{:S(2)}) collective-permute-start(bf16[256,1024]{1,0:T(8,128)(2,1)S(1)} %bitcast.42), channel_id=1, source_target_pairs={{0,1},{1,0},{2,3},{3,2},{4,5},{5,4},{6,7},{7,6},{8,9},{9,8},{10,11... | collective-permute-start | bytes 1572872 | tf_op jit(solution)/shard_map/ppermute | solution.py:821
  58.6 4.9 %collective-permute-start.3 = (bf16[256,1024]{1,0:T(8,128)(2,1)S(1)}, bf16[256,1024]{1,0:T(8,128)(2,1)S(1)}, u32[]{:S(2)}, u32[]{:S(2)}) collective-permute-start(bf16[256,1024]{1,0:T(8,128)(2,1)S(1)} %collective-permute-done.1.refs_1_.refs_5_), channel_id=1, source_target_pairs={{0,1},{1,0},{2,3},{3,2},{4,5},{5,4},{6,7},{7,6},{8,9},{9,8},{10,11... | collective-permute-start | bytes 1572872 | tf_op jit(solution)/shard_map/ppermute | solution.py:821
  62.2 19.6 %collective-permute-start.16 = (bf16[256,1024]{1,0:T(8,128)(2,1)}, bf16[256,1024]{1,0:T(8,128)(2,1)S(1)}, u32[]{:S(2)}, u32[]{:S(2)}) collective-permute-start(bf16[256,1024]{1,0:T(8,128)(2,1)} %bitcast.11.refs_2_.refs_4_.cotangent), channel_id=1, source_target_pairs={{0,2},{2,0},{1,3},{3,1},{4,6},{6,4},{5,7},{7,5},{8,10},{10,8},{9,1... | collective-permute-start | bytes 1572872 | tf_op jit(solution)/shard_map/ppermute | solution.py:821
  84.7 14.0 %collective-permute-start.18 = (bf16[256,1024]{1,0:T(8,128)(2,1)S(1)}, bf16[256,1024]{1,0:T(8,128)(2,1)S(1)}, u32[]{:S(2)}, u32[]{:S(2)}) collective-permute-start(bf16[256,1024]{1,0:T(8,128)(2,1)S(1)} %fusion.2), channel_id=1, source_target_pairs={{0,2},{2,0},{1,3},{3,1},{4,6},{6,4},{5,7},{7,5},{8,10},{10,8},{9,1... | collective-permute-start | bytes 1572872 | tf_op jit(solution)/shard_map/ppermute | solution.py:821
  86.1 16.9 %collective-permute-start.20 = (bf16[256,1024]{1,0:T(8,128)(2,1)}, bf16[256,1024]{1,0:T(8,128)(2,1)}, u32[]{:S(2)}, u32[]{:S(2)}) collective-permute-start(bf16[256,1024]{1,0:T(8,128)(2,1)} %bitcast.11.refs_2_.refs_4_.cotangent), channel_id=1, source_target_pairs={{0,1},{1,0},{2,3},{3,2},{4,5},{5,4},{6,7},{7,6},{8,9},{9,8},{10,11... | collective-permute-start | bytes 1572872 | tf_op jit(solution)/shard_map/ppermute | solution.py:821
  101.0 14.3 %collective-permute-start.22 = (bf16[256,1024]{1,0:T(8,128)(2,1)S(1)}, bf16[256,1024]{1,0:T(8,128)(2,1)S(1)}, u32[]{:S(2)}, u32[]{:S(2)}) collective-permute-start(bf16[256,1024]{1,0:T(8,128)(2,1)S(1)} %get-tuple-element.92.refs_0_), channel_id=1, source_target_pairs={{0,2},{2,0},{1,3},{3,1},{4,6},{6,4},{5,7},{7,5},{8,10},{10,8},{9,1... | collective-permute-start | bytes 1572872 | tf_op jit(solution)/shard_map/ppermute | solution.py:821
  102.3 13.5 %collective-permute-start.24 = (bf16[256,1024]{1,0:T(8,128)(2,1)S(1)}, bf16[256,1024]{1,0:T(8,128)(2,1)}, u32[]{:S(2)}, u32[]{:S(2)}) collective-permute-start(bf16[256,1024]{1,0:T(8,128)(2,1)S(1)} %collective-permute-done.16.refs_2_.refs_5_), channel_id=1, source_target_pairs={{0,1},{1,0},{2,3},{3,2},{4,5},{5,4},{6,7},{7,6},{8,9},{9,8},{10,11... | collective-permute-start | bytes 1572872 | tf_op jit(solution)/shard_map/ppermute | solution.py:821
  115.3 11.4 %collective-permute-start.21 = (bf16[256,1024]{1,0:T(8,128)(2,1)S(1)}, bf16[256,1024]{1,0:T(8,128)(2,1)S(1)}, u32[]{:S(2)}, u32[]{:S(2)}) collective-permute-start(bf16[256,1024]{1,0:T(8,128)(2,1)S(1)} %get-tuple-element.97), channel_id=1, source_target_pairs={{0,1},{1,0},{2,3},{3,2},{4,5},{5,4},{6,7},{7,6},{8,9},{9,8},{10,11... | collective-permute-start | bytes 1572872 | tf_op jit(solution)/shard_map/ppermute | solution.py:821
  128.7 14.0 %collective-permute-start.26 = (bf16[256,1024]{1,0:T(8,128)(2,1)S(1)}, bf16[256,1024]{1,0:T(8,128)(2,1)S(1)}, u32[]{:S(2)}, u32[]{:S(2)}) collective-permute-start(bf16[256,1024]{1,0:T(8,128)(2,1)S(1)} %add_convert_fusion.2), channel_id=1, source_target_pairs={{0,2},{2,0},{1,3},{3,1},{4,6},{6,4},{5,7},{7,5},{8,10},{10,8},{9,1... | collective-permute-start | bytes 1572872 | tf_op jit(solution)/shard_map/ppermute | solution.py:821
  145.5 13.1 %collective-permute-start.29 = (bf16[256,1024]{1,0:T(8,128)(2,1)S(1)}, bf16[256,1024]{1,0:T(8,128)(2,1)S(1)}, u32[]{:S(2)}, u32[]{:S(2)}) collective-permute-start(bf16[256,1024]{1,0:T(8,128)(2,1)S(1)} %get-tuple-element.108.refs_0_), channel_id=1, source_target_pairs={{0,2},{2,0},{1,3},{3,1},{4,6},{6,4},{5,7},{7,5},{8,10},{10,8},{9,1... | collective-permute-start | bytes 1572872 | tf_op jit(solution)/shard_map/ppermute | solution.py:821
  146.8 11.8 %collective-permute-start.30 = (bf16[256,1024]{1,0:T(8,128)(2,1)S(1)}, bf16[256,1024]{1,0:T(8,128)(2,1)S(1)}, u32[]{:S(2)}, u32[]{:S(2)}) collective-permute-start(bf16[256,1024]{1,0:T(8,128)(2,1)S(1)} %get-tuple-element.108.refs_0_), channel_id=1, source_target_pairs={{0,1},{1,0},{2,3},{3,2},{4,5},{5,4},{6,7},{7,6},{8,9},{9,8},{10,11... | collective-permute-start | bytes 1572872 | tf_op jit(solution)/shard_map/ppermute | solution.py:821
  187.0 58.8 %all-to-all-start = ((bf16[16,64,1664]{2,1,0:T(8,128)(2,1)}), bf16[16,64,1664]{2,1,0:T(8,128)(2,1)S(1)}, u32[]{:S(2)}, u32[]{:S(2)}) async-start(bf16[16,64,1664]{2,1,0:T(8,128)(2,1)} %bitcast.43), calls=%async_computation | async-start | bytes 6815744 | tf_op jit(solution)/shard_map/all_to_all | solution.py:842
  194.0 59.1 %reduce-scatter.5.cloned.1.call-start = ((), (), s32[]{:S(2)}) async-start(), calls=%async_computation.5 | async-start | bytes 1474560 | tf_op jit(solution)/shard_map/reduce_scatter | solution.py:948
  194.8 5.5 %collective-permute-start.32 = (bf16[2,256,1024]{2,1,0:T(8,128)(2,1)}, bf16[2,256,1024]{2,1,0:T(8,128)(2,1)S(1)}, u32[]{:S(2)}, u32[]{:S(2)}) collective-permute-start(bf16[2,256,1024]{2,1,0:T(8,128)(2,1)} %get-tuple-element.123), channel_id=1, source_target_pairs={{0,1},{1,0},{2,3},{3,2},{4,5},{5,4},{6,7},{7,6},{8,9},{9,8},{10,11... | collective-permute-start | bytes 3145736 | tf_op jit(solution)/shard_map/ppermute | solution.py:821
  198.9 14.8 %collective-permute-start.28 = (bf16[256,1024]{1,0:T(8,128)(2,1)S(1)}, bf16[256,1024]{1,0:T(8,128)(2,1)S(1)}, u32[]{:S(2)}, u32[]{:S(2)}) collective-permute-start(bf16[256,1024]{1,0:T(8,128)(2,1)S(1)} %fusion.3), channel_id=1, source_target_pairs={{0,2},{2,0},{1,3},{3,1},{4,6},{6,4},{5,7},{7,5},{8,10},{10,8},{9,1... | collective-permute-start | bytes 1572872 | tf_op jit(solution)/shard_map/ppermute | solution.py:821
  201.7 22.5 %collective-permute-start.33 = (bf16[256,1024]{1,0:T(8,128)(2,1)S(1)}, bf16[256,1024]{1,0:T(8,128)(2,1)S(1)}, u32[]{:S(2)}, u32[]{:S(2)}) collective-permute-start(bf16[256,1024]{1,0:T(8,128)(2,1)S(1)} %fusion.4), channel_id=1, source_target_pairs={{0,2},{2,0},{1,3},{3,1},{4,6},{6,4},{5,7},{7,5},{8,10},{10,8},{9,1... | collective-permute-start | bytes 1572872 | tf_op jit(solution)/shard_map/ppermute | solution.py:821
  246.9 6.2 %collective-permute-start.34 = (bf16[32,1664]{1,0:T(8,128)(2,1)S(1)}, bf16[32,1664]{1,0:T(8,128)(2,1)S(1)}, u32[]{:S(2)}, u32[]{:S(2)}) collective-permute-start(bf16[32,1664]{1,0:T(8,128)(2,1)S(1)} %get-tuple-element.129), channel_id=1, source_target_pairs={{0,4},{4,0},{1,5},{5,1},{2,6},{6,2},{3,7},{7,3},{8,12},{12,8},{9,1... | collective-permute-start | bytes 319496 | tf_op jit(solution)/shard_map/ppermute | solution.py:821
  254.1 10.3 %collective-permute-start.38 = (bf16[32,2304]{1,0:T(8,128)(2,1)S(1)}, bf16[32,2304]{1,0:T(8,128)(2,1)S(1)}, u32[]{:S(2)}, u32[]{:S(2)}) collective-permute-start(bf16[32,2304]{1,0:T(8,128)(2,1)S(1)} %get-tuple-element.141), channel_id=1, source_target_pairs={{0,4},{4,0},{1,5},{5,1},{2,6},{6,2},{3,7},{7,3},{8,12},{12,8},{9,1... | collective-permute-start | bytes 442376 | tf_op jit(solution)/shard_map/ppermute | solution.py:821
  (35 other events, 404.1 us)
Sparse Core Ops, SparseCore 0:
  49.4 53.7 all-gather.1
  140.3 51.0 reduce-scatter.2
  197.2 52.5 reduce-scatter.4

commit v2 on v1

--- a/solution.py
+++ b/solution.py
@@ -143,17 +143,28 @@
     pieces, refs = refs[4 : 4 + n_pieces], refs[4 + n_pieces :]
     cos, sin = refs[:2]
     first, qraw, kraw, low, att, totals, mine, other, gains, head_gains, ordered = refs[2:13]
-    rows, keys, values, weights, piece_sems, ordered_sem = refs[13:]
+    rows, scaled, keys, values, weights, piece_sems, ordered_sem = refs[13:]
     i = pl.program_id(0)
     nq, nqkv = qraw.shape[1], low.shape[1]
     wqkv = weights.at[:, :nqkv]
     wo = weights.at[:, nqkv : nqkv + nq]
     columns = weights.at[:, nqkv + nq :]
     keep = pltpu.make_async_copy(weights, ordered, ordered_sem)
+    loads = load_pieces(order, pieces, weights, piece_sems)
 
     @pl.when(i == 0)
     def _():
-        for copy in load_pieces(order, pieces, weights, piece_sems):
+        for copy in loads:
+            copy.start()
+
+    for a in range(2):
+        pick(place[2 * i + a], tokens, rows.at[a * ROWS : (a + 1) * ROWS, :])
+    x = rows[...].astype(f32)
+    scaled[...] = x * inverse_rms(x)
+
+    @pl.when(i == 0)
+    def _():
+        for copy in loads:
             copy.wait()
         keep.start()
         gains[:2, :] = jnp.concatenate([row_of(columns, 0), row_of(columns, 1)], axis=0)
@@ -162,10 +173,7 @@
         head_gains[2:, :] = jnp.zeros_like(head_gains[2:, :])
 
     gain, qgain, kgain = gains[:1, :], head_gains[:1, :], head_gains[1:2, :]
-    for a in range(2):
-        pick(place[2 * i + a], tokens, rows.at[a * ROWS : (a + 1) * ROWS, :])
-    x = rows[...].astype(f32)
-    normed = (x * inverse_rms(x) * gain).astype(bf16)
+    normed = (scaled[...] * gain).astype(bf16)
     first[...] = normed
     qkv = matmul(normed, wqkv[...])
     nq, nk = qraw.shape[1], kraw.shape[1]
@@ -257,6 +265,7 @@
             out_specs=[o[2] for o in out],
             scratch_shapes=[
                 pltpu.VMEM((2 * ROWS, width), bf16),
+                pltpu.VMEM((2 * ROWS, width), f32),
                 pltpu.VMEM((nk // HD, length, HD), bf16),
                 pltpu.VMEM((nk // HD, length, 2 * HD), bf16),
                 pltpu.VMEM((width, nqkv + nq + HD), bf16),
@@ -811,7 +820,6 @@
                         target.at[pl.ds(place, rows), side * cut : side * cut + wide],
                         semaphores.at[side, n],
                     )
-                    copy.start()
                     copies.append(copy)
                     n += 1
     return copies
@@ -842,7 +850,7 @@
     return lax.all_to_all(blocks, PLANE, 0, 0, tiled=True)
 
 
-def by_distance(sides):
+def by_distance(sides, staged):
     done = [{0: own} for own, _ in sides]
     before = []
     for near in (True, False):
@@ -854,7 +862,7 @@
                     perm = [(s, (s - j) % n) for s in range(n)]
                     kept[j] = lax.ppermute(after(own, *before) if before else own, axis, perm)
                     arrived.append(kept[j])
-        before = arrived
+        before = arrived if staged else []
     return [[kept[j] for j in sorted(kept)] for kept in done]
 
 
@@ -919,9 +927,9 @@
     split = nq + 2 * nk + nq + HD
     left, right, feed = pair(lax.axis_index("zh").reshape(1), shard, over_zh, nq + nk, split)
     order = gathered_order()
-    left, right = by_distance([(left, "x"), (right, "y")])
+    left, right = by_distance([(left, "x"), (right, "y")], False)
     token_blocks = tp_gather(after(x, over_zh))
-    left, right = by_distance([(jnp.stack(left), "y"), (jnp.stack(right), "x")])
+    left, right = by_distance([(jnp.stack(left), "y"), (jnp.stack(right), "x")], True)
     feed = lax.all_gather(after(feed, left[1], left[-1], right[1], right[-1]), PLANE, axis=0, tiled=True)
     grads_over_z = swapped(after(dy, *left, *right), "zl")
 

time: 277 us -> 275 us (level)
  waiting for transfers between devices: 114 us -> 109 us
    ppermute x12, waiting for transfers between devices: 19.7 us -> 15 us  [by_distance(): kept[j] = lax.ppermute(after(own, *before) if before else own, axis, perm)]
where the time goes in v2:
time: 275 us; the launch traced here: 269 us
  waiting for transfers between devices  109 us (40%)
  Pallas kernels  90.7 us (33%)
  starting transfers between devices  45.2 us (16%)
  between operations  14.4 us (5%)
  other arithmetic  5.27 us (2%)
  local copies, waits for them, and re-layouts  4.46 us (2%)
    ppermute x26, waiting for transfers between devices, swapped(): return lax.ppermute(value, axis, [(0, 1), (1, 0)])  73.1 us
    pallas_call x1, Pallas kernels, backward_attention(): pl.pallas_call(functools.partial(backward_attention_kernel, width // lax....  26.5 us
    ppermute x26, starting transfers between devices, swapped(): return lax.ppermute(value, axis, [(0, 1), (1, 0)])  25.5 us
    all_to_all x1, waiting for transfers between devices, sent_rows(): return lax.all_to_all(blocks, PLANE, 0, 0, tiled=True)  19 us
    pallas_call x2, Pallas kernels, feed_step(): pl.pallas_call(feed_kernel, in_specs=[pl.BlockSpec(memory_space=pl.ANY)]...  18.4 us
    pallas_call x1, Pallas kernels, forward_attention(): pl.pallas_call(functools.partial(forward_attention_kernel, width // lax.a...  18.1 us
    ppermute x12, waiting for transfers between devices, by_distance(): kept[j] = lax.ppermute(after(own, *before) if before else own, axis, perm)  15 us
    ppermute x12, starting transfers between devices, by_distance(): kept[j] = lax.ppermute(after(own, *before) if before else own, axis, perm)  12.6 us
  transfers between devices with their start and end apart: 43, of which 24 were waited for; matrix products, arithmetic and copies ran while one was open for 2% of the time, Pallas kernels for 32%

profile of v2, /device:TPU:28, one launch (start us, length us, event | category | flops | bytes accessed | tf_op | source)
XLA Modules:
  0.0 269.4 jit_solution(7744356075732821628)
XLA Ops:
  9.1 4.0 %collective-permute-start = (bf16[32,3968]{1,0:T(8,128)(2,1)S(1)}, bf16[32,3968]{1,0:T(8,128)(2,1)S(1)}, u32[]{:S(2)}, u32[]{:S(2)}) collective-permute-start(bf16[32,3968]{1,0:T(8,128)(2,1)S(1)} %pack.1.shard), channel_id=1, source_target_pairs={{0,4},{4,0},{1,5},{5,1},{2,6},{6,2},{3,7},{7,3},{8,12},{12,8},{9,1... | collective-permute-start | bytes 761864 | tf_op jit(solution)/shard_map/ppermute | solution.py:829
  13.0 6.1 %collective-permute-done.other = bf16[32,3968]{1,0:T(8,128)(2,1)S(1)} collective-permute-done((bf16[32,3968]{1,0:T(8,128)(2,1)S(1)}, bf16[32,3968]{1,0:T(8,128)(2,1)S(1)}, u32[]{:S(2)}, u32[]{:S(2)}) %collective-permute-start) | collective-permute-done | bytes 253984 | tf_op jit(solution)/shard_map/ppermute | solution.py:829
  20.2 2.6 collective-permute-start.10
  31.2 4.5 %collective-permute-start.8 = (bf16[4,2,32,768]{3,2,1,0:T(8,128)(2,1)S(1)}, bf16[4,2,32,768]{3,2,1,0:T(8,128)(2,1)S(1)}, u32[]{:S(2)}, u32[]{:S(2)}) collective-permute-start(bf16[4,2,32,768]{3,2,1,0:T(8,128)(2,1)S(1)} %pad_maximum_fusion.1.refs_4_), channel_id=1, source_target_pairs={{0,8},{8,16},{16,24},{24,0},{1,9},{9,17},{17,25},{25,1},{2,10},{10... | collective-permute-start | bytes 1179656 | tf_op jit(solution)/shard_map/ppermute | solution.py:863
  35.6 5.3 %collective-permute-done.8.refs_7_ = bf16[4,2,32,768]{3,2,1,0:T(8,128)(2,1)S(1)} collective-permute-done((bf16[4,2,32,768]{3,2,1,0:T(8,128)(2,1)S(1)}, bf16[4,2,32,768]{3,2,1,0:T(8,128)(2,1)S(1)}, u32[]{:S(2)}, u32[]{:S(2)}) %collective-permute-start.8) | collective-permute-done | bytes 393248 | tf_op jit(solution)/shard_map/ppermute | solution.py:863
  40.9 3.7 %collective-permute-done.7.refs_5_ = bf16[4,2,32,768]{3,2,1,0:T(8,128)(2,1)S(1)} collective-permute-done((bf16[4,2,32,768]{3,2,1,0:T(8,128)(2,1)S(1)}, bf16[4,2,32,768]{3,2,1,0:T(8,128)(2,1)S(1)}, u32[]{:S(2)}, u32[]{:S(2)}) %collective-permute-start.7) | collective-permute-done | bytes 393248 | tf_op jit(solution)/shard_map/ppermute | solution.py:863
  48.8 6.8 %collective-permute-done.1.refs_1_.refs_5_ = bf16[256,1024]{1,0:T(8,128)(2,1)S(1)} collective-permute-done((bf16[256,1024]{1,0:T(8,128)(2,1)S(1)}, bf16[256,1024]{1,0:T(8,128)(2,1)S(1)}, u32[]{:S(2)}, u32[]{:S(2)}) %collective-permute-start.1) | collective-permute-done | bytes 524320 | tf_op jit(solution)/shard_map/ppermute | solution.py:829
  55.6 2.3 collective-permute-done.14.refs_6_
  60.3 18.1 %forward_attention.1 = (bf16[1024,1024]{1,0:T(8,128)(2,1)}, f32[1024,512]{1,0:T(8,128)}, f32[1024,256]{1,0:T(8,128)}, bf16[1024,1024]{1,0:T(8,128)(2,1)}, bf16[1...) custom-call(s32[8]{0:T(128)S(1)} %pad_add_fusion.1.place, ...), custom_call_target="tpu_custom_call" | custom-call | flops 875000000 | bytes 2000000 | tf_op jit(solution)/shard_map/forward_attention/pallas_call | solution.py:254
  78.5 2.6 collective-permute-done.17.from_core
  82.8 12.6 %collective-permute-done.18.from_z = bf16[256,1024]{1,0:T(8,128)(2,1)S(1)} collective-permute-done((bf16[256,1024]{1,0:T(8,128)(2,1)S(1)}, bf16[256,1024]{1,0:T(8,128)(2,1)S(1)}, u32[]{:S(2)}, u32[]{:S(2)}) %collective-permute-start.18) | collective-permute-done | bytes 524320 | tf_op jit(solution)/shard_map/ppermute | solution.py:829
  95.4 2.2 middle_step.1
  100.3 9.1 %feed_step.2 = (bf16[512,768]{1,0:T(8,128)(2,1)}, bf16[512,1536]{1,0:T(8,128)(2,1)}, bf16[256,1024]{1,0:T(8,128)(2,1)S(1)}, bf16[256,1024]{1,0:T(8,128)(2,1)S(1)}) custom-call(bf16[256,1024]{1,0:T(8,128)(2,1)S(1)} %get-tuple-element.88.refs_0_, bf16[256,1024]{1,0:T(8,128)(2,1)S(1)} %collective-permute-done.19.refs_1_.refs_2_, ...), custom_call_target="tpu_custom_call" | custom-call | flops 500000000 | bytes 1000000 | tf_op jit(solution)/shard_map/feed_step/pallas_call | solution.py:347
  109.4 2.6 collective-permute-done.22.refs_0_.refs_1_
  113.9 9.3 %feed_step.3 = (bf16[512,768]{1,0:T(8,128)(2,1)}, bf16[512,1536]{1,0:T(8,128)(2,1)}, bf16[256,1024]{1,0:T(8,128)(2,1)S(1)}, bf16[256,1024]{1,0:T(8,128)(2,1)S(1)}) custom-call(bf16[256,1024]{1,0:T(8,128)(2,1)S(1)} %collective-permute-done.22.refs_0_.refs_1_, bf16[256,1024]{1,0:T(8,128)(2,1)S(1)} %collective-permute-done.23.refs_1_.refs_3_, ...), custom_call_target="tpu_custom_call" | custom-call | flops 500000000 | bytes 1000000 | tf_op jit(solution)/shard_map/feed_step/pallas_call | solution.py:347
  126.8 10.0 %feed_weights.1 = bf16[1024,2304]{1,0:T(8,128)(2,1)} custom-call(bf16[256,1024]{1,0:T(8,128)(2,1)} %copy-done.1, bf16[256,1024]{1,0:T(8,128)(2,1)} %copy-done.3, bf16[256,1024]{1,0:T(8,128)(2,1)} %copy-done.2, bf16[256,1024]{1,0:T(8,128)(2,1)} %copy-done.4, bf16[256,1024]{1,0:T(8,128)(2,1)} %bitcast.11.refs_2_.refs_4_.cotangent, ...), custom_call_target="tpu_custom_call" | custom-call | flops 600000000 | bytes 1750000 | tf_op jit(solution)/shard_map/feed_weights/pallas_call | solution.py:412
  136.9 2.6 collective-permute-done.26.from_z
  139.5 2.7 %middle_back.1 = (f32[256,1024]{1,0:T(8,128)}, bf16[256,1024]{1,0:T(8,128)(2,1)S(1)}, f32[8,1024]{1,0:T(8,128)}) custom-call(f32[256,1024]{1,0:T(8,128)} %get-tuple-element.87.middle, bf16[256,1024]{1,0:T(8,128)(2,1)S(1)} %get-tuple-element.92.mine, bf16[256,1024]{1,0:T(8,128)(2,1)S(1)} %collective-permute-done.21.from_core, ...), custom_call_target="tpu_custom_call" | custom-call | flops 500000 | bytes 625000 | tf_op jit(solution)/shard_map/middle_back/pallas_call | solution.py:447
  143.5 4.9 %feed_out.1 = (bf16[2,256,1024]{2,1,0:T(8,128)(2,1)}, bf16[2,256,1024]{2,1,0:T(8,128)(2,1)}) custom-call(bf16[512,768]{1,0:T(8,128)(2,1)} %get-tuple-element.105.refs_10_.first, bf16[512,768]{1,0:T(8,128)(2,1)} %get-tuple-element.102.refs_11_.then, bf16[1024,2304]{1,0:T(8,128)(2,1)} %all-gather.2.cloned.1.call-done.refs_4_.wd), custom_call_target="tpu_custom_call" | custom-call | flops 200000000 | bytes 625000 | tf_op jit(solution)/shard_map/feed_out/pallas_call | solution.py:381
  148.4 6.9 %collective-permute-done.29.refs_1_ = bf16[256,1024]{1,0:T(8,128)(2,1)S(1)} collective-permute-done((bf16[256,1024]{1,0:T(8,128)(2,1)S(1)}, bf16[256,1024]{1,0:T(8,128)(2,1)S(1)}, u32[]{:S(2)}, u32[]{:S(2)}) %collective-permute-start.29) | collective-permute-done | bytes 524320 | tf_op jit(solution)/shard_map/ppermute | solution.py:829
  155.3 1.9 collective-permute-done.31.refs_3_
  157.2 26.5 %backward_attention.1 = (bf16[2,256,1024]{2,1,0:T(8,128)(2,1)}, bf16[2,256,1024]{2,1,0:T(8,128)(2,1)}, bf16[1024,1664]{1,0:T(8,128)(2,1)}) custom-call(s32[8]{0:T(128)S(1)} %pad_add_fusion.1.place, bf16[256,1024]{1,0:T(8,128)(2,1)S(1)} %get-tuple-element.104.refs_0_, bf16[256,1024]{1,0:T(8,128)(2,1)S(1)} %collective-permute-done.29.refs_1_, ...), custom_call_target="tpu_custom_call" | custom-call | flops 74999996416 | bytes 2250000 | tf_op jit(solution)/shard_map/backward_attention/pallas_call | solution.py:607
  183.7 6.9 %all-to-all-start = ((bf16[16,64,1664]{2,1,0:T(8,128)(2,1)}), bf16[16,64,1664]{2,1,0:T(8,128)(2,1)S(1)}, u32[]{:S(2)}, u32[]{:S(2)}) async-start(bf16[16,64,1664]{2,1,0:T(8,128)(2,1)} %bitcast.43), calls=%async_computation | async-start | bytes 6815744 | tf_op jit(solution)/shard_map/all_to_all | solution.py:850
  192.0 2.4 collective-permute-done.27
  199.1 11.3 %collective-permute-done.28 = bf16[256,1024]{1,0:T(8,128)(2,1)S(1)} collective-permute-done((bf16[256,1024]{1,0:T(8,128)(2,1)S(1)}, bf16[256,1024]{1,0:T(8,128)(2,1)S(1)}, u32[]{:S(2)}, u32[]{:S(2)}) %collective-permute-start.28) | collective-permute-done | bytes 524320 | tf_op jit(solution)/shard_map/ppermute | solution.py:829
  211.6 9.3 %collective-permute-done.33.from_z = bf16[256,1024]{1,0:T(8,128)(2,1)S(1)} collective-permute-done((bf16[256,1024]{1,0:T(8,128)(2,1)S(1)}, bf16[256,1024]{1,0:T(8,128)(2,1)S(1)}, u32[]{:S(2)}, u32[]{:S(2)}) %collective-permute-start.33) | collective-permute-done | bytes 524320 | tf_op jit(solution)/shard_map/ppermute | solution.py:829
  220.9 2.6 tokens_back.1
  223.5 19.0 %all-to-all-done.parts = bf16[16,64,1664]{2,1,0:T(8,128)(2,1)S(1)} async-done(((bf16[16,64,1664]{2,1,0:T(8,128)(2,1)}), bf16[16,64,1664]{2,1,0:T(8,128)(2,1)S(1)}, u32[]{:S(2)}, u32[]{:S(2)}) %all-to-all-start) | async-done | bytes 3407904 | tf_op jit(solution)/shard_map/all_to_all | solution.py:850
  243.6 3.6 %collective-permute-start.34 = (bf16[32,1664]{1,0:T(8,128)(2,1)S(1)}, bf16[32,1664]{1,0:T(8,128)(2,1)S(1)}, u32[]{:S(2)}, u32[]{:S(2)}) collective-permute-start(bf16[32,1664]{1,0:T(8,128)(2,1)S(1)} %get-tuple-element.125), channel_id=1, source_target_pairs={{0,4},{4,0},{1,5},{5,1},{2,6},{6,2},{3,7},{7,3},{8,12},{12,8},{9,1... | collective-permute-start | bytes 319496 | tf_op jit(solution)/shard_map/ppermute | solution.py:829
  247.2 2.7 collective-permute-done.34.arrived
  250.9 3.6 %collective-permute-start.38 = (bf16[32,2304]{1,0:T(8,128)(2,1)S(1)}, bf16[32,2304]{1,0:T(8,128)(2,1)S(1)}, u32[]{:S(2)}, u32[]{:S(2)}) collective-permute-start(bf16[32,2304]{1,0:T(8,128)(2,1)S(1)} %get-tuple-element.137), channel_id=1, source_target_pairs={{0,4},{4,0},{1,5},{5,1},{2,6},{6,2},{3,7},{7,3},{8,12},{12,8},{9,1... | collective-permute-start | bytes 442376 | tf_op jit(solution)/shard_map/ppermute | solution.py:829
  259.3 2.0 collective-permute-done.35.refs_1_
  (138 shorter events, 44.3 us)
Async XLA Ops:
  7.2 93.1 %all-gather.2.cloned.1.call-start = ((), (), s32[]{:S(2)}) async-start(), calls=%async_computation.3 | async-start | bytes 5013504 | tf_op jit(solution)/shard_map/all_gather | solution.py:933
  9.1 10.1 %collective-permute-start = (bf16[32,3968]{1,0:T(8,128)(2,1)S(1)}, bf16[32,3968]{1,0:T(8,128)(2,1)S(1)}, u32[]{:S(2)}, u32[]{:S(2)}) collective-permute-start(bf16[32,3968]{1,0:T(8,128)(2,1)S(1)} %pack.1.shard), channel_id=1, source_target_pairs={{0,4},{4,0},{1,5},{5,1},{2,6},{6,2},{3,7},{7,3},{8,12},{12,8},{9,1... | collective-permute-start | bytes 761864 | tf_op jit(solution)/shard_map/ppermute | solution.py:829
  19.9 5.6 %collective-permute-start.11 = (bf16[2,32,896]{2,1,0:T(8,128)(2,1)S(1)}, bf16[2,32,896]{2,1,0:T(8,128)(2,1)S(1)}, u32[]{:S(2)}, u32[]{:S(2)}) collective-permute-start(bf16[2,32,896]{2,1,0:T(8,128)(2,1)S(1)} %get-tuple-element.79), channel_id=1, source_target_pairs={{0,8},{8,16},{16,24},{24,0},{1,9},{9,17},{17,25},{25,1},{2,10},{10... | collective-permute-start | bytes 344072 | tf_op jit(solution)/shard_map/ppermute | solution.py:863
  20.2 7.4 %collective-permute-start.10 = (bf16[2,32,896]{2,1,0:T(8,128)(2,1)S(1)}, bf16[2,32,896]{2,1,0:T(8,128)(2,1)S(1)}, u32[]{:S(2)}, u32[]{:S(2)}) collective-permute-start(bf16[2,32,896]{2,1,0:T(8,128)(2,1)S(1)} %get-tuple-element.79), channel_id=1, source_target_pairs={{0,16},{8,24},{16,0},{24,8},{1,17},{9,25},{17,1},{25,9},{2,18},{10... | collective-permute-start | bytes 344072 | tf_op jit(solution)/shard_map/ppermute | solution.py:863
  22.7 6.2 %collective-permute-start.9 = (bf16[2,32,896]{2,1,0:T(8,128)(2,1)S(1)}, bf16[2,32,896]{2,1,0:T(8,128)(2,1)S(1)}, u32[]{:S(2)}, u32[]{:S(2)}) collective-permute-start(bf16[2,32,896]{2,1,0:T(8,128)(2,1)S(1)} %get-tuple-element.79), channel_id=1, source_target_pairs={{0,24},{8,0},{16,8},{24,16},{1,25},{9,1},{17,9},{25,17},{2,26},{10... | collective-permute-start | bytes 344072 | tf_op jit(solution)/shard_map/ppermute | solution.py:863
  22.7 8.3 %collective-permute-start.6 = (bf16[2,32,768]{2,1,0:T(8,128)(2,1)S(1)}, bf16[2,32,768]{2,1,0:T(8,128)(2,1)S(1)}, u32[]{:S(2)}, u32[]{:S(2)}) collective-permute-start(bf16[2,32,768]{2,1,0:T(8,128)(2,1)S(1)} %get-tuple-element.78), channel_id=1, source_target_pairs={{0,32},{32,64},{64,96},{96,0},{1,33},{33,65},{65,97},{97,1},{2,34}... | collective-permute-start | bytes 294920 | tf_op jit(solution)/shard_map/ppermute | solution.py:863
  23.9 7.2 %collective-permute-start.5 = (bf16[2,32,768]{2,1,0:T(8,128)(2,1)S(1)}, bf16[2,32,768]{2,1,0:T(8,128)(2,1)S(1)}, u32[]{:S(2)}, u32[]{:S(2)}) collective-permute-start(bf16[2,32,768]{2,1,0:T(8,128)(2,1)S(1)} %get-tuple-element.78), channel_id=1, source_target_pairs={{0,64},{32,96},{64,0},{96,32},{1,65},{33,97},{65,1},{97,33},{2,66}... | collective-permute-start | bytes 294920 | tf_op jit(solution)/shard_map/ppermute | solution.py:863
  25.5 5.6 %collective-permute-start.4 = (bf16[2,32,768]{2,1,0:T(8,128)(2,1)S(1)}, bf16[2,32,768]{2,1,0:T(8,128)(2,1)S(1)}, u32[]{:S(2)}, u32[]{:S(2)}) collective-permute-start(bf16[2,32,768]{2,1,0:T(8,128)(2,1)S(1)} %get-tuple-element.78), channel_id=1, source_target_pairs={{0,96},{32,0},{64,32},{96,64},{1,97},{33,1},{65,33},{97,65},{2,98}... | collective-permute-start | bytes 294920 | tf_op jit(solution)/shard_map/ppermute | solution.py:863
  29.0 15.6 %collective-permute-start.13 = (bf16[4,2,32,896]{3,2,1,0:T(8,128)(2,1)S(1)}, bf16[4,2,32,896]{3,2,1,0:T(8,128)(2,1)S(1)}, u32[]{:S(2)}, u32[]{:S(2)}) collective-permute-start(bf16[4,2,32,896]{3,2,1,0:T(8,128)(2,1)S(1)} %pad_maximum_fusion.refs_8_), channel_id=1, source_target_pairs={{0,32},{32,64},{64,96},{96,0},{1,33},{33,65},{65,97},{97,1},{2,34}... | collective-permute-start | bytes 1376264 | tf_op jit(solution)/shard_map/ppermute | solution.py:863
  30.3 14.4 %collective-permute-start.12 = (bf16[4,2,32,896]{3,2,1,0:T(8,128)(2,1)S(1)}, bf16[4,2,32,896]{3,2,1,0:T(8,128)(2,1)S(1)}, u32[]{:S(2)}, u32[]{:S(2)}) collective-permute-start(bf16[4,2,32,896]{3,2,1,0:T(8,128)(2,1)S(1)} %pad_maximum_fusion.refs_8_), channel_id=1, source_target_pairs={{0,96},{32,0},{64,32},{96,64},{1,97},{33,1},{65,33},{97,65},{2,98}... | collective-permute-start | bytes 1376264 | tf_op jit(solution)/shard_map/ppermute | solution.py:863
  31.2 9.7 %collective-permute-start.8 = (bf16[4,2,32,768]{3,2,1,0:T(8,128)(2,1)S(1)}, bf16[4,2,32,768]{3,2,1,0:T(8,128)(2,1)S(1)}, u32[]{:S(2)}, u32[]{:S(2)}) collective-permute-start(bf16[4,2,32,768]{3,2,1,0:T(8,128)(2,1)S(1)} %pad_maximum_fusion.1.refs_4_), channel_id=1, source_target_pairs={{0,8},{8,16},{16,24},{24,0},{1,9},{9,17},{17,25},{25,1},{2,10},{10... | collective-permute-start | bytes 1179656 | tf_op jit(solution)/shard_map/ppermute | solution.py:863
  35.6 9.0 %collective-permute-start.7 = (bf16[4,2,32,768]{3,2,1,0:T(8,128)(2,1)S(1)}, bf16[4,2,32,768]{3,2,1,0:T(8,128)(2,1)S(1)}, u32[]{:S(2)}, u32[]{:S(2)}) collective-permute-start(bf16[4,2,32,768]{3,2,1,0:T(8,128)(2,1)S(1)} %pad_maximum_fusion.1.refs_4_), channel_id=1, source_target_pairs={{0,24},{8,0},{16,8},{24,16},{1,25},{9,1},{17,9},{25,17},{2,26},{10... | collective-permute-start | bytes 1179656 | tf_op jit(solution)/shard_map/ppermute | solution.py:863
  46.3 144.4 %reduce-scatter.3.cloned.1.call-start = ((), (), s32[]{:S(2)}) async-start(), calls=%async_computation.4 | async-start | bytes 5898240 | tf_op jit(solution)/shard_map/reduce_scatter | solution.py:955
  46.4 9.3 %collective-permute-start.1 = (bf16[256,1024]{1,0:T(8,128)(2,1)S(1)}, bf16[256,1024]{1,0:T(8,128)(2,1)S(1)}, u32[]{:S(2)}, u32[]{:S(2)}) collective-permute-start(bf16[256,1024]{1,0:T(8,128)(2,1)S(1)} %bitcast.41), channel_id=1, source_target_pairs={{0,2},{2,0},{1,3},{3,1},{4,6},{6,4},{5,7},{7,5},{8,10},{10,8},{9,1... | collective-permute-start | bytes 1572872 | tf_op jit(solution)/shard_map/ppermute | solution.py:829
  48.0 10.0 %collective-permute-start.15 = (bf16[4,2,32,896]{3,2,1,0:T(8,128)(2,1)S(1)}, bf16[4,2,32,896]{3,2,1,0:T(8,128)(2,1)S(1)}, u32[]{:S(2)}, u32[]{:S(2)}) collective-permute-start(bf16[4,2,32,896]{3,2,1,0:T(8,128)(2,1)S(1)} %pad_maximum_fusion.refs_8_), channel_id=1, source_target_pairs={{0,64},{32,96},{64,0},{96,32},{1,65},{33,97},{65,1},{97,33},{2,66}... | collective-permute-start | bytes 1376264 | tf_op jit(solution)/shard_map/ppermute | solution.py:863
  48.7 9.3 %collective-permute-start.14 = (bf16[4,2,32,768]{3,2,1,0:T(8,128)(2,1)S(1)}, bf16[4,2,32,768]{3,2,1,0:T(8,128)(2,1)S(1)}, u32[]{:S(2)}, u32[]{:S(2)}) collective-permute-start(bf16[4,2,32,768]{3,2,1,0:T(8,128)(2,1)S(1)} %pad_maximum_fusion.1.refs_4_), channel_id=1, source_target_pairs={{0,16},{8,24},{16,0},{24,8},{1,17},{9,25},{17,1},{25,9},{2,18},{10... | collective-permute-start | bytes 1179656 | tf_op jit(solution)/shard_map/ppermute | solution.py:863
  48.8 11.4 %collective-permute-start.2 = (bf16[256,1024]{1,0:T(8,128)(2,1)S(1)}, bf16[256,1024]{1,0:T(8,128)(2,1)S(1)}, u32[]{:S(2)}, u32[]{:S(2)}) collective-permute-start(bf16[256,1024]{1,0:T(8,128)(2,1)S(1)} %bitcast.42), channel_id=1, source_target_pairs={{0,1},{1,0},{2,3},{3,2},{4,5},{5,4},{6,7},{7,6},{8,9},{9,8},{10,11... | collective-permute-start | bytes 1572872 | tf_op jit(solution)/shard_map/ppermute | solution.py:829
  58.9 19.5 %collective-permute-start.16 = (bf16[256,1024]{1,0:T(8,128)(2,1)}, bf16[256,1024]{1,0:T(8,128)(2,1)S(1)}, u32[]{:S(2)}, u32[]{:S(2)}) collective-permute-start(bf16[256,1024]{1,0:T(8,128)(2,1)} %bitcast.11.refs_2_.refs_4_.cotangent), channel_id=1, source_target_pairs={{0,2},{2,0},{1,3},{3,1},{4,6},{6,4},{5,7},{7,5},{8,10},{10,8},{9,1... | collective-permute-start | bytes 1572872 | tf_op jit(solution)/shard_map/ppermute | solution.py:829
  81.4 14.0 %collective-permute-start.18 = (bf16[256,1024]{1,0:T(8,128)(2,1)S(1)}, bf16[256,1024]{1,0:T(8,128)(2,1)S(1)}, u32[]{:S(2)}, u32[]{:S(2)}) collective-permute-start(bf16[256,1024]{1,0:T(8,128)(2,1)S(1)} %fusion.2), channel_id=1, source_target_pairs={{0,2},{2,0},{1,3},{3,1},{4,6},{6,4},{5,7},{7,5},{8,10},{10,8},{9,1... | collective-permute-start | bytes 1572872 | tf_op jit(solution)/shard_map/ppermute | solution.py:829
  82.8 16.9 %collective-permute-start.20 = (bf16[256,1024]{1,0:T(8,128)(2,1)}, bf16[256,1024]{1,0:T(8,128)(2,1)}, u32[]{:S(2)}, u32[]{:S(2)}) collective-permute-start(bf16[256,1024]{1,0:T(8,128)(2,1)} %bitcast.11.refs_2_.refs_4_.cotangent), channel_id=1, source_target_pairs={{0,1},{1,0},{2,3},{3,2},{4,5},{5,4},{6,7},{7,6},{8,9},{9,8},{10,11... | collective-permute-start | bytes 1572872 | tf_op jit(solution)/shard_map/ppermute | solution.py:829
  97.6 14.3 %collective-permute-start.22 = (bf16[256,1024]{1,0:T(8,128)(2,1)S(1)}, bf16[256,1024]{1,0:T(8,128)(2,1)S(1)}, u32[]{:S(2)}, u32[]{:S(2)}) collective-permute-start(bf16[256,1024]{1,0:T(8,128)(2,1)S(1)} %get-tuple-element.88.refs_0_), channel_id=1, source_target_pairs={{0,2},{2,0},{1,3},{3,1},{4,6},{6,4},{5,7},{7,5},{8,10},{10,8},{9,1... | collective-permute-start | bytes 1572872 | tf_op jit(solution)/shard_map/ppermute | solution.py:829
  99.0 13.5 %collective-permute-start.24 = (bf16[256,1024]{1,0:T(8,128)(2,1)S(1)}, bf16[256,1024]{1,0:T(8,128)(2,1)}, u32[]{:S(2)}, u32[]{:S(2)}) collective-permute-start(bf16[256,1024]{1,0:T(8,128)(2,1)S(1)} %collective-permute-done.16.refs_2_.refs_5_), channel_id=1, source_target_pairs={{0,1},{1,0},{2,3},{3,2},{4,5},{5,4},{6,7},{7,6},{8,9},{9,8},{10,11... | collective-permute-start | bytes 1572872 | tf_op jit(solution)/shard_map/ppermute | solution.py:829
  112.0 11.4 %collective-permute-start.21 = (bf16[256,1024]{1,0:T(8,128)(2,1)S(1)}, bf16[256,1024]{1,0:T(8,128)(2,1)S(1)}, u32[]{:S(2)}, u32[]{:S(2)}) collective-permute-start(bf16[256,1024]{1,0:T(8,128)(2,1)S(1)} %get-tuple-element.93), channel_id=1, source_target_pairs={{0,1},{1,0},{2,3},{3,2},{4,5},{5,4},{6,7},{7,6},{8,9},{9,8},{10,11... | collective-permute-start | bytes 1572872 | tf_op jit(solution)/shard_map/ppermute | solution.py:829
  125.4 14.0 %collective-permute-start.26 = (bf16[256,1024]{1,0:T(8,128)(2,1)S(1)}, bf16[256,1024]{1,0:T(8,128)(2,1)S(1)}, u32[]{:S(2)}, u32[]{:S(2)}) collective-permute-start(bf16[256,1024]{1,0:T(8,128)(2,1)S(1)} %add_convert_fusion.2), channel_id=1, source_target_pairs={{0,2},{2,0},{1,3},{3,1},{4,6},{6,4},{5,7},{7,5},{8,10},{10,8},{9,1... | collective-permute-start | bytes 1572872 | tf_op jit(solution)/shard_map/ppermute | solution.py:829
  142.2 13.1 %collective-permute-start.29 = (bf16[256,1024]{1,0:T(8,128)(2,1)S(1)}, bf16[256,1024]{1,0:T(8,128)(2,1)S(1)}, u32[]{:S(2)}, u32[]{:S(2)}) collective-permute-start(bf16[256,1024]{1,0:T(8,128)(2,1)S(1)} %get-tuple-element.104.refs_0_), channel_id=1, source_target_pairs={{0,2},{2,0},{1,3},{3,1},{4,6},{6,4},{5,7},{7,5},{8,10},{10,8},{9,1... | collective-permute-start | bytes 1572872 | tf_op jit(solution)/shard_map/ppermute | solution.py:829
  143.5 11.8 %collective-permute-start.30 = (bf16[256,1024]{1,0:T(8,128)(2,1)S(1)}, bf16[256,1024]{1,0:T(8,128)(2,1)S(1)}, u32[]{:S(2)}, u32[]{:S(2)}) collective-permute-start(bf16[256,1024]{1,0:T(8,128)(2,1)S(1)} %get-tuple-element.104.refs_0_), channel_id=1, source_target_pairs={{0,1},{1,0},{2,3},{3,2},{4,5},{5,4},{6,7},{7,6},{8,9},{9,8},{10,11... | collective-permute-start | bytes 1572872 | tf_op jit(solution)/shard_map/ppermute | solution.py:829
  183.7 58.8 %all-to-all-start = ((bf16[16,64,1664]{2,1,0:T(8,128)(2,1)}), bf16[16,64,1664]{2,1,0:T(8,128)(2,1)S(1)}, u32[]{:S(2)}, u32[]{:S(2)}) async-start(bf16[16,64,1664]{2,1,0:T(8,128)(2,1)} %bitcast.43), calls=%async_computation | async-start | bytes 6815744 | tf_op jit(solution)/shard_map/all_to_all | solution.py:850
  190.7 59.2 %reduce-scatter.5.cloned.1.call-start = ((), (), s32[]{:S(2)}) async-start(), calls=%async_computation.5 | async-start | bytes 1474560 | tf_op jit(solution)/shard_map/reduce_scatter | solution.py:956
  195.6 14.8 %collective-permute-start.28 = (bf16[256,1024]{1,0:T(8,128)(2,1)S(1)}, bf16[256,1024]{1,0:T(8,128)(2,1)S(1)}, u32[]{:S(2)}, u32[]{:S(2)}) collective-permute-start(bf16[256,1024]{1,0:T(8,128)(2,1)S(1)} %fusion.3), channel_id=1, source_target_pairs={{0,2},{2,0},{1,3},{3,1},{4,6},{6,4},{5,7},{7,5},{8,10},{10,8},{9,1... | collective-permute-start | bytes 1572872 | tf_op jit(solution)/shard_map/ppermute | solution.py:829
  198.3 22.6 %collective-permute-start.33 = (bf16[256,1024]{1,0:T(8,128)(2,1)S(1)}, bf16[256,1024]{1,0:T(8,128)(2,1)S(1)}, u32[]{:S(2)}, u32[]{:S(2)}) collective-permute-start(bf16[256,1024]{1,0:T(8,128)(2,1)S(1)} %fusion.4), channel_id=1, source_target_pairs={{0,2},{2,0},{1,3},{3,1},{4,6},{6,4},{5,7},{7,5},{8,10},{10,8},{9,1... | collective-permute-start | bytes 1572872 | tf_op jit(solution)/shard_map/ppermute | solution.py:829
  243.6 6.2 %collective-permute-start.34 = (bf16[32,1664]{1,0:T(8,128)(2,1)S(1)}, bf16[32,1664]{1,0:T(8,128)(2,1)S(1)}, u32[]{:S(2)}, u32[]{:S(2)}) collective-permute-start(bf16[32,1664]{1,0:T(8,128)(2,1)S(1)} %get-tuple-element.125), channel_id=1, source_target_pairs={{0,4},{4,0},{1,5},{5,1},{2,6},{6,2},{3,7},{7,3},{8,12},{12,8},{9,1... | collective-permute-start | bytes 319496 | tf_op jit(solution)/shard_map/ppermute | solution.py:829
  250.9 11.0 %collective-permute-start.38 = (bf16[32,2304]{1,0:T(8,128)(2,1)S(1)}, bf16[32,2304]{1,0:T(8,128)(2,1)S(1)}, u32[]{:S(2)}, u32[]{:S(2)}) collective-permute-start(bf16[32,2304]{1,0:T(8,128)(2,1)S(1)} %get-tuple-element.137), channel_id=1, source_target_pairs={{0,4},{4,0},{1,5},{5,1},{2,6},{6,2},{3,7},{7,3},{8,12},{12,8},{9,1... | collective-permute-start | bytes 442376 | tf_op jit(solution)/shard_map/ppermute | solution.py:829
  (35 other events, 406.7 us)
Sparse Core Ops, SparseCore 0:
  46.4 53.7 all-gather.1
  137.0 50.9 reduce-scatter.2
  193.9 52.5 reduce-scatter.4

commit v3 on v2

--- a/solution.py
+++ b/solution.py
@@ -974,7 +974,7 @@
     keep, give = close(zh, parts)
     arrived = swapped(give, "zh")
     query, key, value, out, columns = finish(keep, arrived, (nq, nk, nk, nq, HD))
-    feed_keep, feed_give = close(zh, after(feed_sums, arrived)[None])
+    feed_keep, feed_give = close(zh, after(feed_sums, columns)[None])
     gate, up, down = finish(feed_keep, swapped(feed_give, "zh"), (units, units, units))
     both = ("zl", "core")
     across = lax.ppermute(columns, both, [(s, 3 - s) for s in range(4)])

time: 275 us -> 273 us (level)
  transfers between devices with their start and end apart: 43 -> 43, of which waited for: 24 -> 24; matrix products, arithmetic and copies ran while one was open for 2% -> 2% of each run, Pallas kernels for 32% -> 33%
where the time goes in v3:
time: 273 us; the launch traced here: 268 us
  waiting for transfers between devices  110 us (40%)
  Pallas kernels  90.6 us (33%)
  starting transfers between devices  44.9 us (16%)
  between operations  14.4 us (5%)
  other arithmetic  5.27 us (2%)
  local copies, waits for them, and re-layouts  2.85 us (1%)
    ppermute x26, waiting for transfers between devices, swapped(): return lax.ppermute(value, axis, [(0, 1), (1, 0)])  73.3 us
    pallas_call x1, Pallas kernels, backward_attention(): pl.pallas_call(functools.partial(backward_attention_kernel, width // lax....  26.5 us
    ppermute x26, starting transfers between devices, swapped(): return lax.ppermute(value, axis, [(0, 1), (1, 0)])  25.2 us
    all_to_all x1, waiting for transfers between devices, sent_rows(): return lax.all_to_all(blocks, PLANE, 0, 0, tiled=True)  18.9 us
    pallas_call x2, Pallas kernels, feed_step(): pl.pallas_call(feed_kernel, in_specs=[pl.BlockSpec(memory_space=pl.ANY)]...  18.3 us
    pallas_call x1, Pallas kernels, forward_attention(): pl.pallas_call(functools.partial(forward_attention_kernel, width // lax.a...  18.1 us
    ppermute x12, waiting for transfers between devices, by_distance(): kept[j] = lax.ppermute(after(own, *before) if before else own, axis, perm)  15 us
    ppermute x12, starting transfers between devices, by_distance(): kept[j] = lax.ppermute(after(own, *before) if before else own, axis, perm)  12.6 us
  transfers between devices with their start and end apart: 43, of which 24 were waited for; matrix products, arithmetic and copies ran while one was open for 2% of the time, Pallas kernels for 33%

profile of v3, /device:TPU:28, one launch (start us, length us, event | category | flops | bytes accessed | tf_op | source)
XLA Modules:
  0.0 267.6 jit_solution(241658707553602793)
XLA Ops:
  9.1 4.0 %collective-permute-start = (bf16[32,3968]{1,0:T(8,128)(2,1)S(1)}, bf16[32,3968]{1,0:T(8,128)(2,1)S(1)}, u32[]{:S(2)}, u32[]{:S(2)}) collective-permute-start(bf16[32,3968]{1,0:T(8,128)(2,1)S(1)} %pack.1.shard), channel_id=1, source_target_pairs={{0,4},{4,0},{1,5},{5,1},{2,6},{6,2},{3,7},{7,3},{8,12},{12,8},{9,1... | collective-permute-start | bytes 761864 | tf_op jit(solution)/shard_map/ppermute | solution.py:829
  13.0 6.1 %collective-permute-done.other = bf16[32,3968]{1,0:T(8,128)(2,1)S(1)} collective-permute-done((bf16[32,3968]{1,0:T(8,128)(2,1)S(1)}, bf16[32,3968]{1,0:T(8,128)(2,1)S(1)}, u32[]{:S(2)}, u32[]{:S(2)}) %collective-permute-start) | collective-permute-done | bytes 253984 | tf_op jit(solution)/shard_map/ppermute | solution.py:829
  20.2 2.6 collective-permute-start.10
  31.2 4.5 %collective-permute-start.8 = (bf16[4,2,32,768]{3,2,1,0:T(8,128)(2,1)S(1)}, bf16[4,2,32,768]{3,2,1,0:T(8,128)(2,1)S(1)}, u32[]{:S(2)}, u32[]{:S(2)}) collective-permute-start(bf16[4,2,32,768]{3,2,1,0:T(8,128)(2,1)S(1)} %pad_maximum_fusion.1.refs_4_), channel_id=1, source_target_pairs={{0,8},{8,16},{16,24},{24,0},{1,9},{9,17},{17,25},{25,1},{2,10},{10... | collective-permute-start | bytes 1179656 | tf_op jit(solution)/shard_map/ppermute | solution.py:863
  35.6 5.3 %collective-permute-done.8.refs_7_ = bf16[4,2,32,768]{3,2,1,0:T(8,128)(2,1)S(1)} collective-permute-done((bf16[4,2,32,768]{3,2,1,0:T(8,128)(2,1)S(1)}, bf16[4,2,32,768]{3,2,1,0:T(8,128)(2,1)S(1)}, u32[]{:S(2)}, u32[]{:S(2)}) %collective-permute-start.8) | collective-permute-done | bytes 393248 | tf_op jit(solution)/shard_map/ppermute | solution.py:863
  40.9 3.7 %collective-permute-done.7.refs_5_ = bf16[4,2,32,768]{3,2,1,0:T(8,128)(2,1)S(1)} collective-permute-done((bf16[4,2,32,768]{3,2,1,0:T(8,128)(2,1)S(1)}, bf16[4,2,32,768]{3,2,1,0:T(8,128)(2,1)S(1)}, u32[]{:S(2)}, u32[]{:S(2)}) %collective-permute-start.7) | collective-permute-done | bytes 393248 | tf_op jit(solution)/shard_map/ppermute | solution.py:863
  48.8 6.8 %collective-permute-done.1.refs_1_.refs_5_ = bf16[256,1024]{1,0:T(8,128)(2,1)S(1)} collective-permute-done((bf16[256,1024]{1,0:T(8,128)(2,1)S(1)}, bf16[256,1024]{1,0:T(8,128)(2,1)S(1)}, u32[]{:S(2)}, u32[]{:S(2)}) %collective-permute-start.1) | collective-permute-done | bytes 524320 | tf_op jit(solution)/shard_map/ppermute | solution.py:829
  55.7 2.3 collective-permute-done.14.refs_6_
  60.3 18.1 %forward_attention.1 = (bf16[1024,1024]{1,0:T(8,128)(2,1)}, f32[1024,512]{1,0:T(8,128)}, f32[1024,256]{1,0:T(8,128)}, bf16[1024,1024]{1,0:T(8,128)(2,1)}, bf16[1...) custom-call(s32[8]{0:T(128)S(1)} %pad_add_fusion.1.place, ...), custom_call_target="tpu_custom_call" | custom-call | flops 875000000 | bytes 2000000 | tf_op jit(solution)/shard_map/forward_attention/pallas_call | solution.py:254
  78.6 2.6 collective-permute-done.17.from_core
  82.8 12.7 %collective-permute-done.18.from_z = bf16[256,1024]{1,0:T(8,128)(2,1)S(1)} collective-permute-done((bf16[256,1024]{1,0:T(8,128)(2,1)S(1)}, bf16[256,1024]{1,0:T(8,128)(2,1)S(1)}, u32[]{:S(2)}, u32[]{:S(2)}) %collective-permute-start.18) | collective-permute-done | bytes 524320 | tf_op jit(solution)/shard_map/ppermute | solution.py:829
  95.4 2.2 middle_step.1
  100.3 9.1 %feed_step.2 = (bf16[512,768]{1,0:T(8,128)(2,1)}, bf16[512,1536]{1,0:T(8,128)(2,1)}, bf16[256,1024]{1,0:T(8,128)(2,1)S(1)}, bf16[256,1024]{1,0:T(8,128)(2,1)S(1)}) custom-call(bf16[256,1024]{1,0:T(8,128)(2,1)S(1)} %get-tuple-element.88.refs_0_, bf16[256,1024]{1,0:T(8,128)(2,1)S(1)} %collective-permute-done.19.refs_1_.refs_2_, ...), custom_call_target="tpu_custom_call" | custom-call | flops 500000000 | bytes 1000000 | tf_op jit(solution)/shard_map/feed_step/pallas_call | solution.py:347
  109.4 2.6 collective-permute-done.22.refs_0_.refs_1_
  113.9 9.3 %feed_step.3 = (bf16[512,768]{1,0:T(8,128)(2,1)}, bf16[512,1536]{1,0:T(8,128)(2,1)}, bf16[256,1024]{1,0:T(8,128)(2,1)S(1)}, bf16[256,1024]{1,0:T(8,128)(2,1)S(1)}) custom-call(bf16[256,1024]{1,0:T(8,128)(2,1)S(1)} %collective-permute-done.22.refs_0_.refs_1_, bf16[256,1024]{1,0:T(8,128)(2,1)S(1)} %collective-permute-done.23.refs_1_.refs_3_, ...), custom_call_target="tpu_custom_call" | custom-call | flops 500000000 | bytes 1000000 | tf_op jit(solution)/shard_map/feed_step/pallas_call | solution.py:347
  126.8 10.0 %feed_weights.1 = bf16[1024,2304]{1,0:T(8,128)(2,1)} custom-call(bf16[256,1024]{1,0:T(8,128)(2,1)} %copy-done.1, bf16[256,1024]{1,0:T(8,128)(2,1)} %copy-done.3, bf16[256,1024]{1,0:T(8,128)(2,1)} %copy-done.2, bf16[256,1024]{1,0:T(8,128)(2,1)} %copy-done.4, bf16[256,1024]{1,0:T(8,128)(2,1)} %bitcast.11.refs_2_.refs_4_.cotangent, ...), custom_call_target="tpu_custom_call" | custom-call | flops 600000000 | bytes 1750000 | tf_op jit(solution)/shard_map/feed_weights/pallas_call | solution.py:412
  136.8 2.6 collective-permute-done.26.from_z
  139.5 2.7 %middle_back.1 = (f32[256,1024]{1,0:T(8,128)}, bf16[256,1024]{1,0:T(8,128)(2,1)S(1)}, f32[8,1024]{1,0:T(8,128)}) custom-call(f32[256,1024]{1,0:T(8,128)} %get-tuple-element.87.middle, bf16[256,1024]{1,0:T(8,128)(2,1)S(1)} %get-tuple-element.92.mine, bf16[256,1024]{1,0:T(8,128)(2,1)S(1)} %collective-permute-done.21.from_core, ...), custom_call_target="tpu_custom_call" | custom-call | flops 500000 | bytes 625000 | tf_op jit(solution)/shard_map/middle_back/pallas_call | solution.py:447
  143.5 4.9 %feed_out.1 = (bf16[2,256,1024]{2,1,0:T(8,128)(2,1)}, bf16[2,256,1024]{2,1,0:T(8,128)(2,1)}) custom-call(bf16[512,768]{1,0:T(8,128)(2,1)} %get-tuple-element.105.refs_10_.first, bf16[512,768]{1,0:T(8,128)(2,1)} %get-tuple-element.102.refs_11_.then, bf16[1024,2304]{1,0:T(8,128)(2,1)} %all-gather.2.cloned.1.call-done.refs_4_.wd), custom_call_target="tpu_custom_call" | custom-call | flops 200000000 | bytes 625000 | tf_op jit(solution)/shard_map/feed_out/pallas_call | solution.py:381
  148.4 6.9 %collective-permute-done.29.refs_1_ = bf16[256,1024]{1,0:T(8,128)(2,1)S(1)} collective-permute-done((bf16[256,1024]{1,0:T(8,128)(2,1)S(1)}, bf16[256,1024]{1,0:T(8,128)(2,1)S(1)}, u32[]{:S(2)}, u32[]{:S(2)}) %collective-permute-start.29) | collective-permute-done | bytes 524320 | tf_op jit(solution)/shard_map/ppermute | solution.py:829
  155.3 1.9 collective-permute-done.31.refs_3_
  157.2 26.5 %backward_attention.1 = (bf16[2,256,1024]{2,1,0:T(8,128)(2,1)}, bf16[2,256,1024]{2,1,0:T(8,128)(2,1)}, bf16[1024,1664]{1,0:T(8,128)(2,1)}) custom-call(s32[8]{0:T(128)S(1)} %pad_add_fusion.1.place, bf16[256,1024]{1,0:T(8,128)(2,1)S(1)} %get-tuple-element.104.refs_0_, bf16[256,1024]{1,0:T(8,128)(2,1)S(1)} %collective-permute-done.29.refs_1_, ...), custom_call_target="tpu_custom_call" | custom-call | flops 74999996416 | bytes 2250000 | tf_op jit(solution)/shard_map/backward_attention/pallas_call | solution.py:607
  183.7 6.9 %all-to-all-start = ((bf16[16,64,1664]{2,1,0:T(8,128)(2,1)}), bf16[16,64,1664]{2,1,0:T(8,128)(2,1)S(1)}, u32[]{:S(2)}, u32[]{:S(2)}) async-start(bf16[16,64,1664]{2,1,0:T(8,128)(2,1)} %bitcast.43), calls=%async_computation | async-start | bytes 6815744 | tf_op jit(solution)/shard_map/all_to_all | solution.py:850
  192.0 2.4 collective-permute-done.27
  199.1 11.3 %collective-permute-done.28 = bf16[256,1024]{1,0:T(8,128)(2,1)S(1)} collective-permute-done((bf16[256,1024]{1,0:T(8,128)(2,1)S(1)}, bf16[256,1024]{1,0:T(8,128)(2,1)S(1)}, u32[]{:S(2)}, u32[]{:S(2)}) %collective-permute-start.28) | collective-permute-done | bytes 524320 | tf_op jit(solution)/shard_map/ppermute | solution.py:829
  211.6 9.3 %collective-permute-done.33.from_z = bf16[256,1024]{1,0:T(8,128)(2,1)S(1)} collective-permute-done((bf16[256,1024]{1,0:T(8,128)(2,1)S(1)}, bf16[256,1024]{1,0:T(8,128)(2,1)S(1)}, u32[]{:S(2)}, u32[]{:S(2)}) %collective-permute-start.33) | collective-permute-done | bytes 524320 | tf_op jit(solution)/shard_map/ppermute | solution.py:829
  220.9 2.6 tokens_back.1
  223.5 18.9 %all-to-all-done.parts = bf16[16,64,1664]{2,1,0:T(8,128)(2,1)S(1)} async-done(((bf16[16,64,1664]{2,1,0:T(8,128)(2,1)}), bf16[16,64,1664]{2,1,0:T(8,128)(2,1)S(1)}, u32[]{:S(2)}, u32[]{:S(2)}) %all-to-all-start) | async-done | bytes 3407904 | tf_op jit(solution)/shard_map/all_to_all | solution.py:850
  242.8 3.4 %collective-permute-start.34 = (bf16[32,1664]{1,0:T(8,128)(2,1)S(1)}, bf16[32,1664]{1,0:T(8,128)(2,1)S(1)}, u32[]{:S(2)}, u32[]{:S(2)}) collective-permute-start(bf16[32,1664]{1,0:T(8,128)(2,1)S(1)} %get-tuple-element.125), channel_id=1, source_target_pairs={{0,4},{4,0},{1,5},{5,1},{2,6},{6,2},{3,7},{7,3},{8,12},{12,8},{9,1... | collective-permute-start | bytes 319496 | tf_op jit(solution)/shard_map/ppermute | solution.py:829
  246.3 2.9 %collective-permute-done.34.arrived = bf16[32,1664]{1,0:T(8,128)(2,1)S(1)} collective-permute-done((bf16[32,1664]{1,0:T(8,128)(2,1)S(1)}, bf16[32,1664]{1,0:T(8,128)(2,1)S(1)}, u32[]{:S(2)}, u32[]{:S(2)}) %collective-permute-start.34) | collective-permute-done | bytes 106528 | tf_op jit(solution)/shard_map/ppermute | solution.py:829
  250.8 3.4 %collective-permute-start.38 = (bf16[32,2304]{1,0:T(8,128)(2,1)S(1)}, bf16[32,2304]{1,0:T(8,128)(2,1)S(1)}, u32[]{:S(2)}, u32[]{:S(2)}) collective-permute-start(bf16[32,2304]{1,0:T(8,128)(2,1)S(1)} %get-tuple-element.137), channel_id=1, source_target_pairs={{0,4},{4,0},{1,5},{5,1},{2,6},{6,2},{3,7},{7,3},{8,12},{12,8},{9,1... | collective-permute-start | bytes 442376 | tf_op jit(solution)/shard_map/ppermute | solution.py:829
  257.6 1.9 collective-permute-done.35.refs_1_
  (134 shorter events, 42.8 us)
Async XLA Ops:
  7.2 93.1 %all-gather.2.cloned.1.call-start = ((), (), s32[]{:S(2)}) async-start(), calls=%async_computation.3 | async-start | bytes 5013504 | tf_op jit(solution)/shard_map/all_gather | solution.py:933
  9.1 10.1 %collective-permute-start = (bf16[32,3968]{1,0:T(8,128)(2,1)S(1)}, bf16[32,3968]{1,0:T(8,128)(2,1)S(1)}, u32[]{:S(2)}, u32[]{:S(2)}) collective-permute-start(bf16[32,3968]{1,0:T(8,128)(2,1)S(1)} %pack.1.shard), channel_id=1, source_target_pairs={{0,4},{4,0},{1,5},{5,1},{2,6},{6,2},{3,7},{7,3},{8,12},{12,8},{9,1... | collective-permute-start | bytes 761864 | tf_op jit(solution)/shard_map/ppermute | solution.py:829
  19.9 5.6 %collective-permute-start.11 = (bf16[2,32,896]{2,1,0:T(8,128)(2,1)S(1)}, bf16[2,32,896]{2,1,0:T(8,128)(2,1)S(1)}, u32[]{:S(2)}, u32[]{:S(2)}) collective-permute-start(bf16[2,32,896]{2,1,0:T(8,128)(2,1)S(1)} %get-tuple-element.79), channel_id=1, source_target_pairs={{0,8},{8,16},{16,24},{24,0},{1,9},{9,17},{17,25},{25,1},{2,10},{10... | collective-permute-start | bytes 344072 | tf_op jit(solution)/shard_map/ppermute | solution.py:863
  20.2 7.4 %collective-permute-start.10 = (bf16[2,32,896]{2,1,0:T(8,128)(2,1)S(1)}, bf16[2,32,896]{2,1,0:T(8,128)(2,1)S(1)}, u32[]{:S(2)}, u32[]{:S(2)}) collective-permute-start(bf16[2,32,896]{2,1,0:T(8,128)(2,1)S(1)} %get-tuple-element.79), channel_id=1, source_target_pairs={{0,16},{8,24},{16,0},{24,8},{1,17},{9,25},{17,1},{25,9},{2,18},{10... | collective-permute-start | bytes 344072 | tf_op jit(solution)/shard_map/ppermute | solution.py:863
  22.8 6.2 %collective-permute-start.9 = (bf16[2,32,896]{2,1,0:T(8,128)(2,1)S(1)}, bf16[2,32,896]{2,1,0:T(8,128)(2,1)S(1)}, u32[]{:S(2)}, u32[]{:S(2)}) collective-permute-start(bf16[2,32,896]{2,1,0:T(8,128)(2,1)S(1)} %get-tuple-element.79), channel_id=1, source_target_pairs={{0,24},{8,0},{16,8},{24,16},{1,25},{9,1},{17,9},{25,17},{2,26},{10... | collective-permute-start | bytes 344072 | tf_op jit(solution)/shard_map/ppermute | solution.py:863
  22.8 8.3 %collective-permute-start.6 = (bf16[2,32,768]{2,1,0:T(8,128)(2,1)S(1)}, bf16[2,32,768]{2,1,0:T(8,128)(2,1)S(1)}, u32[]{:S(2)}, u32[]{:S(2)}) collective-permute-start(bf16[2,32,768]{2,1,0:T(8,128)(2,1)S(1)} %get-tuple-element.78), channel_id=1, source_target_pairs={{0,32},{32,64},{64,96},{96,0},{1,33},{33,65},{65,97},{97,1},{2,34}... | collective-permute-start | bytes 294920 | tf_op jit(solution)/shard_map/ppermute | solution.py:863
  24.0 7.2 %collective-permute-start.5 = (bf16[2,32,768]{2,1,0:T(8,128)(2,1)S(1)}, bf16[2,32,768]{2,1,0:T(8,128)(2,1)S(1)}, u32[]{:S(2)}, u32[]{:S(2)}) collective-permute-start(bf16[2,32,768]{2,1,0:T(8,128)(2,1)S(1)} %get-tuple-element.78), channel_id=1, source_target_pairs={{0,64},{32,96},{64,0},{96,32},{1,65},{33,97},{65,1},{97,33},{2,66}... | collective-permute-start | bytes 294920 | tf_op jit(solution)/shard_map/ppermute | solution.py:863
  25.5 5.6 %collective-permute-start.4 = (bf16[2,32,768]{2,1,0:T(8,128)(2,1)S(1)}, bf16[2,32,768]{2,1,0:T(8,128)(2,1)S(1)}, u32[]{:S(2)}, u32[]{:S(2)}) collective-permute-start(bf16[2,32,768]{2,1,0:T(8,128)(2,1)S(1)} %get-tuple-element.78), channel_id=1, source_target_pairs={{0,96},{32,0},{64,32},{96,64},{1,97},{33,1},{65,33},{97,65},{2,98}... | collective-permute-start | bytes 294920 | tf_op jit(solution)/shard_map/ppermute | solution.py:863
  29.0 15.6 %collective-permute-start.13 = (bf16[4,2,32,896]{3,2,1,0:T(8,128)(2,1)S(1)}, bf16[4,2,32,896]{3,2,1,0:T(8,128)(2,1)S(1)}, u32[]{:S(2)}, u32[]{:S(2)}) collective-permute-start(bf16[4,2,32,896]{3,2,1,0:T(8,128)(2,1)S(1)} %pad_maximum_fusion.refs_8_), channel_id=1, source_target_pairs={{0,32},{32,64},{64,96},{96,0},{1,33},{33,65},{65,97},{97,1},{2,34}... | collective-permute-start | bytes 1376264 | tf_op jit(solution)/shard_map/ppermute | solution.py:863
  30.3 14.4 %collective-permute-start.12 = (bf16[4,2,32,896]{3,2,1,0:T(8,128)(2,1)S(1)}, bf16[4,2,32,896]{3,2,1,0:T(8,128)(2,1)S(1)}, u32[]{:S(2)}, u32[]{:S(2)}) collective-permute-start(bf16[4,2,32,896]{3,2,1,0:T(8,128)(2,1)S(1)} %pad_maximum_fusion.refs_8_), channel_id=1, source_target_pairs={{0,96},{32,0},{64,32},{96,64},{1,97},{33,1},{65,33},{97,65},{2,98}... | collective-permute-start | bytes 1376264 | tf_op jit(solution)/shard_map/ppermute | solution.py:863
  31.2 9.7 %collective-permute-start.8 = (bf16[4,2,32,768]{3,2,1,0:T(8,128)(2,1)S(1)}, bf16[4,2,32,768]{3,2,1,0:T(8,128)(2,1)S(1)}, u32[]{:S(2)}, u32[]{:S(2)}) collective-permute-start(bf16[4,2,32,768]{3,2,1,0:T(8,128)(2,1)S(1)} %pad_maximum_fusion.1.refs_4_), channel_id=1, source_target_pairs={{0,8},{8,16},{16,24},{24,0},{1,9},{9,17},{17,25},{25,1},{2,10},{10... | collective-permute-start | bytes 1179656 | tf_op jit(solution)/shard_map/ppermute | solution.py:863
  35.6 9.0 %collective-permute-start.7 = (bf16[4,2,32,768]{3,2,1,0:T(8,128)(2,1)S(1)}, bf16[4,2,32,768]{3,2,1,0:T(8,128)(2,1)S(1)}, u32[]{:S(2)}, u32[]{:S(2)}) collective-permute-start(bf16[4,2,32,768]{3,2,1,0:T(8,128)(2,1)S(1)} %pad_maximum_fusion.1.refs_4_), channel_id=1, source_target_pairs={{0,24},{8,0},{16,8},{24,16},{1,25},{9,1},{17,9},{25,17},{2,26},{10... | collective-permute-start | bytes 1179656 | tf_op jit(solution)/shard_map/ppermute | solution.py:863
  46.3 144.4 %reduce-scatter.3.cloned.1.call-start = ((), (), s32[]{:S(2)}) async-start(), calls=%async_computation.4 | async-start | bytes 5898240 | tf_op jit(solution)/shard_map/reduce_scatter | solution.py:955
  46.4 9.3 %collective-permute-start.1 = (bf16[256,1024]{1,0:T(8,128)(2,1)S(1)}, bf16[256,1024]{1,0:T(8,128)(2,1)S(1)}, u32[]{:S(2)}, u32[]{:S(2)}) collective-permute-start(bf16[256,1024]{1,0:T(8,128)(2,1)S(1)} %bitcast.41), channel_id=1, source_target_pairs={{0,2},{2,0},{1,3},{3,1},{4,6},{6,4},{5,7},{7,5},{8,10},{10,8},{9,1... | collective-permute-start | bytes 1572872 | tf_op jit(solution)/shard_map/ppermute | solution.py:829
  48.0 10.0 %collective-permute-start.15 = (bf16[4,2,32,896]{3,2,1,0:T(8,128)(2,1)S(1)}, bf16[4,2,32,896]{3,2,1,0:T(8,128)(2,1)S(1)}, u32[]{:S(2)}, u32[]{:S(2)}) collective-permute-start(bf16[4,2,32,896]{3,2,1,0:T(8,128)(2,1)S(1)} %pad_maximum_fusion.refs_8_), channel_id=1, source_target_pairs={{0,64},{32,96},{64,0},{96,32},{1,65},{33,97},{65,1},{97,33},{2,66}... | collective-permute-start | bytes 1376264 | tf_op jit(solution)/shard_map/ppermute | solution.py:863
  48.7 9.3 %collective-permute-start.14 = (bf16[4,2,32,768]{3,2,1,0:T(8,128)(2,1)S(1)}, bf16[4,2,32,768]{3,2,1,0:T(8,128)(2,1)S(1)}, u32[]{:S(2)}, u32[]{:S(2)}) collective-permute-start(bf16[4,2,32,768]{3,2,1,0:T(8,128)(2,1)S(1)} %pad_maximum_fusion.1.refs_4_), channel_id=1, source_target_pairs={{0,16},{8,24},{16,0},{24,8},{1,17},{9,25},{17,1},{25,9},{2,18},{10... | collective-permute-start | bytes 1179656 | tf_op jit(solution)/shard_map/ppermute | solution.py:863
  48.8 11.4 %collective-permute-start.2 = (bf16[256,1024]{1,0:T(8,128)(2,1)S(1)}, bf16[256,1024]{1,0:T(8,128)(2,1)S(1)}, u32[]{:S(2)}, u32[]{:S(2)}) collective-permute-start(bf16[256,1024]{1,0:T(8,128)(2,1)S(1)} %bitcast.42), channel_id=1, source_target_pairs={{0,1},{1,0},{2,3},{3,2},{4,5},{5,4},{6,7},{7,6},{8,9},{9,8},{10,11... | collective-permute-start | bytes 1572872 | tf_op jit(solution)/shard_map/ppermute | solution.py:829
  58.9 19.5 %collective-permute-start.16 = (bf16[256,1024]{1,0:T(8,128)(2,1)}, bf16[256,1024]{1,0:T(8,128)(2,1)S(1)}, u32[]{:S(2)}, u32[]{:S(2)}) collective-permute-start(bf16[256,1024]{1,0:T(8,128)(2,1)} %bitcast.11.refs_2_.refs_4_.cotangent), channel_id=1, source_target_pairs={{0,2},{2,0},{1,3},{3,1},{4,6},{6,4},{5,7},{7,5},{8,10},{10,8},{9,1... | collective-permute-start | bytes 1572872 | tf_op jit(solution)/shard_map/ppermute | solution.py:829
  81.4 14.0 %collective-permute-start.18 = (bf16[256,1024]{1,0:T(8,128)(2,1)S(1)}, bf16[256,1024]{1,0:T(8,128)(2,1)S(1)}, u32[]{:S(2)}, u32[]{:S(2)}) collective-permute-start(bf16[256,1024]{1,0:T(8,128)(2,1)S(1)} %fusion.2), channel_id=1, source_target_pairs={{0,2},{2,0},{1,3},{3,1},{4,6},{6,4},{5,7},{7,5},{8,10},{10,8},{9,1... | collective-permute-start | bytes 1572872 | tf_op jit(solution)/shard_map/ppermute | solution.py:829
  82.8 16.9 %collective-permute-start.20 = (bf16[256,1024]{1,0:T(8,128)(2,1)}, bf16[256,1024]{1,0:T(8,128)(2,1)}, u32[]{:S(2)}, u32[]{:S(2)}) collective-permute-start(bf16[256,1024]{1,0:T(8,128)(2,1)} %bitcast.11.refs_2_.refs_4_.cotangent), channel_id=1, source_target_pairs={{0,1},{1,0},{2,3},{3,2},{4,5},{5,4},{6,7},{7,6},{8,9},{9,8},{10,11... | collective-permute-start | bytes 1572872 | tf_op jit(solution)/shard_map/ppermute | solution.py:829
  97.7 14.3 %collective-permute-start.22 = (bf16[256,1024]{1,0:T(8,128)(2,1)S(1)}, bf16[256,1024]{1,0:T(8,128)(2,1)S(1)}, u32[]{:S(2)}, u32[]{:S(2)}) collective-permute-start(bf16[256,1024]{1,0:T(8,128)(2,1)S(1)} %get-tuple-element.88.refs_0_), channel_id=1, source_target_pairs={{0,2},{2,0},{1,3},{3,1},{4,6},{6,4},{5,7},{7,5},{8,10},{10,8},{9,1... | collective-permute-start | bytes 1572872 | tf_op jit(solution)/shard_map/ppermute | solution.py:829
  99.0 13.5 %collective-permute-start.24 = (bf16[256,1024]{1,0:T(8,128)(2,1)S(1)}, bf16[256,1024]{1,0:T(8,128)(2,1)}, u32[]{:S(2)}, u32[]{:S(2)}) collective-permute-start(bf16[256,1024]{1,0:T(8,128)(2,1)S(1)} %collective-permute-done.16.refs_2_.refs_5_), channel_id=1, source_target_pairs={{0,1},{1,0},{2,3},{3,2},{4,5},{5,4},{6,7},{7,6},{8,9},{9,8},{10,11... | collective-permute-start | bytes 1572872 | tf_op jit(solution)/shard_map/ppermute | solution.py:829
  112.0 11.4 %collective-permute-start.21 = (bf16[256,1024]{1,0:T(8,128)(2,1)S(1)}, bf16[256,1024]{1,0:T(8,128)(2,1)S(1)}, u32[]{:S(2)}, u32[]{:S(2)}) collective-permute-start(bf16[256,1024]{1,0:T(8,128)(2,1)S(1)} %get-tuple-element.93), channel_id=1, source_target_pairs={{0,1},{1,0},{2,3},{3,2},{4,5},{5,4},{6,7},{7,6},{8,9},{9,8},{10,11... | collective-permute-start | bytes 1572872 | tf_op jit(solution)/shard_map/ppermute | solution.py:829
  125.4 14.0 %collective-permute-start.26 = (bf16[256,1024]{1,0:T(8,128)(2,1)S(1)}, bf16[256,1024]{1,0:T(8,128)(2,1)S(1)}, u32[]{:S(2)}, u32[]{:S(2)}) collective-permute-start(bf16[256,1024]{1,0:T(8,128)(2,1)S(1)} %add_convert_fusion.2), channel_id=1, source_target_pairs={{0,2},{2,0},{1,3},{3,1},{4,6},{6,4},{5,7},{7,5},{8,10},{10,8},{9,1... | collective-permute-start | bytes 1572872 | tf_op jit(solution)/shard_map/ppermute | solution.py:829
  142.2 13.1 %collective-permute-start.29 = (bf16[256,1024]{1,0:T(8,128)(2,1)S(1)}, bf16[256,1024]{1,0:T(8,128)(2,1)S(1)}, u32[]{:S(2)}, u32[]{:S(2)}) collective-permute-start(bf16[256,1024]{1,0:T(8,128)(2,1)S(1)} %get-tuple-element.104.refs_0_), channel_id=1, source_target_pairs={{0,2},{2,0},{1,3},{3,1},{4,6},{6,4},{5,7},{7,5},{8,10},{10,8},{9,1... | collective-permute-start | bytes 1572872 | tf_op jit(solution)/shard_map/ppermute | solution.py:829
  143.5 11.8 %collective-permute-start.30 = (bf16[256,1024]{1,0:T(8,128)(2,1)S(1)}, bf16[256,1024]{1,0:T(8,128)(2,1)S(1)}, u32[]{:S(2)}, u32[]{:S(2)}) collective-permute-start(bf16[256,1024]{1,0:T(8,128)(2,1)S(1)} %get-tuple-element.104.refs_0_), channel_id=1, source_target_pairs={{0,1},{1,0},{2,3},{3,2},{4,5},{5,4},{6,7},{7,6},{8,9},{9,8},{10,11... | collective-permute-start | bytes 1572872 | tf_op jit(solution)/shard_map/ppermute | solution.py:829
  183.7 58.7 %all-to-all-start = ((bf16[16,64,1664]{2,1,0:T(8,128)(2,1)}), bf16[16,64,1664]{2,1,0:T(8,128)(2,1)S(1)}, u32[]{:S(2)}, u32[]{:S(2)}) async-start(bf16[16,64,1664]{2,1,0:T(8,128)(2,1)} %bitcast.43), calls=%async_computation | async-start | bytes 6815744 | tf_op jit(solution)/shard_map/all_to_all | solution.py:850
  190.7 59.1 %reduce-scatter.5.cloned.1.call-start = ((), (), s32[]{:S(2)}) async-start(), calls=%async_computation.5 | async-start | bytes 1474560 | tf_op jit(solution)/shard_map/reduce_scatter | solution.py:956
  195.6 14.8 %collective-permute-start.28 = (bf16[256,1024]{1,0:T(8,128)(2,1)S(1)}, bf16[256,1024]{1,0:T(8,128)(2,1)S(1)}, u32[]{:S(2)}, u32[]{:S(2)}) collective-permute-start(bf16[256,1024]{1,0:T(8,128)(2,1)S(1)} %fusion.3), channel_id=1, source_target_pairs={{0,2},{2,0},{1,3},{3,1},{4,6},{6,4},{5,7},{7,5},{8,10},{10,8},{9,1... | collective-permute-start | bytes 1572872 | tf_op jit(solution)/shard_map/ppermute | solution.py:829
  198.3 22.6 %collective-permute-start.33 = (bf16[256,1024]{1,0:T(8,128)(2,1)S(1)}, bf16[256,1024]{1,0:T(8,128)(2,1)S(1)}, u32[]{:S(2)}, u32[]{:S(2)}) collective-permute-start(bf16[256,1024]{1,0:T(8,128)(2,1)S(1)} %fusion.4), channel_id=1, source_target_pairs={{0,2},{2,0},{1,3},{3,1},{4,6},{6,4},{5,7},{7,5},{8,10},{10,8},{9,1... | collective-permute-start | bytes 1572872 | tf_op jit(solution)/shard_map/ppermute | solution.py:829
  242.8 6.3 %collective-permute-start.34 = (bf16[32,1664]{1,0:T(8,128)(2,1)S(1)}, bf16[32,1664]{1,0:T(8,128)(2,1)S(1)}, u32[]{:S(2)}, u32[]{:S(2)}) collective-permute-start(bf16[32,1664]{1,0:T(8,128)(2,1)S(1)} %get-tuple-element.125), channel_id=1, source_target_pairs={{0,4},{4,0},{1,5},{5,1},{2,6},{6,2},{3,7},{7,3},{8,12},{12,8},{9,1... | collective-permute-start | bytes 319496 | tf_op jit(solution)/shard_map/ppermute | solution.py:829
  250.8 9.3 %collective-permute-start.38 = (bf16[32,2304]{1,0:T(8,128)(2,1)S(1)}, bf16[32,2304]{1,0:T(8,128)(2,1)S(1)}, u32[]{:S(2)}, u32[]{:S(2)}) collective-permute-start(bf16[32,2304]{1,0:T(8,128)(2,1)S(1)} %get-tuple-element.137), channel_id=1, source_target_pairs={{0,4},{4,0},{1,5},{5,1},{2,6},{6,2},{3,7},{7,3},{8,12},{12,8},{9,1... | collective-permute-start | bytes 442376 | tf_op jit(solution)/shard_map/ppermute | solution.py:829
  (33 other events, 405.3 us)
Sparse Core Ops, SparseCore 0:
  46.5 53.7 all-gather.1
  137.0 50.9 reduce-scatter.2
  193.9 52.4 reduce-scatter.4
